TPU v7x, 256 devices: a whole 4x4x8 slice. The times are simulated.
256 devices in a mesh: area: 32 (over z, x), row: 8 (over y, core).
Axes of the slice: x: 4, y: 4, z: 8, core: 2. Of those that a mesh axis runs over, the one named last changes fastest.
Arguments:
- conductance_inverse: float32 [256, 1024, 1024], P(('area', 'row')), as said below
- cap_history: float32 [256, 1024, 128], P(('area', 'row')), may hold values from -3 to 3
- cap_conductance: float32 [256, 1024], P(('area', 'row')), may hold values from 0.5 to 0.8
- wave_history: float32 [256, 40, 32, 128], P(('area', 'row')), may hold values from -6 to 6
- line_partner: int32 [256, 32], P(('area', 'row')), may hold values from 0 to 255, as said below
- line_node: int32 [256, 32], P(('area', 'row')), may hold values from 0 to 1023
- line_delay: int32 [256, 32], P(('area', 'row')), may hold values from 20 to 40
- line_admittance: float32 [256, 32], P(('area', 'row')), may hold values from 0.2 to 1
- conv_node: int32 [256, 64], P(('area', 'row')), may hold values from 0 to 1023
- conv_count: int32 [256], P(('area', 'row')), may hold values from 1 to 64, as said below
- conv_state: float32 [256, 2, 64, 128], P(('area', 'row')), may hold values from -3 to 3
- conv_reference: float32 [256, 2, 64, 128], P(('area', 'row')), may hold values from -4 to 4
- conv_rate: float32 [256, 64], P(('area', 'row')), may hold values from 0.03 to 0.6
- conv_limit: float32 [256, 64], P(('area', 'row')), may hold values from 1 to 2.5
- port_node: int32 [256, 8], P(('area', 'row')), may hold values from 0 to 1023
- port_admittance: float32 [256, 8], P(('area', 'row')), may hold values from 0.3 to 1.2
- port_voltage_prev: float32 [2, 256, 8, 128], P(None, ('area', 'row')), may hold values from -5 to 5
- port_bus: int32 [256, 8], P('area'), may hold values from 0 to 20479
- transfer_impedance: float32 [2, 20480, 2048], P(None, 'row', 'area'), may hold values from -0.25 to 0.25
Outputs:
- waves: float32 [256, 20, 32, 128], P(('area', 'row'))
- cap_history_out: float32 [256, 1024, 128], P(('area', 'row'))
- conv_state_out: float32 [256, 2, 64, 128], P(('area', 'row'))
- bus_voltage: float32 [2, 20480, 128], P(None, 'row')
- port_voltage: float32 [2, 256, 8, 128], P(None, ('area', 'row'))
Inputs may be any that keep to these rules, and one draw needn't show every extreme that they name: Slot l < 16 of subnetwork s and slot l + 16 of subnetwork (s + k_l) mod 256 are the two ends of one line, with k_l in 1 or 2 the same for every subnetwork and exactly 12 of the k_l equal to 1; so line_partner[s, l] = (s + k_l) mod 256 and line_partner[s, l + 16] = (s - k_l) mod 256. `conv_count`: some subnetwork has all 64 converters in service. `conductance_inverse`: each subnetwork's inverse nodal conductance matrix.
All inputs are finite; a program needn't handle non-finite values.
Results may differ from a plain program's by a relative error of at most 0.0003.
Values sent between devices are 32-bit elements; how exact they have to be, the bound alone decides.
No kernel may reach another device: no remote copies, remote signals or barrier semaphores. Data moves between devices by JAX's collectives and lax.ppermute only.
A program may use at most 64 MiB of HBM per device.

v0:
```python
import math

import jax
import jax.numpy as jnp
from jax import lax
from jax.sharding import Mesh
from jax.sharding import PartitionSpec as P

STEPS = 20
HIST = 40
NEAR = 12
AREA_ROW = ("area_0", "area_1", "row")
AREA = ("area_0", "area_1")


HIGHEST = lax.Precision.HIGHEST
SAG_FACTOR = 0.3


def from_behind(x, axis, by):
    size = lax.axis_size(axis)
    return lax.ppermute(x, axis, [(i, (i + by) % size) for i in range(size)])


def laid_out(parts, dim):
    parts = jnp.moveaxis(parts, 0, dim)
    shape = parts.shape
    return parts.reshape(*shape[:dim], shape[dim] * shape[dim + 1], *shape[dim + 2 :])


def copy_for_each(x, axis):
    size = lax.axis_size(axis)
    return lax.all_to_all(jnp.broadcast_to(x[None], (size, *x.shape)), axis, 0, 0, tiled=True)


def collect(x, axis, dim):
    return laid_out(copy_for_each(x, axis), dim)


def rows_for(lines, size):
    spare = -lines.shape[0] % size
    if not spare:
        return lines
    return jnp.concatenate([lines, jnp.zeros((spare, *lines.shape[1:]), lines.dtype)])


def own_block(parts, axes, order):
    inside = parts.shape[1:]
    parts = parts.reshape(*(lax.axis_size(a) for a in axes), *inside)
    parts = jnp.moveaxis(parts, order, range(len(axes))).reshape(-1, *inside)
    for k in order:
        parts = lax.psum_scatter(parts, axes[k], scatter_dimension=0, tiled=True)
    return parts[0]


def stacked_from(x, axes, order):
    parts = x
    for k in order:
        parts = lax.all_gather(parts, axes[k])
    done = order[::-1]
    back = [done.index(k) for k in range(len(axes))]
    parts = parts.transpose(*back, *range(len(axes), parts.ndim))
    return parts.reshape(-1, *x.shape)


def sum_by_parts(x, axes, order):
    size, lines = (lax.axis_size(axes), x.reshape(-1, *x.shape[1:][-1:]))
    parts = rows_for(lines, size).reshape(size, -1, *lines.shape[1:])
    own = own_block(parts, axes, order)
    whole = stacked_from(own, axes, order[::-1]).reshape(-1, *lines.shape[1:])
    return whole[: len(lines)].reshape(x.shape)


def split_up(x, dim, size):
    before, after = (x.shape[:dim], x.shape[dim + 1 :])
    return jnp.moveaxis(x.reshape(*before, size, -1, *after), dim, 0)


def sum_at_owner(x, axis, dim):
    size = lax.axis_size(axis)
    parts = lax.all_to_all(split_up(x, dim, size), axis, 0, 0, tiled=True)
    return jnp.sum(parts, axis=0)


def window(
    ginv,
    start_hist,
    gcap,
    incoming,
    lnode,
    ladm,
    cnode,
    ccount,
    cstate,
    setpoint_flow,
    crate,
    climit,
    pnode,
    padm,
    pvolt,
):
    nodes = ginv.shape[0]
    lines = lnode.shape[0]
    convs = cnode.shape[0]
    index = jnp.concatenate([lnode, cnode, pnode])
    onehot = (jnp.arange(nodes, dtype=jnp.int32)[:, None] == index[None, :]).astype(jnp.float32)
    picker = onehot.T
    live = (jnp.arange(convs, dtype=jnp.int32) < ccount)[:, None]
    angles = jnp.arange(1, STEPS + 1, dtype=jnp.float32) * jnp.float32(2.0 * math.pi / STEPS)
    limit = climit[:, None]
    slew_limit = crate[:, None]

    def advance(carry, inputs):
        hist_now, inverter_axial_part, inverter_normal_part, acc_re, acc_im = carry
        inward, angle = inputs
        angle_cos_factor = jnp.cos(angle)
        angle_sin_factor = jnp.sin(angle)
        drive = jnp.where(
            live,
            inverter_axial_part * angle_cos_factor - inverter_normal_part * angle_sin_factor,
            0.0,
        )
        source = padm[:, None] * (pvolt[0] * angle_cos_factor - pvolt[1] * angle_sin_factor)
        stacked = jnp.concatenate([inward, drive, source], axis=0)
        right = hist_now + jnp.dot(onehot, stacked, precision=HIGHEST)
        volt = jnp.dot(ginv, right, precision=HIGHEST)
        probe = jnp.dot(picker, volt, precision=HIGHEST)
        at_line = probe[:lines]
        inverter_emf = probe[lines : lines + convs]
        at_port = probe[lines + convs :]
        outward = 2.0 * ladm[:, None] * at_line - inward
        flow = source - padm[:, None] * at_port
        acc_re = acc_re + flow * angle_cos_factor
        acc_im = acc_im - flow * angle_sin_factor
        unclipped_axial_part = (
            inverter_axial_part
            + slew_limit * (setpoint_flow[0] - inverter_axial_part)
            - SAG_FACTOR * inverter_emf * angle_cos_factor
        )
        unclipped_normal_part = (
            inverter_normal_part
            + slew_limit * (setpoint_flow[1] - inverter_normal_part)
            + SAG_FACTOR * inverter_emf * angle_sin_factor
        )
        inverter_axial_part = jnp.where(
            live, limit * jnp.tanh(unclipped_axial_part / limit), inverter_axial_part
        )
        inverter_normal_part = jnp.where(
            live, limit * jnp.tanh(unclipped_normal_part / limit), inverter_normal_part
        )
        hist_now = 2.0 * gcap[:, None] * volt - hist_now
        return ((hist_now, inverter_axial_part, inverter_normal_part, acc_re, acc_im), outward)

    zeros = jnp.zeros(pvolt.shape[1:], dtype=jnp.float32)
    carry = (start_hist, cstate[0], cstate[1], zeros, zeros)
    carry, outward = lax.scan(advance, carry, (incoming, angles))
    hist_end, inverter_axial_part, inverter_normal_part, acc_re, acc_im = carry
    current = jnp.stack([acc_re, acc_im]) * jnp.float32(2.0 / STEPS)
    return (outward, hist_end, jnp.stack([inverter_axial_part, inverter_normal_part]), current)


def per_device(
    conductance_inverse,
    cap_history,
    cap_conductance,
    wave_history,
    line_partner,
    line_node,
    line_delay,
    line_admittance,
    conv_node,
    conv_count,
    conv_state,
    conv_reference,
    conv_rate,
    conv_limit,
    port_node,
    port_admittance,
    port_voltage_prev,
    port_bus,
    transfer_impedance,
):
    subnets = lax.axis_size(AREA_ROW)
    own = lax.axis_index(AREA_ROW)
    history = wave_history[0]
    lines = history.shape[1]
    partner = line_partner[0]
    offset = (partner - own) % subnets
    signed = jnp.where(offset > subnets // 2, offset - subnets, offset)
    remote = (jnp.arange(lines, dtype=jnp.int32) + lines // 2) % lines
    combined = jnp.zeros(history.shape, jnp.float32)
    for reach in (1, -1, 2, -2):
        count = NEAR if abs(reach) == 1 else lines // 2 - NEAR
        sending = signed == reach
        order = jnp.argsort(jnp.where(sending, 0, 1), stable=True)[:count]
        packed = jnp.take(history, order, axis=1)
        arrived = from_behind(packed, AREA_ROW, reach)
        rank = jnp.cumsum(sending.astype(jnp.int32)) - 1
        slot = jnp.clip(rank[remote], 0, count - 1)
        picked = jnp.take(arrived, slot, axis=1)
        combined = combined + jnp.where((signed == -reach)[None, :, None], picked, 0.0)
    delay = line_delay[0]
    where_now = jnp.arange(STEPS, dtype=jnp.int32)[:, None] - delay[None, :] + HIST
    select = (where_now[:, None, :] == jnp.arange(HIST, dtype=jnp.int32)[None, :, None]).astype(
        jnp.float32
    )
    incoming = jnp.einsum("thl,hlc->tlc", select, combined, precision=HIGHEST)
    outward, hist_end, conv_out, current = window(
        conductance_inverse[0],
        cap_history[0],
        cap_conductance[0],
        incoming,
        line_node[0],
        line_admittance[0],
        conv_node[0],
        conv_count[0],
        conv_state[0],
        conv_reference[0],
        conv_rate[0],
        conv_limit[0],
        port_node[0],
        port_admittance[0],
        port_voltage_prev[:, 0],
    )
    bus_rows = transfer_impedance.shape[1]
    cases = current.shape[2]
    piece = collect(current[:, None], "row", 1)
    members = piece.shape[1]
    ports = piece.shape[2]
    flat = piece.reshape(2, members * ports, cases)
    real = jnp.dot(transfer_impedance[0], flat[0], precision=HIGHEST) - jnp.dot(
        transfer_impedance[1], flat[1], precision=HIGHEST
    )
    imag = jnp.dot(transfer_impedance[0], flat[1], precision=HIGHEST) + jnp.dot(
        transfer_impedance[1], flat[0], precision=HIGHEST
    )
    partial_bus = jnp.stack([real, imag])
    bus_voltage = sum_by_parts(partial_bus, AREA, (0, 1))
    first_row = lax.axis_index("row") * bus_rows
    local_bus = (port_bus - first_row).reshape(-1)
    pick_rows = (local_bus[:, None] == jnp.arange(bus_rows, dtype=jnp.int32)[None, :]).astype(
        jnp.float32
    )
    gathered = jnp.einsum("jb,xbc->xjc", pick_rows, bus_voltage, precision=HIGHEST)
    gathered = gathered.reshape(2, port_bus.shape[0], port_bus.shape[1], cases)
    port_voltage = sum_at_owner(gathered, "row", 1)
    return (outward[None], hist_end[None], conv_out[None], bus_voltage, port_voltage)


def solution(mesh):
    torus = Mesh(mesh.devices.reshape(8, 4, mesh.shape["row"]), ("area_0", "area_1", "row"))
    return jax.shard_map(
        per_device,
        mesh=torus,
        in_specs=(
            P(AREA_ROW, None, None),
            P(AREA_ROW, None, None),
            P(AREA_ROW, None),
            P(AREA_ROW, None, None, None),
            P(AREA_ROW, None),
            P(AREA_ROW, None),
            P(AREA_ROW, None),
            P(AREA_ROW, None),
            P(AREA_ROW, None),
            P(AREA_ROW),
            P(AREA_ROW, None, None, None),
            P(AREA_ROW, None, None, None),
            P(AREA_ROW, None),
            P(AREA_ROW, None),
            P(AREA_ROW, None),
            P(AREA_ROW, None),
            P(None, AREA_ROW, None, None),
            P(AREA, None),
            P(None, "row", AREA),
        ),
        out_specs=(
            P(AREA_ROW, None, None, None),
            P(AREA_ROW, None, None),
            P(AREA_ROW, None, None, None),
            P(None, "row", None),
            P(None, AREA_ROW, None, None),
        ),
        check_vma=False,
    )
```

profile of v0, /device:TPU:2, one launch (start us, length us, event | category | flops | bytes accessed | tf_op | source)
XLA Modules:
  0.0 458.9 jit_solution(6466544314705339276)
XLA Ops:
  15.5 2.6 collective-permute-start.3
  34.7 2.7 convolution_bitcast_fusion.2
  37.5 253.8 %while.23 = (s32[]{:T(128)}, f32[1024,128]{0,1:T(8,128)S(1)}, f32[64,128]{1,0:T(8,128)S(1)}, f32[64,128]{1,0:T(8,128)S(1)}, f32[8,128]{1,0:T(8,128)S(1)}, /*inde...) while((s32[]{:T(128)}, f32[1024,128]{0,1:T(8,128)S(1)}, ...), condition=%wide.region_9.14_spmd.clone.clone.clone, body=%wide.region_8.13_spmd.clone.clone.clone.sunk | while | flops 1938803712 | bytes 8437999 | solution.py:156
  42.0 6.7 %bitcast_subtract_fusion.4 = (f32[1024,128]{0,1:T(8,128)S(1)}, f32[128,1024]{1,0:T(8,128)S(1)}) fusion(f32[1024,128]{0,1:T(8,128)S(1)} %get-tuple-element.576, f32[1024]{0:T(1024)S(1)} %bitcast.228, f32[1024,128]{0,1:T(8,128)S(1)} %fusion.99, f32[1024,1024]{1,0:T(8,128)} %get-tuple-element.609), kind=kOutput, calls=%fused_computation.18.clone.1 | convolution fusion | flops 1610874880 | bytes 6295552 | tf_op jit(solution)/shard_map/while/body/eval_jaxpr/dot_general | solution.py:126
  54.7 6.7 %bitcast_subtract_fusion.4 = (f32[1024,128]{0,1:T(8,128)S(1)}, f32[128,1024]{1,0:T(8,128)S(1)}) fusion(f32[1024,128]{0,1:T(8,128)S(1)} %get-tuple-element.576, f32[1024]{0:T(1024)S(1)} %bitcast.228, f32[1024,128]{0,1:T(8,128)S(1)} %fusion.99, f32[1024,1024]{1,0:T(8,128)} %get-tuple-element.609), kind=kOutput, calls=%fused_computation.18.clone.1 | convolution fusion | flops 1610874880 | bytes 6295552 | tf_op jit(solution)/shard_map/while/body/eval_jaxpr/dot_general | solution.py:126
  67.4 6.7 %bitcast_subtract_fusion.4 = (f32[1024,128]{0,1:T(8,128)S(1)}, f32[128,1024]{1,0:T(8,128)S(1)}) fusion(f32[1024,128]{0,1:T(8,128)S(1)} %get-tuple-element.576, f32[1024]{0:T(1024)S(1)} %bitcast.228, f32[1024,128]{0,1:T(8,128)S(1)} %fusion.99, f32[1024,1024]{1,0:T(8,128)} %get-tuple-element.609), kind=kOutput, calls=%fused_computation.18.clone.1 | convolution fusion | flops 1610874880 | bytes 6295552 | tf_op jit(solution)/shard_map/while/body/eval_jaxpr/dot_general | solution.py:126
  80.0 6.7 %bitcast_subtract_fusion.4 = (f32[1024,128]{0,1:T(8,128)S(1)}, f32[128,1024]{1,0:T(8,128)S(1)}) fusion(f32[1024,128]{0,1:T(8,128)S(1)} %get-tuple-element.576, f32[1024]{0:T(1024)S(1)} %bitcast.228, f32[1024,128]{0,1:T(8,128)S(1)} %fusion.99, f32[1024,1024]{1,0:T(8,128)} %get-tuple-element.609), kind=kOutput, calls=%fused_computation.18.clone.1 | convolution fusion | flops 1610874880 | bytes 6295552 | tf_op jit(solution)/shard_map/while/body/eval_jaxpr/dot_general | solution.py:126
  92.7 6.7 %bitcast_subtract_fusion.4 = (f32[1024,128]{0,1:T(8,128)S(1)}, f32[128,1024]{1,0:T(8,128)S(1)}) fusion(f32[1024,128]{0,1:T(8,128)S(1)} %get-tuple-element.576, f32[1024]{0:T(1024)S(1)} %bitcast.228, f32[1024,128]{0,1:T(8,128)S(1)} %fusion.99, f32[1024,1024]{1,0:T(8,128)} %get-tuple-element.609), kind=kOutput, calls=%fused_computation.18.clone.1 | convolution fusion | flops 1610874880 | bytes 6295552 | tf_op jit(solution)/shard_map/while/body/eval_jaxpr/dot_general | solution.py:126
  105.4 6.7 %bitcast_subtract_fusion.4 = (f32[1024,128]{0,1:T(8,128)S(1)}, f32[128,1024]{1,0:T(8,128)S(1)}) fusion(f32[1024,128]{0,1:T(8,128)S(1)} %get-tuple-element.576, f32[1024]{0:T(1024)S(1)} %bitcast.228, f32[1024,128]{0,1:T(8,128)S(1)} %fusion.99, f32[1024,1024]{1,0:T(8,128)} %get-tuple-element.609), kind=kOutput, calls=%fused_computation.18.clone.1 | convolution fusion | flops 1610874880 | bytes 6295552 | tf_op jit(solution)/shard_map/while/body/eval_jaxpr/dot_general | solution.py:126
  118.1 6.7 %bitcast_subtract_fusion.4 = (f32[1024,128]{0,1:T(8,128)S(1)}, f32[128,1024]{1,0:T(8,128)S(1)}) fusion(f32[1024,128]{0,1:T(8,128)S(1)} %get-tuple-element.576, f32[1024]{0:T(1024)S(1)} %bitcast.228, f32[1024,128]{0,1:T(8,128)S(1)} %fusion.99, f32[1024,1024]{1,0:T(8,128)} %get-tuple-element.609), kind=kOutput, calls=%fused_computation.18.clone.1 | convolution fusion | flops 1610874880 | bytes 6295552 | tf_op jit(solution)/shard_map/while/body/eval_jaxpr/dot_general | solution.py:126
  130.8 6.7 %bitcast_subtract_fusion.4 = (f32[1024,128]{0,1:T(8,128)S(1)}, f32[128,1024]{1,0:T(8,128)S(1)}) fusion(f32[1024,128]{0,1:T(8,128)S(1)} %get-tuple-element.576, f32[1024]{0:T(1024)S(1)} %bitcast.228, f32[1024,128]{0,1:T(8,128)S(1)} %fusion.99, f32[1024,1024]{1,0:T(8,128)} %get-tuple-element.609), kind=kOutput, calls=%fused_computation.18.clone.1 | convolution fusion | flops 1610874880 | bytes 6295552 | tf_op jit(solution)/shard_map/while/body/eval_jaxpr/dot_general | solution.py:126
  143.5 6.7 %bitcast_subtract_fusion.4 = (f32[1024,128]{0,1:T(8,128)S(1)}, f32[128,1024]{1,0:T(8,128)S(1)}) fusion(f32[1024,128]{0,1:T(8,128)S(1)} %get-tuple-element.576, f32[1024]{0:T(1024)S(1)} %bitcast.228, f32[1024,128]{0,1:T(8,128)S(1)} %fusion.99, f32[1024,1024]{1,0:T(8,128)} %get-tuple-element.609), kind=kOutput, calls=%fused_computation.18.clone.1 | convolution fusion | flops 1610874880 | bytes 6295552 | tf_op jit(solution)/shard_map/while/body/eval_jaxpr/dot_general | solution.py:126
  156.2 6.7 %bitcast_subtract_fusion.4 = (f32[1024,128]{0,1:T(8,128)S(1)}, f32[128,1024]{1,0:T(8,128)S(1)}) fusion(f32[1024,128]{0,1:T(8,128)S(1)} %get-tuple-element.576, f32[1024]{0:T(1024)S(1)} %bitcast.228, f32[1024,128]{0,1:T(8,128)S(1)} %fusion.99, f32[1024,1024]{1,0:T(8,128)} %get-tuple-element.609), kind=kOutput, calls=%fused_computation.18.clone.1 | convolution fusion | flops 1610874880 | bytes 6295552 | tf_op jit(solution)/shard_map/while/body/eval_jaxpr/dot_general | solution.py:126
  168.9 6.7 %bitcast_subtract_fusion.4 = (f32[1024,128]{0,1:T(8,128)S(1)}, f32[128,1024]{1,0:T(8,128)S(1)}) fusion(f32[1024,128]{0,1:T(8,128)S(1)} %get-tuple-element.576, f32[1024]{0:T(1024)S(1)} %bitcast.228, f32[1024,128]{0,1:T(8,128)S(1)} %fusion.99, f32[1024,1024]{1,0:T(8,128)} %get-tuple-element.609), kind=kOutput, calls=%fused_computation.18.clone.1 | convolution fusion | flops 1610874880 | bytes 6295552 | tf_op jit(solution)/shard_map/while/body/eval_jaxpr/dot_general | solution.py:126
  181.6 6.7 %bitcast_subtract_fusion.4 = (f32[1024,128]{0,1:T(8,128)S(1)}, f32[128,1024]{1,0:T(8,128)S(1)}) fusion(f32[1024,128]{0,1:T(8,128)S(1)} %get-tuple-element.576, f32[1024]{0:T(1024)S(1)} %bitcast.228, f32[1024,128]{0,1:T(8,128)S(1)} %fusion.99, f32[1024,1024]{1,0:T(8,128)} %get-tuple-element.609), kind=kOutput, calls=%fused_computation.18.clone.1 | convolution fusion | flops 1610874880 | bytes 6295552 | tf_op jit(solution)/shard_map/while/body/eval_jaxpr/dot_general | solution.py:126
  194.3 6.7 %bitcast_subtract_fusion.4 = (f32[1024,128]{0,1:T(8,128)S(1)}, f32[128,1024]{1,0:T(8,128)S(1)}) fusion(f32[1024,128]{0,1:T(8,128)S(1)} %get-tuple-element.576, f32[1024]{0:T(1024)S(1)} %bitcast.228, f32[1024,128]{0,1:T(8,128)S(1)} %fusion.99, f32[1024,1024]{1,0:T(8,128)} %get-tuple-element.609), kind=kOutput, calls=%fused_computation.18.clone.1 | convolution fusion | flops 1610874880 | bytes 6295552 | tf_op jit(solution)/shard_map/while/body/eval_jaxpr/dot_general | solution.py:126
  207.0 6.7 %bitcast_subtract_fusion.4 = (f32[1024,128]{0,1:T(8,128)S(1)}, f32[128,1024]{1,0:T(8,128)S(1)}) fusion(f32[1024,128]{0,1:T(8,128)S(1)} %get-tuple-element.576, f32[1024]{0:T(1024)S(1)} %bitcast.228, f32[1024,128]{0,1:T(8,128)S(1)} %fusion.99, f32[1024,1024]{1,0:T(8,128)} %get-tuple-element.609), kind=kOutput, calls=%fused_computation.18.clone.1 | convolution fusion | flops 1610874880 | bytes 6295552 | tf_op jit(solution)/shard_map/while/body/eval_jaxpr/dot_general | solution.py:126
  219.6 6.7 %bitcast_subtract_fusion.4 = (f32[1024,128]{0,1:T(8,128)S(1)}, f32[128,1024]{1,0:T(8,128)S(1)}) fusion(f32[1024,128]{0,1:T(8,128)S(1)} %get-tuple-element.576, f32[1024]{0:T(1024)S(1)} %bitcast.228, f32[1024,128]{0,1:T(8,128)S(1)} %fusion.99, f32[1024,1024]{1,0:T(8,128)} %get-tuple-element.609), kind=kOutput, calls=%fused_computation.18.clone.1 | convolution fusion | flops 1610874880 | bytes 6295552 | tf_op jit(solution)/shard_map/while/body/eval_jaxpr/dot_general | solution.py:126
  232.3 6.7 %bitcast_subtract_fusion.4 = (f32[1024,128]{0,1:T(8,128)S(1)}, f32[128,1024]{1,0:T(8,128)S(1)}) fusion(f32[1024,128]{0,1:T(8,128)S(1)} %get-tuple-element.576, f32[1024]{0:T(1024)S(1)} %bitcast.228, f32[1024,128]{0,1:T(8,128)S(1)} %fusion.99, f32[1024,1024]{1,0:T(8,128)} %get-tuple-element.609), kind=kOutput, calls=%fused_computation.18.clone.1 | convolution fusion | flops 1610874880 | bytes 6295552 | tf_op jit(solution)/shard_map/while/body/eval_jaxpr/dot_general | solution.py:126
  245.0 6.7 %bitcast_subtract_fusion.4 = (f32[1024,128]{0,1:T(8,128)S(1)}, f32[128,1024]{1,0:T(8,128)S(1)}) fusion(f32[1024,128]{0,1:T(8,128)S(1)} %get-tuple-element.576, f32[1024]{0:T(1024)S(1)} %bitcast.228, f32[1024,128]{0,1:T(8,128)S(1)} %fusion.99, f32[1024,1024]{1,0:T(8,128)} %get-tuple-element.609), kind=kOutput, calls=%fused_computation.18.clone.1 | convolution fusion | flops 1610874880 | bytes 6295552 | tf_op jit(solution)/shard_map/while/body/eval_jaxpr/dot_general | solution.py:126
  257.7 6.7 %bitcast_subtract_fusion.4 = (f32[1024,128]{0,1:T(8,128)S(1)}, f32[128,1024]{1,0:T(8,128)S(1)}) fusion(f32[1024,128]{0,1:T(8,128)S(1)} %get-tuple-element.576, f32[1024]{0:T(1024)S(1)} %bitcast.228, f32[1024,128]{0,1:T(8,128)S(1)} %fusion.99, f32[1024,1024]{1,0:T(8,128)} %get-tuple-element.609), kind=kOutput, calls=%fused_computation.18.clone.1 | convolution fusion | flops 1610874880 | bytes 6295552 | tf_op jit(solution)/shard_map/while/body/eval_jaxpr/dot_general | solution.py:126
  270.4 6.7 %bitcast_subtract_fusion.4 = (f32[1024,128]{0,1:T(8,128)S(1)}, f32[128,1024]{1,0:T(8,128)S(1)}) fusion(f32[1024,128]{0,1:T(8,128)S(1)} %get-tuple-element.576, f32[1024]{0:T(1024)S(1)} %bitcast.228, f32[1024,128]{0,1:T(8,128)S(1)} %fusion.99, f32[1024,1024]{1,0:T(8,128)} %get-tuple-element.609), kind=kOutput, calls=%fused_computation.18.clone.1 | convolution fusion | flops 1610874880 | bytes 6295552 | tf_op jit(solution)/shard_map/while/body/eval_jaxpr/dot_general | solution.py:126
  283.1 6.7 %bitcast_subtract_fusion.4 = (f32[1024,128]{0,1:T(8,128)S(1)}, f32[128,1024]{1,0:T(8,128)S(1)}) fusion(f32[1024,128]{0,1:T(8,128)S(1)} %get-tuple-element.576, f32[1024]{0:T(1024)S(1)} %bitcast.228, f32[1024,128]{0,1:T(8,128)S(1)} %fusion.99, f32[1024,1024]{1,0:T(8,128)} %get-tuple-element.609), kind=kOutput, calls=%fused_computation.18.clone.1 | convolution fusion | flops 1610874880 | bytes 6295552 | tf_op jit(solution)/shard_map/while/body/eval_jaxpr/dot_general | solution.py:126
  291.4 10.1 %all_to_all.10 = f32[8,2,1,8,128]{4,3,2,1,0:T(8,128)S(1)} all-to-all(f32[8,2,1,8,128]{4,3,2,1,0:T(8,128)S(1)} %broadcast_in_dim.148), channel_id=1, replica_groups=mesh['area_0'=8,'area_1'=4,'row'=8] {'row'}, dimensions={0} | all-to-all | bytes 131072 | tf_op jit(solution)/shard_map/all_to_all | solution.py:33
  306.6 2.1 copy.46
  308.8 47.2 %reduce-scatter.3.cloned.1.call-done = f32[4,160,128]{2,1,0:T(8,128)} async-done(((f32[32,160,128]{2,1,0:T(8,128)}), f32[4,160,128]{2,1,0:T(8,128)}) %reduce-scatter.3.cloned.1.call-update) | async-done | bytes 327696 | tf_op jit(solution)/shard_map/reduce_scatter | solution.py:52
  356.1 23.2 %reduce-scatter.5.cloned.1.call-done = f32[1,160,128]{2,1,0:T(8,128)} async-done(((f32[4,160,128]{2,1,0:T(8,128)}), f32[1,160,128]{2,1,0:T(8,128)}) %reduce-scatter.5.cloned.1.call-update) | async-done | bytes 81936 | tf_op jit(solution)/shard_map/reduce_scatter | solution.py:52
  379.3 13.9 %all_gather.9 = f32[4,160,128]{2,1,0:T(8,128)} all-gather(f32[1,160,128]{2,1,0:T(8,128)} %reduce-scatter.5.cloned.1.call-done), channel_id=1, replica_groups=mesh['area_0'=8,'area_1'=4,'row'=8] {'area_1'}, dimensions={0}, use_global_device_ids=true | all-gather | bytes 409600 | tf_op jit(solution)/shard_map/all_gather | solution.py:59
  394.4 42.3 %all-gather.3.cloned.1.call-done = f32[32,160,128]{2,1,0:T(8,128)} async-done(((f32[4,160,128]{2,1,0:T(8,128)}), f32[32,160,128]{2,1,0:T(8,128)}) %all-gather.3.cloned.1.call-update) | async-done | bytes 2621456 | tf_op jit(solution)/shard_map/all_gather | solution.py:59
  436.7 3.1 convolution_bitcast_fusion.3
  440.4 4.3 all-to-all-start.1
  445.3 5.0 %all-to-all-done.1 = f32[8,2,1,8,128]{4,3,1,2,0:T(8,128)S(1)} async-done(((f32[8,2,1,8,128]{4,3,1,2,0:T(8,128)}), f32[8,2,1,8,128]{4,3,1,2,0:T(8,128)S(1)}, u32[]{:S(2)}, u32[]{:S(2)}) %all-to-all-start.1) | async-done | bytes 65568 | tf_op jit(solution)/shard_map/all_to_all | solution.py:81
  (382 shorter events, 123.9 us)
Async XLA Ops:
  7.2 348.8 %reduce-scatter.3.cloned.1.call-start = ((), (), s32[]{:S(2)}) async-start(), calls=%async_computation.4 | async-start | bytes 2949120 | tf_op jit(solution)/shard_map/reduce_scatter | solution.py:52
  11.6 19.4 %collective-permute-start.2 = (f32[40,4,128]{2,0,1:T(8,128)S(1)}, f32[40,4,128]{2,0,1:T(8,128)S(1)}, u32[]{:S(2)}, u32[]{:S(2)}) collective-permute-start(f32[40,4,128]{2,0,1:T(8,128)S(1)} %select_bitcast_fusion.3), channel_id=1, source_target_pairs={{0,2},{1,3},{2,4},{3,5},{4,6},{5,7},{6,8},{7,9},{8,10},{9,11},{10,... | collective-permute-start | bytes 245768 | tf_op jit(solution)/shard_map/ppermute | solution.py:22
  14.9 8.5 %copy-start.14 = (s32[1,32]{1,0:T(1,128)S(1)}, s32[1,32]{1,0:T(1,128)}, u32[]{:S(2)}) copy-start(s32[1,32]{1,0:T(1,128)} %param.33) | copy-start | bytes 388
  14.9 9.3 %copy-start.13 = (s32[1,32]{1,0:T(1,128)S(1)}, s32[1,32]{1,0:T(1,128)}, u32[]{:S(2)}) copy-start(s32[1,32]{1,0:T(1,128)} %param.35) | copy-start | bytes 388
  15.5 14.9 %collective-permute-start.3 = (f32[40,4,128]{2,0,1:T(8,128)S(1)}, f32[40,4,128]{2,0,1:T(8,128)S(1)}, u32[]{:S(2)}, u32[]{:S(2)}) collective-permute-start(f32[40,4,128]{2,0,1:T(8,128)S(1)} %select_bitcast_fusion.2), channel_id=1, source_target_pairs={{0,254},{1,255},{2,0},{3,1},{4,2},{5,3},{6,4},{7,5},{8,6},{9,7},{1... | collective-permute-start | bytes 245768 | tf_op jit(solution)/shard_map/ppermute | solution.py:22
  20.4 12.7 %collective-permute-start.1 = (f32[40,12,128]{2,0,1:T(8,128)S(1)}, f32[40,12,128]{2,0,1:T(8,128)S(1)}, u32[]{:S(2)}, u32[]{:S(2)}) collective-permute-start(f32[40,12,128]{2,0,1:T(8,128)S(1)} %select_bitcast_fusion), channel_id=1, source_target_pairs={{0,255},{1,0},{2,1},{3,2},{4,3},{5,4},{6,5},{7,6},{8,7},{9,8},{10,... | collective-permute-start | bytes 737288 | tf_op jit(solution)/shard_map/ppermute | solution.py:22
  22.8 6.8 %copy-start.7 = (f32[1,2,64,128]{3,2,1,0:T(8,128)S(1)}, f32[1,2,64,128]{3,2,1,0:T(8,128)}, u32[]{:S(2)}) copy-start(f32[1,2,64,128]{3,2,1,0:T(8,128)} %param.39) | copy-start | bytes 196612
  22.8 7.3 %copy-start.5 = (f32[1,1024,128]{2,1,0:T(8,128)S(1)}, f32[1,1024,128]{2,1,0:T(8,128)}, u32[]{:S(2)}) copy-start(f32[1,1024,128]{2,1,0:T(8,128)} %param.30) | copy-start | bytes 1572868
  22.8 9.7 %collective-permute-start = (f32[40,12,128]{2,0,1:T(8,128)S(1)}, f32[40,12,128]{2,0,1:T(8,128)S(1)}, u32[]{:S(2)}, u32[]{:S(2)}) collective-permute-start(f32[40,12,128]{2,0,1:T(8,128)S(1)} %select_bitcast_fusion.1), channel_id=1, source_target_pairs={{0,1},{1,2},{2,3},{3,4},{4,5},{5,6},{6,7},{7,8},{8,9},{9,10},{10,1... | collective-permute-start | bytes 737288 | tf_op jit(solution)/shard_map/ppermute | solution.py:22
  26.6 3.7 copy-start.15
  26.6 3.7 copy-start.16
  26.6 3.7 copy-start.17
  32.5 2.1 copy-start.18
  32.5 2.1 copy-start.19
  32.5 2.1 copy-start.20
  32.5 2.1 copy-start.21
  32.5 2.1 copy-start.22
  32.5 2.1 copy-start.23
  34.6 2.8 copy-start.2
  34.6 2.8 copy-start.3
  34.6 2.8 copy-start.6
  34.7 2.8 copy-start.8
  34.7 2.8 copy-start.10
  34.7 2.8 copy-start.11
  34.7 2.8 copy-start.24
  34.7 2.8 copy-start.25
  37.5 263.9 %copy-start.1 = (f32[2,2560,64]{1,2,0:T(8,128)S(1)}, f32[2,2560,64]{1,2,0:T(8,128)}, u32[]{:S(2)}) copy-start(f32[2,2560,64]{1,2,0:T(8,128)} %param.47) | copy-start | bytes 3932164
  308.7 84.5 %copy-start.12 = (s32[8,8]{1,0:T(8,128)S(1)}, s32[8,8]{1,0:T(8,128)}, u32[]{:S(2)}) copy-start(s32[8,8]{1,0:T(8,128)} %param.46) | copy-start | bytes 772
  308.8 70.6 %reduce-scatter.5.cloned.1.call-start = ((), (), s32[]{:S(2)}) async-start(), calls=%async_computation.5 | async-start | bytes 409600 | tf_op jit(solution)/shard_map/reduce_scatter | solution.py:52
  356.0 80.7 %all-gather.3.cloned.1.call-start = ((), (), s32[]{:S(2)}) async-start(), calls=%async_computation.6 | async-start | bytes 2949120 | tf_op jit(solution)/shard_map/all_gather | solution.py:59
  436.7 14.2 %copy-start = (f32[32,160,128]{2,1,0:T(8,128)S(1)}, f32[32,160,128]{2,1,0:T(8,128)}, u32[]{:S(2)}) copy-start(f32[32,160,128]{2,1,0:T(8,128)} %all-gather.3.cloned.1.call-done) | copy-start | bytes 7864324
  440.4 9.9 %all-to-all-start.1 = ((f32[8,2,1,8,128]{4,3,1,2,0:T(8,128)}), f32[8,2,1,8,128]{4,3,1,2,0:T(8,128)S(1)}, u32[]{:S(2)}, u32[]{:S(2)}) async-start(f32[8,2,1,8,128]{4,3,1,2,0:T(8,128)} %bitcast.169), calls=%async_computation.3 | async-start | bytes 131072 | tf_op jit(solution)/shard_map/all_to_all | solution.py:81
  (2 other events, 3.6 us)
Sparse Core Ops, SparseCore 0:
  308.9 47.0 reduce-scatter.2
  358.5 20.7 reduce-scatter.4
  393.4 43.2 all-gather.2
where the time goes:
time: 462 us; the launch traced here: 459 us
  matrix products  171 us (37%)
  waiting for transfers between devices  118 us (26%)
  local copies, waits for them, and re-layouts  46.3 us (10%)
  other arithmetic  46 us (10%)
  loops' own time  29.9 us (6%)
  blocking collectives  24 us (5%)
  between operations  14.3 us (3%)
  starting transfers between devices  9.23 us (2%)
    dot_general x20, matrix products, advance(): volt = jnp.dot(ginv, right, precision=HIGHEST)  134 us
    reduce_scatter x2, waiting for transfers between devices, own_block(): parts = lax.psum_scatter(parts, axes[k], scatter_dimension=0, tiled=True)  70.4 us
    all_gather x1, waiting for transfers between devices, stacked_from(): parts = lax.all_gather(parts, axes[k])  42.3 us
    dynamic_slice x40, local copies, waits for them, and re-layouts, window(): carry, outward = lax.scan(advance, carry, (incoming, angles))  30 us
    another operation x1, loops' own time, window(): carry, outward = lax.scan(advance, carry, (incoming, angles))  29.9 us
    all_gather x1, blocking collectives, stacked_from(): parts = lax.all_gather(parts, axes[k])  13.9 us
    dynamic_update_slice x20, other arithmetic, window(): carry, outward = lax.scan(advance, carry, (incoming, angles))  13.7 us
    dot_general x20, matrix products, advance(): probe = jnp.dot(picker, volt, precision=HIGHEST)  13.4 us
  transfers between devices with their start and end apart: 8, of which 4 were waited for; matrix products, arithmetic and copies ran while one was open for 4% of the time, Pallas kernels for 0%

commit v1 on v0

v1 whole, which is shorter than its diff:
```python
import math

import jax
import jax.numpy as jnp
import numpy as np
from jax import lax
from jax.experimental import pallas as pl
from jax.experimental.pallas import tpu as pltpu
from jax.sharding import Mesh
from jax.sharding import PartitionSpec as P

STEPS = 20
HIST = 40
NEAR = 12
LINES = 32
CONV = 64
PORTS = 8
HALF = LINES // 2
PROBES = LINES + CONV + PORTS
SAG_FACTOR = 0.3
ALL = ("z", "x", "y", "core")
AREA = ("z", "x")
ROW = ("y", "core")
F32 = jnp.float32
BF16 = jnp.bfloat16

AT_DELAY = 128
AT_PARTNER = 160
AT_COUNT = 192


def dot(a, b):
    return jnp.dot(a, b, preferred_element_type=F32)


def split(x):
    high = x.astype(BF16)
    return high, (x - high.astype(F32)).astype(BF16)


def reach_of(table, line, base):
    return jnp.bitwise_and(table[base + line] - table[base + HALF + line], 255) // 2


def pack_kernel(partner, waves, near_up, far_up, near_down, far_down):
    near = jnp.int32(0)
    for line in range(HALF):
        is_near = reach_of(partner, line, 0) == 1
        up = waves[:, line, :]
        down = waves[:, line + HALF, :]

        @pl.when(is_near)
        def _(near=near, up=up, down=down):
            near_up[near] = up
            near_down[near] = down

        @pl.when(jnp.logical_not(is_near))
        def _(far=line - near, up=up, down=down):
            far_up[far] = up
            far_down[far] = down

        near = near + is_near.astype(jnp.int32)


def pack(partner, waves):
    hist, _, cases = waves.shape
    near = jax.ShapeDtypeStruct((NEAR, hist, cases), F32)
    far = jax.ShapeDtypeStruct((HALF - NEAR, hist, cases), F32)
    vmem = pl.BlockSpec(memory_space=pltpu.VMEM)
    return pl.pallas_call(
        pack_kernel,
        out_shape=(near, far, near, far),
        in_specs=[pl.BlockSpec(memory_space=pltpu.SMEM), vmem],
        out_specs=(vmem,) * 4,
        name="pack_waves",
    )(partner, waves)


def column(row):
    return jnp.broadcast_to(row, (128, 128)).T


def window_kernel(
    table,
    angle,
    g_hbm,
    hist0,
    near_up,
    far_up,
    near_down,
    far_down,
    nodes_row,
    gcap,
    line_row,
    rate_row,
    state0,
    setpoint,
    pvolt,
    waves,
    hist_out,
    state_out,
    current,
    g_in,
    g_high,
    g_low,
    arrived,
    incoming,
    w_even,
    w_odd,
    volt,
    probe,
    stack,
    cap2,
    coef,
    g_sem,
    a_sem,
):
    nodes = g_high.shape[0]
    chunks = g_in.shape[0]
    rows = nodes // chunks
    copies = [
        pltpu.make_async_copy(g_hbm.at[pl.ds(i * rows, rows)], g_in.at[i], g_sem.at[i])
        for i in range(chunks)
    ]
    for copy in copies:
        copy.start()
    first = 0
    moves = []
    for i, part in enumerate((near_up, far_up, near_down, far_down)):
        size = part.shape[0]
        moves.append(
            pltpu.make_async_copy(part, arrived.at[pl.ds(first, size)], a_sem.at[i])
        )
        first += size
    for move in moves:
        move.start()

    coef[0] = column(line_row[...])
    coef[1] = column(rate_row[...])
    for i in range(nodes // 128):
        cap2[pl.ds(i * 128, 128)] = 2.0 * column(gcap[:, pl.ds(i * 128, 128)])
    hist_out[...] = hist0[...]
    high, low = split(hist0[...])
    w_even[pl.ds(0, nodes), pl.ds(0, 128)] = high
    w_even[pl.ds(0, nodes), pl.ds(128, 128)] = low
    zeros = jnp.zeros((256, 128), BF16)
    for w in (w_even, w_odd):
        w[pl.ds(nodes, 256), pl.ds(0, 128)] = zeros
        w[pl.ds(nodes, 256), pl.ds(128, 128)] = zeros
    state_out[...] = state0[...]
    current[...] = jnp.zeros_like(current)
    stack[...] = jnp.zeros_like(stack)

    picks = (
        lax.broadcasted_iota(jnp.int32, (nodes, 128), 0) == nodes_row[...]
    ).astype(BF16)
    for i, copy in enumerate(copies):
        copy.wait()
        high, low = split(g_in[i])
        at = pl.ds(i * rows, rows)
        g_high[at, pl.ds(0, nodes)] = high
        g_low[at, :] = low
        g_high[at, pl.ds(nodes, 128)] = dot(high, picks).astype(BF16)
        g_high[at, pl.ds(nodes + 128, 128)] = dot(low, picks).astype(BF16)

    for move in moves:
        move.wait()
    near = jnp.int32(0)
    for line in range(HALF):
        is_near = reach_of(table, line, AT_PARTNER) == 1
        place = jnp.where(is_near, near, NEAR + line - near)
        near = near + is_near.astype(jnp.int32)
        for slot, at in ((line + HALF, place), (line, place + HALF)):
            start = HIST - table[AT_DELAY + slot]
            incoming[:, slot, :] = arrived[at, pl.ds(start, STEPS), :]

    line_adm = 2.0 * coef[0, :LINES]
    limit = coef[0, LINES : LINES + CONV]
    padm = coef[0, LINES + CONV : PROBES]
    rate = coef[1, LINES : LINES + CONV]
    inverse = 1.0 / limit
    live = lax.broadcasted_iota(jnp.int32, (CONV, 128), 0) < table[AT_COUNT]

    def step(t, w, w_next):
        cos, sin = angle[0, t], angle[1, t]
        axial, normal = state_out[0], state_out[1]
        inward = incoming[t]
        source = padm * (pvolt[0] * cos - pvolt[1] * sin)
        stack[pl.ds(0, LINES)] = inward
        stack[pl.ds(LINES, CONV)] = jnp.where(live, axial * cos - normal * sin, 0.0)
        stack[pl.ds(LINES + CONV, PORTS)] = source
        high, low = split(stack[...])
        w[pl.ds(nodes, 128), pl.ds(0, 128)] = high
        w[pl.ds(nodes, 128), pl.ds(128, 128)] = low
        w[pl.ds(nodes + 128, 128), pl.ds(0, 128)] = high
        block = 256
        for i in range(0, nodes, block):
            at = pl.ds(i, block)
            y = dot(g_high[at, :], w[...])
            z = dot(g_low[at, :], w[pl.ds(0, nodes), pl.ds(0, 128)])
            v = y[:, :128] + y[:, 128:] + z
            volt[at, :] = v
            h = cap2[at, :] * v - hist_out[at, :]
            hist_out[at, :] = h
            high, low = split(h)
            w_next[at, pl.ds(0, 128)] = high
            w_next[at, pl.ds(128, 128)] = low
        for k in range(PROBES):
            probe[pl.ds(k, 1), :] = volt[pl.ds(table[k], 1), :]
        emf = probe[pl.ds(LINES, CONV), :]
        new_axial = axial + rate * (setpoint[0] - axial) - (SAG_FACTOR * cos) * emf
        new_normal = normal + rate * (setpoint[1] - normal) + (SAG_FACTOR * sin) * emf
        state_out[0] = jnp.where(live, limit * jnp.tanh(new_axial * inverse), axial)
        state_out[1] = jnp.where(live, limit * jnp.tanh(new_normal * inverse), normal)
        waves[t] = line_adm * probe[pl.ds(0, LINES), :] - inward
        flow = source - padm * probe[pl.ds(LINES + CONV, PORTS), :]
        current[0] = current[0] + flow * cos
        current[1] = current[1] - flow * sin

    def pair(i, _):
        step(2 * i, w_even, w_odd)
        step(2 * i + 1, w_odd, w_even)
        return 0

    lax.fori_loop(0, STEPS // 2, pair, 0)
    current[...] = current[...] * (2.0 / STEPS)


def window(table, nodes_row, angle, ginv, hist0, arrivals, gcap, line_row, rate_row, state, setpoint, pvolt):
    nodes, cases = hist0.shape
    vmem = pl.BlockSpec(memory_space=pltpu.VMEM)
    smem = pl.BlockSpec(memory_space=pltpu.SMEM)
    far = pl.BlockSpec(memory_space=pl.ANY)
    chunks = 8
    return pl.pallas_call(
        window_kernel,
        out_shape=(
            jax.ShapeDtypeStruct((STEPS, LINES, cases), F32),
            jax.ShapeDtypeStruct((nodes, cases), F32),
            jax.ShapeDtypeStruct(state.shape, F32),
            jax.ShapeDtypeStruct((2, PORTS, cases), F32),
        ),
        in_specs=[smem, smem, far, vmem, far, far, far, far] + [vmem] * 7,
        out_specs=(vmem,) * 4,
        scratch_shapes=[
            pltpu.VMEM((chunks, nodes // chunks, nodes), F32),
            pltpu.VMEM((nodes, nodes + 256), BF16),
            pltpu.VMEM((nodes, nodes), BF16),
            pltpu.VMEM((LINES, HIST, cases), F32),
            pltpu.VMEM((STEPS, LINES, cases), F32),
            pltpu.VMEM((nodes + 256, 256), BF16),
            pltpu.VMEM((nodes + 256, 256), BF16),
            pltpu.VMEM((nodes, cases), F32),
            pltpu.VMEM((PROBES, cases), F32),
            pltpu.VMEM((128, cases), F32),
            pltpu.VMEM((nodes, cases), F32),
            pltpu.VMEM((2, 128, cases), F32),
            pltpu.SemaphoreType.DMA((chunks,)),
            pltpu.SemaphoreType.DMA((4,)),
        ],
        compiler_params=pltpu.CompilerParams(vmem_limit_bytes=40 << 20),
        cost_estimate=pl.CostEstimate(
            flops=6 * STEPS * nodes * nodes * cases,
            bytes_accessed=64 << 20,
            transcendentals=0,
        ),
        name="window",
    )(table, angle, ginv, hist0, *arrivals, nodes_row, gcap, line_row, rate_row, state, setpoint, pvolt)


def bus_kernel(impedance, current, out):
    members, areas = current.shape[:2]
    z = jnp.concatenate([impedance[i] for i in range(areas)], axis=1)
    parts = []
    for i in range(areas):
        real = jnp.concatenate([current[r, i, 0] for r in range(members)], axis=0)
        imag = jnp.concatenate([current[r, i, 1] for r in range(members)], axis=0)
        parts.append(jnp.concatenate([real, imag], axis=1))
        parts.append(jnp.concatenate([-imag, real], axis=1))
    w = jnp.concatenate(parts, axis=0)
    z_high, z_low = split(z)
    w_high, w_low = split(w)
    out[...] = dot(z_high, w_high) + dot(z_low, w_high) + dot(z_high, w_low)


def bus_product(impedance, current):
    vmem = pl.BlockSpec(memory_space=pltpu.VMEM)
    return pl.pallas_call(
        bus_kernel,
        out_shape=jax.ShapeDtypeStruct((impedance.shape[1], 256), F32),
        in_specs=[vmem] * 2,
        out_specs=vmem,
        compiler_params=pltpu.CompilerParams(vmem_limit_bytes=32 << 20),
        name="bus_product",
    )(impedance, current)


def port_kernel(local, volts, out, rows, sem):
    count = out.shape[0]
    most = volts.shape[0]

    def fetch(k):
        b = jnp.clip(local[k], 0, most - 1)
        start = pl.multiple_of((b // 8) * 8, 8)
        return pltpu.make_async_copy(volts.at[pl.ds(start, 8)], rows.at[k], sem.at[k])

    for k in range(count):
        fetch(k).start()
    for k in range(count):
        fetch(k).wait()
        b = local[k]
        here = jnp.logical_and(b >= 0, b < most)
        inside = jnp.bitwise_and(jnp.clip(b, 0, most - 1), 7)
        value = rows[k, pl.ds(inside, 1), :]
        out[pl.ds(k, 1), :] = jnp.where(here, value, 0.0)


def port_rows(local, volts):
    count = local.shape[0]
    width = volts.shape[1]
    return pl.pallas_call(
        port_kernel,
        out_shape=jax.ShapeDtypeStruct((count, width), F32),
        in_specs=[pl.BlockSpec(memory_space=pltpu.SMEM), pl.BlockSpec(memory_space=pl.ANY)],
        out_specs=pl.BlockSpec(memory_space=pltpu.VMEM),
        scratch_shapes=[pltpu.VMEM((count, 8, width), F32), pltpu.SemaphoreType.DMA((count,))],
        name="port_rows",
    )(local, volts)


def shifted(x, by):
    size = lax.axis_size(ALL)
    return lax.ppermute(x, ALL, [(i, (i + by) % size) for i in range(size)])


def copy_for_each(x, axis):
    size = lax.axis_size(axis)
    return lax.all_to_all(jnp.broadcast_to(x[None], (size, *x.shape)), axis, 0, 0, tiled=True)


def per_device(
    conductance_inverse,
    cap_history,
    cap_conductance,
    wave_history,
    line_partner,
    line_node,
    line_delay,
    line_admittance,
    conv_node,
    conv_count,
    conv_state,
    conv_reference,
    conv_rate,
    conv_limit,
    port_node,
    port_admittance,
    port_voltage_prev,
    port_bus,
    transfer_impedance,
):
    areas = lax.axis_size("z")
    bus_rows = transfer_impedance.shape[1]
    with jax.named_scope("wave_exchange"):
        near_up, far_up, near_down, far_down = pack(line_partner[0], wave_history[0])
        arrivals = (
            shifted(near_up, 1),
            shifted(far_up, 2),
            shifted(near_down, -1),
            shifted(far_down, -2),
        )
    with jax.named_scope("impedance_exchange"):
        both = jnp.concatenate([transfer_impedance[0], transfer_impedance[1]], axis=1)
        both = both.reshape(areas, bus_rows // areas, both.shape[1])
        impedance = lax.all_to_all(both, "z", 0, 0, tiled=True)
    with jax.named_scope("tables"):
        spare = jnp.full((128 - PROBES,), -1, jnp.int32)
        nodes = jnp.concatenate([line_node[0], conv_node[0], port_node[0], spare])
        rest = jnp.zeros((256 - AT_COUNT - 1,), jnp.int32)
        table = jnp.concatenate([nodes, line_delay[0], line_partner[0], conv_count, rest])
        gap = jnp.ones((128 - PROBES,), F32)
        line_row = jnp.concatenate([line_admittance[0], conv_limit[0], port_admittance[0], gap])
        rate_row = jnp.concatenate(
            [jnp.zeros((LINES,), F32), conv_rate[0], jnp.zeros((128 - LINES - CONV,), F32)]
        )
        theta = np.arange(1, STEPS + 1, dtype=np.float32) * np.float32(2.0 * math.pi / STEPS)
        angle = jnp.asarray(np.stack([np.cos(theta), np.sin(theta)]).astype(np.float32))
    outward, hist_end, conv_out, current = window(
        table,
        nodes[None],
        angle,
        conductance_inverse[0],
        cap_history[0],
        arrivals,
        cap_conductance,
        line_row[None],
        rate_row[None],
        conv_state[0],
        conv_reference[0],
        port_voltage_prev[:, 0],
    )
    with jax.named_scope("currents"):
        flat = copy_for_each(copy_for_each(current, "z"), ROW)
        flat = flat.reshape(lax.axis_size(ROW), areas, *current.shape)
    with jax.named_scope("bus_voltage"):
        partial = bus_product(impedance, flat)
        size = lax.axis_size("x")
        pieces = partial.reshape(size, -1, partial.shape[1])
        own = jnp.sum(lax.all_to_all(pieces, "x", 0, 0, tiled=True), axis=0)
        volts = copy_for_each(own, "x")
        volts = lax.all_gather(volts.reshape(-1, volts.shape[-1]), "z", tiled=True)
        cases = volts.shape[1] // 2
        bus_voltage = jnp.stack([volts[:, :cases], volts[:, cases:]])
    with jax.named_scope("port_voltage"):
        local = port_bus.reshape(-1) - lax.axis_index(ROW) * bus_rows
        picked = port_rows(local, volts)
        members = port_bus.shape[0]
        picked = picked.reshape(members, PORTS, 2 * cases)
        mine = jnp.sum(lax.all_to_all(picked, ROW, 0, 0, tiled=True), axis=0)
        port_voltage = jnp.stack([mine[:, :cases], mine[:, cases:]])[:, None]
    return (outward[None], hist_end[None], conv_out[None], bus_voltage, port_voltage)


def solution(mesh):
    devices = mesh.devices.reshape(8, 4, 4, 2)
    torus = Mesh(devices, ALL)
    return jax.shard_map(
        per_device,
        mesh=torus,
        in_specs=(
            P(ALL, None, None),
            P(ALL, None, None),
            P(ALL, None),
            P(ALL, None, None, None),
            P(ALL, None),
            P(ALL, None),
            P(ALL, None),
            P(ALL, None),
            P(ALL, None),
            P(ALL),
            P(ALL, None, None, None),
            P(ALL, None, None, None),
            P(ALL, None),
            P(ALL, None),
            P(ALL, None),
            P(ALL, None),
            P(None, ALL, None, None),
            P(AREA, None),
            P(None, ROW, AREA),
        ),
        out_specs=(
            P(ALL, None, None, None),
            P(ALL, None, None),
            P(ALL, None, None, None),
            P(None, ROW, None),
            P(None, ALL, None, None),
        ),
        check_vma=False,
    )
```

time: 462 us -> 219 us (0.47)
  matrix products: 171 us -> 0 us
  waiting for transfers between devices: 118 us -> 45.6 us
  blocking collectives: 24 us -> 79.3 us
  Pallas kernels: 0 us -> 42 us
  other arithmetic: 46 us -> 5.57 us
  local copies, waits for them, and re-layouts: 46.3 us -> 11.4 us
  loops' own time: 29.9 us -> 0 us
  starting transfers between devices: 9.23 us -> 18.2 us
    dot_general x66 -> x0, matrix products: 171 us -> none  [the longest x20 134 us: advance(): volt = jnp.dot(ginv, right, precision=HIGHEST)]
    reduce_scatter x2 -> x0, waiting for transfers between devices: 70.4 us -> none  [own_block(): parts = lax.psum_scatter(parts, axes[k], scatter_dimension=0, tiled=True)]
    all_to_all x0 -> x2, blocking collectives: none -> 52.4 us  [the longest x1 36.8 us: per_device(): impedance = lax.all_to_all(both, 'z', 0, 0, tiled=True)]
    pallas_call x0 -> x4, Pallas kernels: none -> 42 us  [the longest x1 33.9 us: window(): pl.pallas_call(window_kernel, out_shape=(jax.ShapeDtypeStruct((STEPS, LIN...]
    dynamic_slice x40 -> x0, local copies, waits for them, and re-layouts: 30 us -> none  [window(): carry, outward = lax.scan(advance, carry, (incoming, angles))]
    another operation x1 -> x0, loops' own time: 29.9 us -> none  [window(): carry, outward = lax.scan(advance, carry, (incoming, angles))]
    all_to_all x1 -> x2, blocking collectives: 10.1 us -> 26.9 us  [copy_for_each(): lax.all_to_all(jnp.broadcast_to(x[None], (size, *x.shape)), axis, 0, 0, t...]
    all_gather x1 -> x0, blocking collectives: 13.9 us -> none  [stacked_from(): parts = lax.all_gather(parts, axes[k])]
  transfers between devices with their start and end apart: 8 -> 7, of which waited for: 4 -> 3; matrix products, arithmetic and copies ran while one was open for 4% -> 4% of each run, Pallas kernels for 0% -> 0%
where the time goes in v1:
time: 219 us; the launch traced here: 217 us
  blocking collectives  79.3 us (36%)
  waiting for transfers between devices  45.6 us (21%)
  Pallas kernels  42 us (19%)
  starting transfers between devices  18.2 us (8%)
  between operations  14.9 us (7%)
  local copies, waits for them, and re-layouts  11.4 us (5%)
  other arithmetic  5.57 us (3%)
    all_to_all x1, blocking collectives, per_device(): impedance = lax.all_to_all(both, 'z', 0, 0, tiled=True)  36.8 us
    all_gather x1, waiting for transfers between devices, per_device(): volts = lax.all_gather(volts.reshape(-1, volts.shape[-1]), 'z', tiled=True)  35.2 us
    pallas_call x1, Pallas kernels, window(): pl.pallas_call(window_kernel, out_shape=(jax.ShapeDtypeStruct((STEPS, LIN...  33.9 us
    all_to_all x2, blocking collectives, copy_for_each(): lax.all_to_all(jnp.broadcast_to(x[None], (size, *x.shape)), axis, 0, 0, t...  26.9 us
    all_to_all x1, blocking collectives, per_device(): own = jnp.sum(lax.all_to_all(pieces, 'x', 0, 0, tiled=True), axis=0)  15.6 us
    ppermute x4, starting transfers between devices, shifted(): return lax.ppermute(x, ALL, [(i, (i + by) % size) for i in range(size)])  7.99 us
    unnamed x20, local copies, waits for them, and re-layouts  6.98 us
    all_to_all x1, waiting for transfers between devices, copy_for_each(): lax.all_to_all(jnp.broadcast_to(x[None], (size, *x.shape)), axis, 0, 0, t...  6.6 us
  transfers between devices with their start and end apart: 7, of which 3 were waited for; matrix products, arithmetic and copies ran while one was open for 4% of the time, Pallas kernels for 0%

profile of v1, /device:TPU:2, one launch (start us, length us, event | category | flops | bytes accessed | tf_op | source)
XLA Modules:
  0.0 216.9 jit_solution(10959611733301053264)
XLA Ops:
  7.2 2.7 %pack_waves.1 = (f32[12,40,128]{2,1,0:T(8,128)}, f32[4,40,128]{2,1,0:T(8,128)}, f32[12,40,128]{2,1,0:T(8,128)}, f32[4,40,128]{2,1,0:T(8,128)}) custom-call(s32[32]{0:T(128)} %bitcast.56, f32[40,32,128]{2,1,0:T(8,128)} %bitcast.48), custom_call_target="tpu_custom_call" | custom-call | tf_op jit(solution)/shard_map/wave_exchange/pack_waves/pallas_call | solution.py:70
  9.8 3.9 %collective-permute-start.2 = (f32[12,40,128]{2,1,0:T(8,128)}, f32[12,40,128]{2,1,0:T(8,128)S(1)}, u32[]{:S(2)}, u32[]{:S(2)}) collective-permute-start(f32[12,40,128]{2,1,0:T(8,128)} %get-tuple-element.15), channel_id=1, source_target_pairs={{0,255},{1,0},{2,1},{3,2},{4,3},{5,4},{6,5},{7,6},{8,7},{9,8},{10,... | collective-permute-start | bytes 737288 | tf_op jit(solution)/shard_map/wave_exchange/ppermute | solution.py:333
  13.7 4.1 %collective-permute-start.3 = (f32[4,40,128]{2,1,0:T(8,128)}, f32[4,40,128]{2,1,0:T(8,128)S(1)}, u32[]{:S(2)}, u32[]{:S(2)}) collective-permute-start(f32[4,40,128]{2,1,0:T(8,128)} %get-tuple-element.16), channel_id=1, source_target_pairs={{0,254},{1,255},{2,0},{3,1},{4,2},{5,3},{6,4},{7,5},{8,6},{9,7},{1... | collective-permute-start | bytes 245768 | tf_op jit(solution)/shard_map/wave_exchange/ppermute | solution.py:333
  18.5 0.8 concatenate.21.table
  19.3 0.8 maximum_bitcast_fusion.1
  20.1 0.8 add_bitcast_fusion.nodes_row
  20.9 2.2 %copy-done = f32[1,1024,1024]{2,1,0:T(8,128)S(1)} copy-done((f32[1,1024,1024]{2,1,0:T(8,128)S(1)}, f32[1,1024,1024]{2,1,0:T(8,128)}, u32[]{:S(2)}) %copy-start) | copy-done | bytes 4194328
  23.1 1.0 copy-done.1
  24.1 0.8 copy-done.2
  24.9 0.8 copy-done.3
  25.8 0.7 copy-done.4
  26.5 0.7 copy-done.5
  27.2 0.7 copy-done.6
  27.8 33.9 %window.1 = (f32[20,32,128]{2,1,0:T(8,128)}, f32[1024,128]{1,0:T(8,128)}, f32[2,64,128]{2,1,0:T(8,128)}, f32[2,8,128]{2,1,0:T(8,128)S(1)}) custom-call(s32[256]{0:T(256)S(1)} %concatenate.21.table, f32[2,20]{1,0:T(2,128)S(1)} %copy-done.6, f32[1024,1024]{1,0:T(8,128)S(1)} %bitcast.40, f32[1024,128]{1,0:T(8,128)S(1)} %bitcast.41, ...), custom_call_target="tpu_custom_call" | custom-call | flops 16106127360 | bytes 67108864 | tf_op jit(solution)/shard_map/window/pallas_call | solution.py:235
  61.8 16.8 %all_to_all.30 = f32[8,2,8,128]{3,2,1,0:T(8,128)S(1)} all-to-all(f32[8,2,8,128]{3,2,1,0:T(8,128)S(1)} %broadcast_in_dim.49), channel_id=1, replica_groups=mesh['z'=8,'x'=4,'y'=4,'core'=2] {'z'}, dimensions={0} | all-to-all | bytes 131072 | tf_op jit(solution)/shard_map/currents/all_to_all | solution.py:338
  78.6 0.8 broadcast_in_dim.50
  79.5 5.0 %all-to-all-start.2 = ((f32[8,8,2,8,128]{4,3,2,1,0:T(8,128)}), f32[8,8,2,8,128]{4,3,2,1,0:T(8,128)S(1)}, u32[]{:S(2)}, u32[]{:S(2)}) async-start(f32[8,8,2,8,128]{4,3,2,1,0:T(8,128)} %broadcast_in_dim.50), calls=%async_computation.2 | async-start | bytes 1048576 | tf_op jit(solution)/shard_map/currents/all_to_all | solution.py:338
  84.7 0.4 copy.25
  85.1 1.5 copy.26
  86.5 1.7 pad_maximum_fusion.1
  88.3 6.6 %all-to-all-done.2.current = f32[8,8,2,8,128]{4,3,2,1,0:T(8,128)S(1)} async-done(((f32[8,8,2,8,128]{4,3,2,1,0:T(8,128)}), f32[8,8,2,8,128]{4,3,2,1,0:T(8,128)S(1)}, u32[]{:S(2)}, u32[]{:S(2)}) %all-to-all-start.2) | async-done | bytes 524320 | tf_op jit(solution)/shard_map/currents/all_to_all | solution.py:338
  94.9 36.8 %all_to_all.31.impedance = f32[8,320,128]{2,1,0:T(8,128)S(1)} all-to-all(f32[8,320,128]{2,1,0:T(8,128)S(1)} %pad_maximum_fusion.1), channel_id=1, replica_groups=mesh['z'=8,'x'=4,'y'=4,'core'=2] {'z'}, dimensions={0} | all-to-all | bytes 2621440 | tf_op jit(solution)/shard_map/impedance_exchange/all_to_all | solution.py:375
  131.7 0.7 bus_product.1
  132.4 15.6 %all_to_all.32 = f32[4,80,256]{2,1,0:T(8,128)S(1)} all-to-all(f32[4,80,256]{2,1,0:T(8,128)S(1)} %bitcast.39), channel_id=1, replica_groups=mesh['z'=8,'x'=4,'y'=4,'core'=2] {'x'}, dimensions={0} | all-to-all | bytes 655360 | tf_op jit(solution)/shard_map/bus_voltage/all_to_all | solution.py:409
  148.0 10.1 %all_to_all.33 = f32[4,80,256]{2,1,0:T(8,128)} all-to-all(f32[4,80,256]{2,1,0:T(8,128)S(1)} %broadcast_in_dim.51), channel_id=1, replica_groups=mesh['z'=8,'x'=4,'y'=4,'core'=2] {'x'}, dimensions={0} | all-to-all | bytes 655360 | tf_op jit(solution)/shard_map/bus_voltage/all_to_all | solution.py:338
  158.2 0.6 sub.10.local
  158.8 35.2 %all-gather.2.cloned.1.call-done.volts = f32[2560,256]{1,0:T(8,128)} async-done(((f32[320,256]{1,0:T(8,128)}), f32[2560,256]{1,0:T(8,128)}) %all-gather.2.cloned.1.call-update) | async-done | bytes 2621456 | tf_op jit(solution)/shard_map/bus_voltage/all_gather | solution.py:411
  194.0 4.7 %port_rows.1 = f32[64,256]{1,0:T(8,128)} custom-call(s32[64]{0:T(128)} %sub.10.local, f32[2560,256]{1,0:T(8,128)} %all-gather.2.cloned.1.call-done.volts), custom_call_target="tpu_custom_call" | custom-call | tf_op jit(solution)/shard_map/port_voltage/port_rows/pallas_call | solution.py:321
  198.7 5.2 %all-to-all-start.5 = ((f32[8,8,256]{2,1,0:T(8,128)}), f32[8,8,256]{2,1,0:T(8,128)S(1)}, u32[]{:S(2)}, u32[]{:S(2)}) async-start(f32[8,8,256]{2,1,0:T(8,128)} %bitcast.49), calls=%async_computation.5 | async-start | bytes 131072 | tf_op jit(solution)/shard_map/port_voltage/all_to_all | solution.py:419
  204.0 1.7 pad_maximum_fusion
  205.7 3.8 %all-to-all-done.5 = f32[8,8,256]{2,1,0:T(8,128)S(1)} async-done(((f32[8,8,256]{2,1,0:T(8,128)}), f32[8,8,256]{2,1,0:T(8,128)S(1)}, u32[]{:S(2)}, u32[]{:S(2)}) %all-to-all-start.5) | async-done | bytes 65568 | tf_op jit(solution)/shard_map/port_voltage/all_to_all | solution.py:419
  209.5 0.6 maximum_bitcast_fusion
  (33 shorter events, 0.4 us)
Async XLA Ops:
  9.8 11.0 %collective-permute-start = (f32[12,40,128]{2,1,0:T(8,128)}, f32[12,40,128]{2,1,0:T(8,128)S(1)}, u32[]{:S(2)}, u32[]{:S(2)}) collective-permute-start(f32[12,40,128]{2,1,0:T(8,128)} %get-tuple-element.13), channel_id=1, source_target_pairs={{0,1},{1,2},{2,3},{3,4},{4,5},{5,6},{6,7},{7,8},{8,9},{9,10},{10,1... | collective-permute-start | bytes 737288 | tf_op jit(solution)/shard_map/wave_exchange/ppermute | solution.py:333
  9.8 11.0 %collective-permute-start.2 = (f32[12,40,128]{2,1,0:T(8,128)}, f32[12,40,128]{2,1,0:T(8,128)S(1)}, u32[]{:S(2)}, u32[]{:S(2)}) collective-permute-start(f32[12,40,128]{2,1,0:T(8,128)} %get-tuple-element.15), channel_id=1, source_target_pairs={{0,255},{1,0},{2,1},{3,2},{4,3},{5,4},{6,5},{7,6},{8,7},{9,8},{10,... | collective-permute-start | bytes 737288 | tf_op jit(solution)/shard_map/wave_exchange/ppermute | solution.py:333
  13.7 7.2 %collective-permute-start.1 = (f32[4,40,128]{2,1,0:T(8,128)}, f32[4,40,128]{2,1,0:T(8,128)S(1)}, u32[]{:S(2)}, u32[]{:S(2)}) collective-permute-start(f32[4,40,128]{2,1,0:T(8,128)} %get-tuple-element.14), channel_id=1, source_target_pairs={{0,2},{1,3},{2,4},{3,5},{4,6},{5,7},{6,8},{7,9},{8,10},{9,11},{10,... | collective-permute-start | bytes 245768 | tf_op jit(solution)/shard_map/wave_exchange/ppermute | solution.py:333
  13.7 7.2 %collective-permute-start.3 = (f32[4,40,128]{2,1,0:T(8,128)}, f32[4,40,128]{2,1,0:T(8,128)S(1)}, u32[]{:S(2)}, u32[]{:S(2)}) collective-permute-start(f32[4,40,128]{2,1,0:T(8,128)} %get-tuple-element.16), channel_id=1, source_target_pairs={{0,254},{1,255},{2,0},{3,1},{4,2},{5,3},{6,4},{7,5},{8,6},{9,7},{1... | collective-permute-start | bytes 245768 | tf_op jit(solution)/shard_map/wave_exchange/ppermute | solution.py:333
  20.9 2.2 %copy-start = (f32[1,1024,1024]{2,1,0:T(8,128)S(1)}, f32[1,1024,1024]{2,1,0:T(8,128)}, u32[]{:S(2)}) copy-start(f32[1,1024,1024]{2,1,0:T(8,128)} %param.20) | copy-start | bytes 12582916
  23.1 1.0 copy-start.1
  24.1 0.8 copy-start.2
  24.9 0.8 copy-start.3
  25.8 0.7 copy-start.4
  26.5 0.7 copy-start.5
  27.2 0.7 copy-start.6
  61.8 22.8 %copy-start.8 = (f32[2,2560,64]{1,2,0:T(8,128)S(1)}, f32[2,2560,64]{1,2,0:T(8,128)}, u32[]{:S(2)}) copy-start(f32[2,2560,64]{1,2,0:T(8,128)} %param.38) | copy-start | bytes 3932164
  79.5 15.4 %all-to-all-start.2 = ((f32[8,8,2,8,128]{4,3,2,1,0:T(8,128)}), f32[8,8,2,8,128]{4,3,2,1,0:T(8,128)S(1)}, u32[]{:S(2)}, u32[]{:S(2)}) async-start(f32[8,8,2,8,128]{4,3,2,1,0:T(8,128)} %broadcast_in_dim.50), calls=%async_computation.2 | async-start | bytes 1048576 | tf_op jit(solution)/shard_map/currents/all_to_all | solution.py:338
  84.5 109.5 %all-gather.2.cloned.1.call-start = ((), (), s32[]{:S(2)}) async-start(), calls=%async_computation.6 | async-start | bytes 2949120 | tf_op jit(solution)/shard_map/bus_voltage/all_gather | solution.py:411
  132.4 25.8 %copy-start.9 = (s32[8,8]{1,0:T(8,128)S(1)}, s32[8,8]{1,0:T(8,128)}, u32[]{:S(2)}) copy-start(s32[8,8]{1,0:T(8,128)} %param.37) | copy-start | bytes 772
  194.0 9.9 %copy-start.7 = (f32[2560,256]{1,0:T(8,128)S(1)}, f32[2560,256]{1,0:T(8,128)}, u32[]{:S(2)}) copy-start(f32[2560,256]{1,0:T(8,128)} %all-gather.2.cloned.1.call-done.volts) | copy-start | bytes 7864324
  198.7 10.8 %all-to-all-start.5 = ((f32[8,8,256]{2,1,0:T(8,128)}), f32[8,8,256]{2,1,0:T(8,128)S(1)}, u32[]{:S(2)}, u32[]{:S(2)}) async-start(f32[8,8,256]{2,1,0:T(8,128)} %bitcast.49), calls=%async_computation.5 | async-start | bytes 131072 | tf_op jit(solution)/shard_map/port_voltage/all_to_all | solution.py:419
Sparse Core Ops, SparseCore 0:
  158.3 35.6 all-gather.1

commit v2 on v1

v2 whole, which is shorter than its diff:
```python
import math

import jax
import jax.numpy as jnp
import numpy as np
from jax import lax
from jax.experimental import pallas as pl
from jax.experimental.pallas import tpu as pltpu
from jax.sharding import Mesh
from jax.sharding import PartitionSpec as P

STEPS = 20
HIST = 40
NEAR = 12
LINES = 32
CONV = 64
PORTS = 8
HALF = LINES // 2
PROBES = LINES + CONV + PORTS
SAG_FACTOR = 0.3
ALL = ("z", "x", "y", "core")
AREA = ("z", "x")
ROW = ("y", "core")
F32 = jnp.float32
BF16 = jnp.bfloat16


def dot(a, b):
    return jnp.dot(a, b, preferred_element_type=F32)


def split(x):
    high = x.astype(BF16)
    return high, (x - high.astype(F32)).astype(BF16)


def reach_of(partner, line):
    return jnp.bitwise_and(partner[0, line] - partner[0, HALF + line], 255) // 2


def pack_kernel(partner, waves, impedance, ports, near_up, far_up, near_down, far_down, blocks):
    near = jnp.int32(0)
    for line in range(HALF):
        is_near = reach_of(partner, line) == 1
        up = waves[:, line, :]
        down = waves[:, line + HALF, :]

        @pl.when(is_near)
        def _(near=near, up=up, down=down):
            near_up[near] = up
            near_down[near] = down

        @pl.when(jnp.logical_not(is_near))
        def _(far=line - near, up=up, down=down):
            far_up[far] = up
            far_down[far] = down

        near = near + is_near.astype(jnp.int32)
    areas, rows, _ = blocks.shape
    rows = rows - 8
    for first in range(0, areas * rows, 128):
        part = impedance[:, :, pl.ds(first, 128)]
        turned = jnp.concatenate([part[0], part[1]], axis=0).T
        done = 0
        while done < 128:
            area, at = divmod(first + done, rows)
            size = min(128 - done, rows - at)
            blocks[area, pl.ds(at, size), :] = turned[done : done + size]
            done += size
    for area in range(areas):
        blocks[area, pl.ds(rows, 8), :] = jnp.broadcast_to(ports[...], (8, 128))


def pack(partner, waves, impedance, ports, areas):
    hist, _, cases = waves.shape
    near = jax.ShapeDtypeStruct((NEAR, hist, cases), F32)
    far = jax.ShapeDtypeStruct((HALF - NEAR, hist, cases), F32)
    blocks = jax.ShapeDtypeStruct((areas, impedance.shape[2] // areas + 8, 128), F32)
    vmem = pl.BlockSpec(memory_space=pltpu.VMEM)
    return pl.pallas_call(
        pack_kernel,
        out_shape=(near, far, near, far, blocks),
        in_specs=[pl.BlockSpec(memory_space=pltpu.SMEM), vmem, vmem, vmem],
        out_specs=(vmem,) * 5,
        compiler_params=pltpu.CompilerParams(vmem_limit_bytes=32 << 20),
        name="pack_waves",
    )(partner, waves, impedance, ports)


def column(row):
    return jnp.broadcast_to(row, (128, 128)).T


def window_kernel(
    angle,
    partner,
    delay,
    count,
    line_node,
    conv_node,
    port_node,
    g_hbm,
    hist0_hbm,
    gcap_hbm,
    state0_hbm,
    setpoint_hbm,
    pvolt_hbm,
    near_up,
    far_up,
    near_down,
    far_down,
    line_nodes,
    conv_nodes,
    port_nodes,
    line_adms,
    limits,
    rates,
    port_adms,
    waves,
    hist_out,
    state_out,
    current,
    g_in,
    g_high,
    g_low,
    arrived,
    incoming,
    w_even,
    w_odd,
    volt,
    probe,
    stack,
    cap2,
    coef,
    setpoint,
    pvolt,
    gcap,
    nodes_row,
    coef_row,
    g_sem,
    a_sem,
    s_sem,
):
    nodes = g_high.shape[0]
    chunks = g_in.shape[0]
    rows = nodes // chunks
    small = []

    def bring(source, target):
        small.append(pltpu.make_async_copy(source, target, s_sem.at[len(small)]))
        small[-1].start()

    bring(gcap_hbm, gcap)
    bring(hist0_hbm, hist_out)
    bring(state0_hbm, state_out)
    bring(setpoint_hbm, setpoint)
    bring(pvolt_hbm, pvolt)
    copies = [
        pltpu.make_async_copy(g_hbm.at[pl.ds(i * rows, rows)], g_in.at[i], g_sem.at[i])
        for i in range(chunks)
    ]
    for copy in copies:
        copy.start()
    first = 0
    moves = []
    for i, part in enumerate((near_up, far_up, near_down, far_down)):
        size = part.shape[0]
        moves.append(
            pltpu.make_async_copy(part, arrived.at[pl.ds(first, size)], a_sem.at[i])
        )
        first += size
    for move in moves:
        move.start()

    zeros = jnp.zeros((256, 128), BF16)
    for w in (w_even, w_odd):
        w[pl.ds(nodes, 256), pl.ds(0, 128)] = zeros
        w[pl.ds(nodes, 256), pl.ds(128, 128)] = zeros
    current[...] = jnp.zeros_like(current)
    stack[...] = jnp.zeros_like(stack)
    nodes_row[...] = jnp.full(nodes_row.shape, -1, jnp.int32)
    coef_row[...] = jnp.ones(coef_row.shape, F32)
    for copy in small:
        copy.wait()

    at_conv, at_port = pl.ds(LINES, CONV), pl.ds(LINES + CONV, PORTS)
    first_row = pl.ds(0, 1)
    nodes_row[first_row, pl.ds(0, LINES)] = line_nodes[...]
    nodes_row[first_row, at_conv] = conv_nodes[...]
    nodes_row[first_row, at_port] = port_nodes[...]
    coef_row[first_row, pl.ds(0, LINES)] = line_adms[...]
    coef_row[first_row, at_conv] = limits[...]
    coef_row[first_row, at_port] = port_adms[...]
    coef_row[pl.ds(1, 1), at_conv] = rates[...]
    coef[0] = column(coef_row[pl.ds(0, 1), :])
    coef[1] = column(coef_row[pl.ds(1, 1), :])
    for i in range(nodes // 128):
        cap2[pl.ds(i * 128, 128)] = 2.0 * column(gcap[:, pl.ds(i * 128, 128)])
    high, low = split(hist_out[...])
    w_even[pl.ds(0, nodes), pl.ds(0, 128)] = high
    w_even[pl.ds(0, nodes), pl.ds(128, 128)] = low

    picks = (
        lax.broadcasted_iota(jnp.int32, (nodes, 128), 0) == nodes_row[pl.ds(0, 1), :]
    ).astype(BF16)
    for i, copy in enumerate(copies):
        copy.wait()
        high, low = split(g_in[i])
        at = pl.ds(i * rows, rows)
        g_high[at, pl.ds(0, nodes)] = high
        g_low[at, :] = low
        g_high[at, pl.ds(nodes, 128)] = dot(high, picks).astype(BF16)
        g_high[at, pl.ds(nodes + 128, 128)] = dot(low, picks).astype(BF16)

    for move in moves:
        move.wait()
    near = jnp.int32(0)
    for line in range(HALF):
        is_near = reach_of(partner, line) == 1
        place = jnp.where(is_near, near, NEAR + line - near)
        near = near + is_near.astype(jnp.int32)
        for slot, at in ((line + HALF, place), (line, place + HALF)):
            start = HIST - delay[0, slot]
            incoming[:, slot, :] = arrived[at, pl.ds(start, STEPS), :]

    line_adm = 2.0 * coef[0, :LINES]
    limit = coef[0, LINES : LINES + CONV]
    padm = coef[0, LINES + CONV : PROBES]
    rate = coef[1, LINES : LINES + CONV]
    inverse = 1.0 / limit
    live = lax.broadcasted_iota(jnp.int32, (CONV, 128), 0) < count[0]

    def step(t, w, w_next):
        cos, sin = angle[0, t], angle[1, t]
        axial, normal = state_out[0], state_out[1]
        inward = incoming[t]
        source = padm * (pvolt[0] * cos - pvolt[1] * sin)
        stack[pl.ds(0, LINES)] = inward
        stack[pl.ds(LINES, CONV)] = jnp.where(live, axial * cos - normal * sin, 0.0)
        stack[pl.ds(LINES + CONV, PORTS)] = source
        high, low = split(stack[...])
        w[pl.ds(nodes, 128), pl.ds(0, 128)] = high
        w[pl.ds(nodes, 128), pl.ds(128, 128)] = low
        w[pl.ds(nodes + 128, 128), pl.ds(0, 128)] = high
        block = 256
        for i in range(0, nodes, block):
            at = pl.ds(i, block)
            y = dot(g_high[at, :], w[...])
            z = dot(g_low[at, :], w[pl.ds(0, nodes), pl.ds(0, 128)])
            v = y[:, :128] + y[:, 128:] + z
            volt[at, :] = v
            h = cap2[at, :] * v - hist_out[at, :]
            hist_out[at, :] = h
            high, low = split(h)
            w_next[at, pl.ds(0, 128)] = high
            w_next[at, pl.ds(128, 128)] = low
        for base, where in ((0, line_node), (LINES, conv_node), (LINES + CONV, port_node)):
            for k in range(where.shape[1]):
                probe[pl.ds(base + k, 1), :] = volt[pl.ds(where[0, k], 1), :]
        emf = probe[pl.ds(LINES, CONV), :]
        new_axial = axial + rate * (setpoint[0] - axial) - (SAG_FACTOR * cos) * emf
        new_normal = normal + rate * (setpoint[1] - normal) + (SAG_FACTOR * sin) * emf
        state_out[0] = jnp.where(live, limit * jnp.tanh(new_axial * inverse), axial)
        state_out[1] = jnp.where(live, limit * jnp.tanh(new_normal * inverse), normal)
        waves[t] = line_adm * probe[pl.ds(0, LINES), :] - inward
        flow = source - padm * probe[pl.ds(LINES + CONV, PORTS), :]
        current[0] = current[0] + flow * cos
        current[1] = current[1] - flow * sin

    def pair(i, _):
        step(2 * i, w_even, w_odd)
        step(2 * i + 1, w_odd, w_even)
        return 0

    lax.fori_loop(0, STEPS // 2, pair, 0)
    current[...] = current[...] * (2.0 / STEPS)


def window(angle, whole_numbers, ginv, hist0, arrivals, gcap, state, setpoint, pvolt, nodes_of, coefficients):
    nodes, cases = hist0.shape
    smem = pl.BlockSpec(memory_space=pltpu.SMEM)
    vmem = pl.BlockSpec(memory_space=pltpu.VMEM)
    chunks = 8
    scalars = (angle, *whole_numbers, *nodes_of)
    far = (ginv, hist0, gcap, state, setpoint, pvolt)
    rows = (*arrivals, *nodes_of, *coefficients)
    return pl.pallas_call(
        window_kernel,
        out_shape=(
            jax.ShapeDtypeStruct((STEPS, LINES, cases), F32),
            jax.ShapeDtypeStruct((nodes, cases), F32),
            jax.ShapeDtypeStruct(state.shape, F32),
            jax.ShapeDtypeStruct((2, PORTS, cases), F32),
        ),
        in_specs=[smem] * len(scalars)
        + [pl.BlockSpec(memory_space=pl.ANY)] * len(far)
        + [vmem] * len(rows),
        out_specs=(vmem,) * 4,
        scratch_shapes=[
            pltpu.VMEM((chunks, nodes // chunks, nodes), F32),
            pltpu.VMEM((nodes, nodes + 256), BF16),
            pltpu.VMEM((nodes, nodes), BF16),
            pltpu.VMEM((LINES, HIST, cases), F32),
            pltpu.VMEM((STEPS, LINES, cases), F32),
            pltpu.VMEM((nodes + 256, 256), BF16),
            pltpu.VMEM((nodes + 256, 256), BF16),
            pltpu.VMEM((nodes, cases), F32),
            pltpu.VMEM((PROBES, cases), F32),
            pltpu.VMEM((128, cases), F32),
            pltpu.VMEM((nodes, cases), F32),
            pltpu.VMEM((2, 128, cases), F32),
            pltpu.VMEM(setpoint.shape, F32),
            pltpu.VMEM(pvolt.shape, F32),
            pltpu.VMEM(gcap.shape, F32),
            pltpu.VMEM((8, 128), jnp.int32),
            pltpu.VMEM((8, 128), F32),
            pltpu.SemaphoreType.DMA((chunks,)),
            pltpu.SemaphoreType.DMA((4,)),
            pltpu.SemaphoreType.DMA((5,)),
        ],
        compiler_params=pltpu.CompilerParams(vmem_limit_bytes=44 << 20),
        cost_estimate=pl.CostEstimate(
            flops=6 * STEPS * nodes * nodes * cases,
            bytes_accessed=64 << 20,
            transcendentals=0,
        ),
        name="window",
    )(*scalars, *far, *rows)


def spread_kernel(current, impedance, out):
    for i in range(out.shape[0]):
        out[i] = current[...]


def spread(current, impedance, size):
    vmem = pl.BlockSpec(memory_space=pltpu.VMEM)
    return pl.pallas_call(
        spread_kernel,
        out_shape=jax.ShapeDtypeStruct((size, *current.shape), F32),
        in_specs=[vmem, pl.BlockSpec(memory_space=pl.ANY)],
        out_specs=vmem,
        compiler_params=pltpu.CompilerParams(vmem_limit_bytes=16 << 20),
        name="spread_currents",
    )(current, impedance)


def bus_kernel(impedance, current, out):
    areas, members = current.shape[:2]
    rows = pl.ds(0, out.shape[0])
    z = jnp.concatenate([impedance[i, rows, :] for i in range(areas)], axis=1)
    parts = []
    for i in range(areas):
        real = jnp.concatenate([current[i, r, 0] for r in range(members)], axis=0)
        imag = jnp.concatenate([current[i, r, 1] for r in range(members)], axis=0)
        parts.append(jnp.concatenate([real, imag], axis=1))
        parts.append(jnp.concatenate([-imag, real], axis=1))
    w = jnp.concatenate(parts, axis=0)
    z_high, z_low = split(z)
    w_high, w_low = split(w)
    out[...] = dot(z_high, w_high) + dot(z_low, w_high) + dot(z_high, w_low)


def bus_product(impedance, current):
    vmem = pl.BlockSpec(memory_space=pltpu.VMEM)
    return pl.pallas_call(
        bus_kernel,
        out_shape=jax.ShapeDtypeStruct((impedance.shape[1] - 8, 256), F32),
        in_specs=[vmem] * 2,
        out_specs=vmem,
        compiler_params=pltpu.CompilerParams(vmem_limit_bytes=32 << 20),
        name="bus_product",
    )(impedance, current)


def port_kernel(first, ports, volts, out):
    rows = volts.shape[0]
    high, rest = split(volts[...])
    middle = volts[...] - high.astype(F32)
    low = (middle - rest.astype(F32)).astype(BF16)
    row = lax.broadcasted_iota(jnp.int32, (rows, 128), 0) + first[0]
    for area in range(ports.shape[0]):
        wanted = ports[area, pl.ds(rows, 1), :].astype(jnp.int32)
        picks = jnp.where(row == wanted, 1.0, 0.0).T.astype(BF16)
        found = dot(picks, high) + dot(picks, rest) + dot(picks, low)
        count = out.shape[1] * out.shape[2]
        out[area] = found[:count].reshape(out.shape[1:])


def port_rows(first, ports, volts, members):
    vmem = pl.BlockSpec(memory_space=pltpu.VMEM)
    return pl.pallas_call(
        port_kernel,
        out_shape=jax.ShapeDtypeStruct((ports.shape[0], members, PORTS, volts.shape[1]), F32),
        in_specs=[pl.BlockSpec(memory_space=pltpu.SMEM), vmem, vmem],
        out_specs=vmem,
        compiler_params=pltpu.CompilerParams(vmem_limit_bytes=32 << 20),
        name="port_rows",
    )(first, ports, volts)


def shifted(x, by):
    size = lax.axis_size(ALL)
    return lax.ppermute(x, ALL, [(i, (i + by) % size) for i in range(size)])


def copy_for_each(x, axis):
    size = lax.axis_size(axis)
    return lax.all_to_all(jnp.broadcast_to(x[None], (size, *x.shape)), axis, 0, 0, tiled=True)


def per_device(
    conductance_inverse,
    cap_history,
    cap_conductance,
    wave_history,
    line_partner,
    line_node,
    line_delay,
    line_admittance,
    conv_node,
    conv_count,
    conv_state,
    conv_reference,
    conv_rate,
    conv_limit,
    port_node,
    port_admittance,
    port_voltage_prev,
    port_bus,
    transfer_impedance,
):
    areas = lax.axis_size("z")
    members = lax.axis_size(ROW)
    bus_rows = transfer_impedance.shape[1]
    with jax.named_scope("wave_exchange"):
        ports = port_bus.reshape(1, -1).astype(F32)
        ports = jnp.pad(ports, ((0, 0), (0, 128 - ports.shape[1])), constant_values=-1.0)
        turned = jnp.swapaxes(transfer_impedance, 1, 2)
        near_up, far_up, near_down, far_down, blocks = pack(
            line_partner, wave_history[0], turned, ports, areas
        )
        arrivals = (
            shifted(near_up, 1),
            shifted(far_up, 2),
            shifted(near_down, -1),
            shifted(far_down, -2),
        )
    with jax.named_scope("impedance_exchange"):
        impedance = lax.all_to_all(blocks, "z", 0, 0, tiled=True)
    with jax.named_scope("window"):
        theta = np.arange(1, STEPS + 1, dtype=np.float32) * np.float32(2.0 * math.pi / STEPS)
        angle = jnp.asarray(np.stack([np.cos(theta), np.sin(theta)]).astype(np.float32))
        outward, hist_end, conv_out, current = window(
            angle,
            (line_partner, line_delay, conv_count),
            conductance_inverse[0],
            cap_history[0],
            arrivals,
            cap_conductance,
            conv_state[0],
            conv_reference[0],
            port_voltage_prev[:, 0],
            (line_node, conv_node, port_node),
            (line_admittance, conv_limit, conv_rate, port_admittance),
        )
    with jax.named_scope("currents"):
        flat = spread(current, impedance, areas * members)
        flat = lax.all_to_all(flat, ("z", *ROW), 0, 0, tiled=True)
        flat = flat.reshape(areas, members, *current.shape)
    with jax.named_scope("bus_voltage"):
        partial = bus_product(impedance, flat)
        size = lax.axis_size("x")
        pieces = partial.reshape(size, -1, partial.shape[1])
        own = jnp.sum(lax.all_to_all(pieces, "x", 0, 0, tiled=True), axis=0)
        block = copy_for_each(own, "x").reshape(partial.shape)
        volts = lax.all_gather(block, "z", tiled=True)
        cases = volts.shape[1] // 2
        bus_voltage = jnp.stack([volts[:, :cases], volts[:, cases:]])
    with jax.named_scope("port_voltage"):
        first = lax.axis_index(ROW) * bus_rows + lax.axis_index("z") * partial.shape[0]
        picked = port_rows(first[None].astype(jnp.int32), impedance, block, members)
        picked = picked.reshape(areas * members, PORTS, 2 * cases)
        mine = jnp.sum(lax.all_to_all(picked, ("z", *ROW), 0, 0, tiled=True), axis=0)
        port_voltage = jnp.stack([mine[:, :cases], mine[:, cases:]])[:, None]
    return (outward[None], hist_end[None], conv_out[None], bus_voltage, port_voltage)


def solution(mesh):
    devices = mesh.devices.reshape(8, 4, 4, 2)
    torus = Mesh(devices, ALL)
    return jax.shard_map(
        per_device,
        mesh=torus,
        in_specs=(
            P(ALL, None, None),
            P(ALL, None, None),
            P(ALL, None),
            P(ALL, None, None, None),
            P(ALL, None),
            P(ALL, None),
            P(ALL, None),
            P(ALL, None),
            P(ALL, None),
            P(ALL),
            P(ALL, None, None, None),
            P(ALL, None, None, None),
            P(ALL, None),
            P(ALL, None),
            P(ALL, None),
            P(ALL, None),
            P(None, ALL, None, None),
            P(AREA, None),
            P(None, ROW, AREA),
        ),
        out_specs=(
            P(ALL, None, None, None),
            P(ALL, None, None),
            P(ALL, None, None, None),
            P(None, ROW, None),
            P(None, ALL, None, None),
        ),
        check_vma=False,
    )
```

time: 219 us -> 203 us (0.927)
  waiting for transfers between devices: 45.6 us -> 19.6 us
  blocking collectives: 79.3 us -> 101 us
  Pallas kernels: 42 us -> 38.8 us
  local copies, waits for them, and re-layouts: 11.4 us -> 8.28 us
  other arithmetic: 5.57 us -> 3.04 us
    all_to_all x1 -> x2, blocking collectives: 36.8 us -> 57.5 us  [the longest x1 29.1 us: per_device(): flat = lax.all_to_all(flat, ('z', *ROW), 0, 0, tiled=True)]
    all_to_all x1, blocking collectives: 15.6 us -> 33.6 us  [per_device(): own = jnp.sum(lax.all_to_all(pieces, 'x', 0, 0, tiled=True), axis=0)]
    all_gather x1, waiting for transfers between devices: 35.2 us -> 17.8 us  [per_device(): volts = lax.all_gather(block, 'z', tiled=True)]
    all_to_all x2 -> x1, blocking collectives: 26.9 us -> 10.1 us  [copy_for_each(): lax.all_to_all(jnp.broadcast_to(x[None], (size, *x.shape)), axis, 0, 0, t...]
    all_to_all x2 -> x1, waiting for transfers between devices: 10.4 us -> 0.01 us  [per_device(): impedance = lax.all_to_all(blocks, 'z', 0, 0, tiled=True)]
    pallas_call x2 -> x3, Pallas kernels: 7.37 us -> 3.81 us  [the longest x1 2.73 us: pack(): pl.pallas_call(pack_kernel, out_shape=(near, far, near, far, blocks), in_...]
    all_to_all x2 -> x1, starting transfers between devices: 10.2 us -> 8.61 us  [per_device(): impedance = lax.all_to_all(blocks, 'z', 0, 0, tiled=True)]
    unnamed x20 -> x40, local copies, waits for them, and re-layouts: 6.98 us -> 6.29 us
  transfers between devices with their start and end apart: 7 -> 6, of which waited for: 3 -> 2; matrix products, arithmetic and copies ran while one was open for 4% -> 0% of each run, Pallas kernels for 0% -> 17%
where the time goes in v2:
time: 203 us
  blocking collectives  101 us (50%)
  Pallas kernels  38.8 us (19%)
  waiting for transfers between devices  19.6 us (10%)
  starting transfers between devices  16.7 us (8%)
  between operations  15 us (7%)
  local copies, waits for them, and re-layouts  8.28 us (4%)
  other arithmetic  3.04 us (1%)
    pallas_call x1, Pallas kernels, window(): pl.pallas_call(window_kernel, out_shape=(jax.ShapeDtypeStruct((STEPS, LIN...  34.3 us
    all_to_all x1, blocking collectives, per_device(): own = jnp.sum(lax.all_to_all(pieces, 'x', 0, 0, tiled=True), axis=0)  33.6 us
    all_to_all x1, blocking collectives, per_device(): flat = lax.all_to_all(flat, ('z', *ROW), 0, 0, tiled=True)  29.1 us
    all_to_all x1, blocking collectives, per_device(): lax.all_to_all(picked, ('z', *ROW), 0, 0, tiled=True)  28.4 us
    all_gather x1, waiting for transfers between devices, per_device(): volts = lax.all_gather(block, 'z', tiled=True)  17.8 us
    all_to_all x1, blocking collectives, copy_for_each(): lax.all_to_all(jnp.broadcast_to(x[None], (size, *x.shape)), axis, 0, 0, t...  10.1 us
    all_to_all x1, starting transfers between devices, per_device(): impedance = lax.all_to_all(blocks, 'z', 0, 0, tiled=True)  8.61 us
    ppermute x4, starting transfers between devices, shifted(): return lax.ppermute(x, ALL, [(i, (i + by) % size) for i in range(size)])  8.06 us
  transfers between devices with their start and end apart: 6, of which 2 were waited for; matrix products, arithmetic and copies ran while one was open for 0% of the time, Pallas kernels for 17%

profile of v2, /device:TPU:2, one launch (start us, length us, event | category | flops | bytes accessed | tf_op | source)
XLA Modules:
  0.0 202.7 jit_solution(3466503016582118686)
XLA Ops:
  7.2 0.7 convert_element_type.14
  7.9 0.1 convert_element_type.15
  8.0 1.3 copy-done.1
  9.3 1.1 copy-done.2
  10.4 0.7 copy-done.3
  11.0 2.7 %pack_waves.1 = (f32[12,40,128]{2,1,0:T(8,128)S(1)}, f32[4,40,128]{2,1,0:T(8,128)S(1)}, f32[12,40,128]{2,1,0:T(8,128)S(1)}, f32[4,40,128]{2,1,0:T(8,128)S(1)}, f32[8,328,128]{2,1,0:T(8,128)}) custom-call(s32[1,32]{1,0:T(1,128)S(1)} %copy-done.3, f32[40,32,128]{2,1,0:T(8,128)S(1)} %bitcast.31, f32[2,64,2560]{2,1,0:T(8,128)S(1)} %bitcast.29, ...), custom_call_target="tpu_custom_call" | custom-call | tf_op jit(solution)/shard_map/wave_exchange/pack_waves/pallas_call | solution.py:80
  13.8 0.0 copy-start.11
  13.8 0.0 copy-start.12
  13.8 0.0 copy-start.15
  13.8 0.0 copy-start.16
  13.9 0.0 copy-start.19
  13.9 8.6 %all-to-all-start = ((f32[8,328,128]{2,1,0:T(8,128)}), f32[8,328,128]{2,1,0:T(8,128)S(1)}, u32[]{:S(2)}, u32[]{:S(2)}) async-start(f32[8,328,128]{2,1,0:T(8,128)} %get-tuple-element.21), calls=%async_computation | async-start | bytes 2686976 | tf_op jit(solution)/shard_map/impedance_exchange/all_to_all | solution.py:450
  22.5 0.0 all-gather.2.cloned.1.call-start
  22.5 0.1 collective-permute-start
  22.6 3.8 %collective-permute-start.2 = (f32[12,40,128]{2,1,0:T(8,128)S(1)}, f32[12,40,128]{2,1,0:T(8,128)S(1)}, u32[]{:S(2)}, u32[]{:S(2)}) collective-permute-start(f32[12,40,128]{2,1,0:T(8,128)S(1)} %get-tuple-element.16), channel_id=1, source_target_pairs={{0,255},{1,0},{2,1},{3,2},{4,3},{5,4},{6,5},{7,6},{8,7},{9,8},{10,... | collective-permute-start | bytes 737288 | tf_op jit(solution)/shard_map/wave_exchange/ppermute | solution.py:404
  26.5 4.1 %collective-permute-start.3 = (f32[4,40,128]{2,1,0:T(8,128)S(1)}, f32[4,40,128]{2,1,0:T(8,128)S(1)}, u32[]{:S(2)}, u32[]{:S(2)}) collective-permute-start(f32[4,40,128]{2,1,0:T(8,128)S(1)} %get-tuple-element.17), channel_id=1, source_target_pairs={{0,254},{1,255},{2,0},{3,1},{4,2},{5,3},{6,4},{7,5},{8,6},{9,7},{1... | collective-permute-start | bytes 245768 | tf_op jit(solution)/shard_map/wave_exchange/ppermute | solution.py:404
  31.3 1.8 collective-permute-done.1.far_up
  33.2 2.2 %copy-done.5 = f32[1,1024,1024]{2,1,0:T(8,128)S(1)} copy-done((f32[1,1024,1024]{2,1,0:T(8,128)S(1)}, f32[1,1024,1024]{2,1,0:T(8,128)}, u32[]{:S(2)}) %copy-start.5) | copy-done | bytes 4194328
  35.4 34.3 %window.1 = (f32[20,32,128]{2,1,0:T(8,128)}, f32[1024,128]{1,0:T(8,128)}, f32[2,64,128]{2,1,0:T(8,128)}, f32[2,8,128]{2,1,0:T(8,128)S(1)}) custom-call(f32[2,20]{1,0:T(2,128)S(1)} %copy-done.19, s32[1,32]{1,0:T(1,128)S(1)} %copy-done.4, s32[1,32]{1,0:T(1,128)S(1)} %copy-done.11, s32[1]{0:T(128)S(6)} %copy.25.count, s32[1,32]{1,0:T(1,128)S(1)} %copy-done.12, ...), custom_call_target="tpu_custom_call" | custom-call | flops 16106127360 | bytes 67108864 | tf_op jit(solution)/shard_map/window/window/pallas_call | solution.py:287
  69.7 29.1 %all_to_all.25 = f32[64,2,8,128]{3,2,1,0:T(8,128)S(1)} all-to-all(f32[64,2,8,128]{3,2,1,0:T(8,128)S(1)} %spread_currents.1), channel_id=1, replica_groups=mesh['z'=8,'x'=4,'y'=4,'core'=2] {'z','y','core'}, dimensions={0} | all-to-all | bytes 1048576 | tf_op jit(solution)/shard_map/currents/all_to_all | solution.py:469
  98.8 0.7 bus_product.1
  99.5 33.6 %all_to_all.26 = f32[4,80,256]{2,1,0:T(8,128)S(1)} all-to-all(f32[4,80,256]{2,1,0:T(8,128)S(1)} %bitcast.30), channel_id=1, replica_groups=mesh['z'=8,'x'=4,'y'=4,'core'=2] {'x'}, dimensions={0} | all-to-all | bytes 655360 | tf_op jit(solution)/shard_map/bus_voltage/all_to_all | solution.py:475
  133.2 10.1 %all_to_all.27 = f32[4,80,256]{2,1,0:T(8,128)} all-to-all(f32[4,80,256]{2,1,0:T(8,128)S(1)} %broadcast_in_dim.24), channel_id=1, replica_groups=mesh['z'=8,'x'=4,'y'=4,'core'=2] {'x'}, dimensions={0} | all-to-all | bytes 655360 | tf_op jit(solution)/shard_map/bus_voltage/all_to_all | solution.py:409
  143.3 0.0 all-gather.2.cloned.1.call-update
  143.3 1.0 copy-done
  144.3 1.0 port_rows.1
  145.3 28.4 %all_to_all.28 = f32[64,8,256]{2,1,0:T(8,128)S(1)} all-to-all(f32[64,8,256]{2,1,0:T(8,128)S(1)} %bitcast.27), channel_id=1, replica_groups=mesh['z'=8,'x'=4,'y'=4,'core'=2] {'z','y','core'}, dimensions={0} | all-to-all | bytes 1048576 | tf_op jit(solution)/shard_map/port_voltage/all_to_all | solution.py:484
  173.8 0.1 reduce_sum.19
  173.8 0.6 maximum_bitcast_fusion
  174.4 17.8 %all-gather.2.cloned.1.call-done = f32[2560,256]{1,0:T(8,128)} async-done(((f32[320,256]{1,0:T(8,128)}), f32[2560,256]{1,0:T(8,128)}) %all-gather.2.cloned.1.call-update) | async-done | bytes 2621456 | tf_op jit(solution)/shard_map/bus_voltage/all_gather | solution.py:477
  192.3 1.9 slice_bitcast_fusion.1
  194.2 1.7 pad_maximum_fusion
  (40 shorter events, 0.2 us)
Async XLA Ops:
  7.9 1.3 copy-start.1
  9.3 1.1 copy-start.2
  10.4 0.7 copy-start.3
  13.7 19.3 %copy-start.4 = (s32[1,32]{1,0:T(1,128)S(1)}, s32[1,32]{1,0:T(1,128)}, u32[]{:S(2)}) copy-start(s32[1,32]{1,0:T(1,128)} %partner.3) | copy-start | bytes 388
  13.7 19.3 %copy-start.6 = (f32[1,1024,128]{2,1,0:T(8,128)S(1)}, f32[1,1024,128]{2,1,0:T(8,128)}, u32[]{:S(2)}) copy-start(f32[1,1024,128]{2,1,0:T(8,128)} %param.21) | copy-start | bytes 1572868
  13.7 19.3 %copy-start.7 = (f32[1,2,64,128]{3,2,1,0:T(8,128)S(1)}, f32[1,2,64,128]{3,2,1,0:T(8,128)}, u32[]{:S(2)}) copy-start(f32[1,2,64,128]{3,2,1,0:T(8,128)} %param.30) | copy-start | bytes 196612
  13.7 19.3 %copy-start.8 = (f32[1,2,64,128]{3,2,1,0:T(8,128)S(1)}, f32[1,2,64,128]{3,2,1,0:T(8,128)}, u32[]{:S(2)}) copy-start(f32[1,2,64,128]{3,2,1,0:T(8,128)} %param.31) | copy-start | bytes 196612
  13.8 19.3 %copy-start.9 = (f32[2,1,8,128]{3,2,1,0:T(8,128)S(1)}, f32[2,1,8,128]{3,2,1,0:T(8,128)}, u32[]{:S(2)}) copy-start(f32[2,1,8,128]{3,2,1,0:T(8,128)} %param.36) | copy-start | bytes 24580
  13.8 19.3 %copy-start.10 = (f32[1,1024]{1,0:T(1,128)S(1)}, f32[1,1024]{1,0:T(1,128)}, u32[]{:S(2)}) copy-start(f32[1,1024]{1,0:T(1,128)} %gcap_hbm.1) | copy-start | bytes 12292
  13.8 19.3 %copy-start.11 = (s32[1,32]{1,0:T(1,128)S(1)}, s32[1,32]{1,0:T(1,128)}, u32[]{:S(2)}) copy-start(s32[1,32]{1,0:T(1,128)} %delay.1) | copy-start | bytes 388
  13.8 19.3 %copy-start.12 = (s32[1,32]{1,0:T(1,128)S(1)}, s32[1,32]{1,0:T(1,128)}, u32[]{:S(2)}) copy-start(s32[1,32]{1,0:T(1,128)} %line_nodes.1) | copy-start | bytes 388
  13.8 19.3 %copy-start.13 = (s32[1,64]{1,0:T(1,128)S(1)}, s32[1,64]{1,0:T(1,128)}, u32[]{:S(2)}) copy-start(s32[1,64]{1,0:T(1,128)} %conv_nodes.1) | copy-start | bytes 772
  13.8 19.3 %copy-start.14 = (s32[1,8]{1,0:T(1,128)S(1)}, s32[1,8]{1,0:T(1,128)}, u32[]{:S(2)}) copy-start(s32[1,8]{1,0:T(1,128)} %port_nodes.1) | copy-start | bytes 100
  13.8 19.3 %copy-start.15 = (f32[1,32]{1,0:T(1,128)S(1)}, f32[1,32]{1,0:T(1,128)}, u32[]{:S(2)}) copy-start(f32[1,32]{1,0:T(1,128)} %line_adms.1) | copy-start | bytes 388
  13.8 19.3 %copy-start.16 = (f32[1,64]{1,0:T(1,128)S(1)}, f32[1,64]{1,0:T(1,128)}, u32[]{:S(2)}) copy-start(f32[1,64]{1,0:T(1,128)} %limits.1) | copy-start | bytes 772
  13.8 19.3 %copy-start.17 = (f32[1,64]{1,0:T(1,128)S(1)}, f32[1,64]{1,0:T(1,128)}, u32[]{:S(2)}) copy-start(f32[1,64]{1,0:T(1,128)} %rates.1) | copy-start | bytes 772
  13.9 19.3 %copy-start.18 = (f32[1,8]{1,0:T(1,128)S(1)}, f32[1,8]{1,0:T(1,128)}, u32[]{:S(2)}) copy-start(f32[1,8]{1,0:T(1,128)} %port_adms.1) | copy-start | bytes 100
  13.9 19.3 %copy-start.19 = (f32[2,20]{1,0:T(2,128)S(1)}, f32[2,20]{1,0:T(2,128)}, u32[]{:S(2)}) copy-start(f32[2,20]{1,0:T(2,128)} %constant.26.clone.angle) | copy-start | bytes 484
  13.9 55.8 %all-to-all-start = ((f32[8,328,128]{2,1,0:T(8,128)}), f32[8,328,128]{2,1,0:T(8,128)S(1)}, u32[]{:S(2)}, u32[]{:S(2)}) async-start(f32[8,328,128]{2,1,0:T(8,128)} %get-tuple-element.21), calls=%async_computation | async-start | bytes 2686976 | tf_op jit(solution)/shard_map/impedance_exchange/all_to_all | solution.py:450
  22.5 169.8 %all-gather.2.cloned.1.call-start = ((), (), s32[]{:S(2)}) async-start(), calls=%async_computation.5 | async-start | bytes 2949120 | tf_op jit(solution)/shard_map/bus_voltage/all_gather | solution.py:477
  22.5 10.5 %collective-permute-start = (f32[12,40,128]{2,1,0:T(8,128)S(1)}, f32[12,40,128]{2,1,0:T(8,128)S(1)}, u32[]{:S(2)}, u32[]{:S(2)}) collective-permute-start(f32[12,40,128]{2,1,0:T(8,128)S(1)} %get-tuple-element.14), channel_id=1, source_target_pairs={{0,1},{1,2},{2,3},{3,4},{4,5},{5,6},{6,7},{7,8},{8,9},{9,10},{10,1... | collective-permute-start | bytes 737288 | tf_op jit(solution)/shard_map/wave_exchange/ppermute | solution.py:404
  22.6 10.4 %collective-permute-start.2 = (f32[12,40,128]{2,1,0:T(8,128)S(1)}, f32[12,40,128]{2,1,0:T(8,128)S(1)}, u32[]{:S(2)}, u32[]{:S(2)}) collective-permute-start(f32[12,40,128]{2,1,0:T(8,128)S(1)} %get-tuple-element.16), channel_id=1, source_target_pairs={{0,255},{1,0},{2,1},{3,2},{4,3},{5,4},{6,5},{7,6},{8,7},{9,8},{10,... | collective-permute-start | bytes 737288 | tf_op jit(solution)/shard_map/wave_exchange/ppermute | solution.py:404
  26.5 6.6 %collective-permute-start.1 = (f32[4,40,128]{2,1,0:T(8,128)S(1)}, f32[4,40,128]{2,1,0:T(8,128)S(1)}, u32[]{:S(2)}, u32[]{:S(2)}) collective-permute-start(f32[4,40,128]{2,1,0:T(8,128)S(1)} %get-tuple-element.15), channel_id=1, source_target_pairs={{0,2},{1,3},{2,4},{3,5},{4,6},{5,7},{6,8},{7,9},{8,10},{9,11},{10,... | collective-permute-start | bytes 245768 | tf_op jit(solution)/shard_map/wave_exchange/ppermute | solution.py:404
  26.5 6.6 %collective-permute-start.3 = (f32[4,40,128]{2,1,0:T(8,128)S(1)}, f32[4,40,128]{2,1,0:T(8,128)S(1)}, u32[]{:S(2)}, u32[]{:S(2)}) collective-permute-start(f32[4,40,128]{2,1,0:T(8,128)S(1)} %get-tuple-element.17), channel_id=1, source_target_pairs={{0,254},{1,255},{2,0},{3,1},{4,2},{5,3},{6,4},{7,5},{8,6},{9,7},{1... | collective-permute-start | bytes 245768 | tf_op jit(solution)/shard_map/wave_exchange/ppermute | solution.py:404
  33.2 2.2 %copy-start.5 = (f32[1,1024,1024]{2,1,0:T(8,128)S(1)}, f32[1,1024,1024]{2,1,0:T(8,128)}, u32[]{:S(2)}) copy-start(f32[1,1024,1024]{2,1,0:T(8,128)} %param.20) | copy-start | bytes 12582916
  143.3 1.0 copy-start
Sparse Core Ops, SparseCore 0:
  143.4 48.8 all-gather.1

commit v3 on v2

--- a/solution.py
+++ b/solution.py
@@ -38,7 +38,7 @@
     return jnp.bitwise_and(partner[0, line] - partner[0, HALF + line], 255) // 2
 
 
-def pack_kernel(partner, waves, impedance, ports, near_up, far_up, near_down, far_down, blocks):
+def pack_kernel(partner, waves, near_up, far_up, near_down, far_down):
     near = jnp.int32(0)
     for line in range(HALF):
         is_near = reach_of(partner, line) == 1
@@ -56,6 +56,25 @@
             far_down[far] = down
 
         near = near + is_near.astype(jnp.int32)
+
+
+def pack(partner, waves):
+    hist, _, cases = waves.shape
+    near = jax.ShapeDtypeStruct((NEAR, hist, cases), F32)
+    far = jax.ShapeDtypeStruct((HALF - NEAR, hist, cases), F32)
+    vmem = pl.BlockSpec(memory_space=pltpu.VMEM)
+    return pl.pallas_call(
+        pack_kernel,
+        out_shape=(near, far, near, far),
+        in_specs=[pl.BlockSpec(memory_space=pltpu.SMEM), vmem],
+        out_specs=(vmem,) * 4,
+        compiler_params=pltpu.CompilerParams(vmem_limit_bytes=32 << 20),
+        name="pack_waves",
+    )(partner, waves)
+
+
+def turn_kernel(impedance, ports, *rest):
+    blocks = rest[-1]
     areas, rows, _ = blocks.shape
     rows = rows - 8
     for first in range(0, areas * rows, 128):
@@ -71,20 +90,16 @@
         blocks[area, pl.ds(rows, 8), :] = jnp.broadcast_to(ports[...], (8, 128))
 
 
-def pack(partner, waves, impedance, ports, areas):
-    hist, _, cases = waves.shape
-    near = jax.ShapeDtypeStruct((NEAR, hist, cases), F32)
-    far = jax.ShapeDtypeStruct((HALF - NEAR, hist, cases), F32)
-    blocks = jax.ShapeDtypeStruct((areas, impedance.shape[2] // areas + 8, 128), F32)
+def turn(impedance, ports, arrivals, areas):
     vmem = pl.BlockSpec(memory_space=pltpu.VMEM)
     return pl.pallas_call(
-        pack_kernel,
-        out_shape=(near, far, near, far, blocks),
-        in_specs=[pl.BlockSpec(memory_space=pltpu.SMEM), vmem, vmem, vmem],
-        out_specs=(vmem,) * 5,
+        turn_kernel,
+        out_shape=jax.ShapeDtypeStruct((areas, impedance.shape[2] // areas + 8, 128), F32),
+        in_specs=[vmem] * (2 + len(arrivals)),
+        out_specs=vmem,
         compiler_params=pltpu.CompilerParams(vmem_limit_bytes=32 << 20),
-        name="pack_waves",
-    )(partner, waves, impedance, ports)
+        name="turn_impedance",
+    )(impedance, ports, *arrivals)
 
 
 def column(row):
@@ -293,7 +308,7 @@
             jax.ShapeDtypeStruct((2, PORTS, cases), F32),
         ),
         in_specs=[smem] * len(scalars)
-        + [pl.BlockSpec(memory_space=pl.ANY)] * len(far)
+        + [pl.BlockSpec(memory_space=pltpu.HBM)] * len(far)
         + [vmem] * len(rows),
         out_specs=(vmem,) * 4,
         scratch_shapes=[
@@ -318,7 +333,7 @@
             pltpu.SemaphoreType.DMA((4,)),
             pltpu.SemaphoreType.DMA((5,)),
         ],
-        compiler_params=pltpu.CompilerParams(vmem_limit_bytes=44 << 20),
+        compiler_params=pltpu.CompilerParams(vmem_limit_bytes=59 << 20),
         cost_estimate=pl.CostEstimate(
             flops=6 * STEPS * nodes * nodes * cases,
             bytes_accessed=64 << 20,
@@ -346,26 +361,32 @@
 
 
 def bus_kernel(impedance, current, out):
-    areas, members = current.shape[:2]
-    rows = pl.ds(0, out.shape[0])
+    members, areas = current.shape[:2]
+    rows = pl.ds(0, out.shape[0] * out.shape[2])
     z = jnp.concatenate([impedance[i, rows, :] for i in range(areas)], axis=1)
     parts = []
     for i in range(areas):
-        real = jnp.concatenate([current[i, r, 0] for r in range(members)], axis=0)
-        imag = jnp.concatenate([current[i, r, 1] for r in range(members)], axis=0)
+        real = jnp.concatenate([current[r, i, 0] for r in range(members)], axis=0)
+        imag = jnp.concatenate([current[r, i, 1] for r in range(members)], axis=0)
         parts.append(jnp.concatenate([real, imag], axis=1))
         parts.append(jnp.concatenate([-imag, real], axis=1))
     w = jnp.concatenate(parts, axis=0)
     z_high, z_low = split(z)
     w_high, w_low = split(w)
-    out[...] = dot(z_high, w_high) + dot(z_low, w_high) + dot(z_high, w_low)
-
-
-def bus_product(impedance, current):
+    volts = dot(z_high, w_high) + dot(z_low, w_high) + dot(z_high, w_low)
+    size = out.shape[2]
+    for i in range(out.shape[0]):
+        for k in range(2):
+            out[i, k] = volts[i * size : (i + 1) * size, k * 128 : (k + 1) * 128]
+
+
+def bus_product(impedance, current, pieces):
     vmem = pl.BlockSpec(memory_space=pltpu.VMEM)
     return pl.pallas_call(
         bus_kernel,
-        out_shape=jax.ShapeDtypeStruct((impedance.shape[1] - 8, 256), F32),
+        out_shape=jax.ShapeDtypeStruct(
+            (pieces, 2, (impedance.shape[1] - 8) // pieces, 128), F32
+        ),
         in_specs=[vmem] * 2,
         out_specs=vmem,
         compiler_params=pltpu.CompilerParams(vmem_limit_bytes=32 << 20),
@@ -374,24 +395,25 @@
 
 
 def port_kernel(first, ports, volts, out):
-    rows = volts.shape[0]
-    high, rest = split(volts[...])
-    middle = volts[...] - high.astype(F32)
+    rows = volts.shape[1]
+    both = jnp.concatenate([volts[0], volts[1]], axis=1)
+    high, rest = split(both)
+    middle = both - high.astype(F32)
     low = (middle - rest.astype(F32)).astype(BF16)
     row = lax.broadcasted_iota(jnp.int32, (rows, 128), 0) + first[0]
     for area in range(ports.shape[0]):
         wanted = ports[area, pl.ds(rows, 1), :].astype(jnp.int32)
         picks = jnp.where(row == wanted, 1.0, 0.0).T.astype(BF16)
         found = dot(picks, high) + dot(picks, rest) + dot(picks, low)
-        count = out.shape[1] * out.shape[2]
-        out[area] = found[:count].reshape(out.shape[1:])
+        for member in range(out.shape[0]):
+            out[member, area] = found[member * PORTS : (member + 1) * PORTS]
 
 
 def port_rows(first, ports, volts, members):
     vmem = pl.BlockSpec(memory_space=pltpu.VMEM)
     return pl.pallas_call(
         port_kernel,
-        out_shape=jax.ShapeDtypeStruct((ports.shape[0], members, PORTS, volts.shape[1]), F32),
+        out_shape=jax.ShapeDtypeStruct((members, ports.shape[0], PORTS, 2 * volts.shape[2]), F32),
         in_specs=[pl.BlockSpec(memory_space=pltpu.SMEM), vmem, vmem],
         out_specs=vmem,
         compiler_params=pltpu.CompilerParams(vmem_limit_bytes=32 << 20),
@@ -434,12 +456,7 @@
     members = lax.axis_size(ROW)
     bus_rows = transfer_impedance.shape[1]
     with jax.named_scope("wave_exchange"):
-        ports = port_bus.reshape(1, -1).astype(F32)
-        ports = jnp.pad(ports, ((0, 0), (0, 128 - ports.shape[1])), constant_values=-1.0)
-        turned = jnp.swapaxes(transfer_impedance, 1, 2)
-        near_up, far_up, near_down, far_down, blocks = pack(
-            line_partner, wave_history[0], turned, ports, areas
-        )
+        near_up, far_up, near_down, far_down = pack(line_partner, wave_history[0])
         arrivals = (
             shifted(near_up, 1),
             shifted(far_up, 2),
@@ -447,6 +464,9 @@
             shifted(far_down, -2),
         )
     with jax.named_scope("impedance_exchange"):
+        ports = port_bus.reshape(1, -1).astype(F32)
+        ports = jnp.pad(ports, ((0, 0), (0, 128 - ports.shape[1])), constant_values=-1.0)
+        blocks = turn(jnp.swapaxes(transfer_impedance, 1, 2), ports, arrivals, areas)
         impedance = lax.all_to_all(blocks, "z", 0, 0, tiled=True)
     with jax.named_scope("window"):
         theta = np.arange(1, STEPS + 1, dtype=np.float32) * np.float32(2.0 * math.pi / STEPS)
@@ -465,23 +485,21 @@
             (line_admittance, conv_limit, conv_rate, port_admittance),
         )
     with jax.named_scope("currents"):
-        flat = spread(current, impedance, areas * members)
-        flat = lax.all_to_all(flat, ("z", *ROW), 0, 0, tiled=True)
-        flat = flat.reshape(areas, members, *current.shape)
+        flat = spread(current, impedance, areas)
+        flat = copy_for_each(lax.all_to_all(flat, "z", 0, 0, tiled=True), ROW)
+        flat = flat.reshape(members, areas, *current.shape)
     with jax.named_scope("bus_voltage"):
-        partial = bus_product(impedance, flat)
-        size = lax.axis_size("x")
-        pieces = partial.reshape(size, -1, partial.shape[1])
+        pieces = bus_product(impedance, flat, lax.axis_size("x"))
         own = jnp.sum(lax.all_to_all(pieces, "x", 0, 0, tiled=True), axis=0)
-        block = copy_for_each(own, "x").reshape(partial.shape)
-        volts = lax.all_gather(block, "z", tiled=True)
-        cases = volts.shape[1] // 2
-        bus_voltage = jnp.stack([volts[:, :cases], volts[:, cases:]])
+        block = jnp.moveaxis(copy_for_each(own, "x"), 0, 1)
+        block = block.reshape(2, -1, block.shape[-1])
+        bus_voltage = lax.all_gather(block, "z", axis=1, tiled=True)
     with jax.named_scope("port_voltage"):
-        first = lax.axis_index(ROW) * bus_rows + lax.axis_index("z") * partial.shape[0]
+        first = lax.axis_index(ROW) * bus_rows + lax.axis_index("z") * block.shape[1]
         picked = port_rows(first[None].astype(jnp.int32), impedance, block, members)
-        picked = picked.reshape(areas * members, PORTS, 2 * cases)
-        mine = jnp.sum(lax.all_to_all(picked, ("z", *ROW), 0, 0, tiled=True), axis=0)
+        mine = jnp.sum(lax.all_to_all(picked, ROW, 0, 0, tiled=True), axis=0)
+        mine = jnp.sum(lax.all_to_all(mine, "z", 0, 0, tiled=True), axis=0)
+        cases = mine.shape[1] // 2
         port_voltage = jnp.stack([mine[:, :cases], mine[:, cases:]])[:, None]
     return (outward[None], hist_end[None], conv_out[None], bus_voltage, port_voltage)
 

time: 203 us -> 175 us (0.86)
  blocking collectives: 101 us -> 80.1 us
  waiting for transfers between devices: 19.6 us -> 12 us
    all_to_all x2 -> x3, blocking collectives: 57.5 us -> 39.5 us  [the longest x1 15.3 us: per_device(): flat = copy_for_each(lax.all_to_all(flat, 'z', 0, 0, tiled=True), ROW)]
    all_to_all x1, blocking collectives: 33.6 us -> 15.6 us  [per_device(): own = jnp.sum(lax.all_to_all(pieces, 'x', 0, 0, tiled=True), axis=0)]
    all_to_all x1 -> x2, blocking collectives: 10.1 us -> 25 us  [copy_for_each(): lax.all_to_all(jnp.broadcast_to(x[None], (size, *x.shape)), axis, 0, 0, t...]
    all_gather x1, waiting for transfers between devices: 17.8 us -> 10.3 us  [per_device(): bus_voltage = lax.all_gather(block, 'z', axis=1, tiled=True)]
    unnamed x40 -> x19, local copies, waits for them, and re-layouts: 6.29 us -> 8.33 us
    pallas_call x3 -> x4, Pallas kernels: 4.45 us -> 4.45 us  [the longest x1 1.47 us: turn(): pl.pallas_call(turn_kernel, out_shape=jax.ShapeDtypeStruct((areas, impeda...]
  transfers between devices with their start and end apart: 6 -> 6, of which waited for: 2 -> 2; matrix products, arithmetic and copies ran while one was open for 0% -> 1% of each run, Pallas kernels for 17% -> 21%
where the time goes in v3:
time: 175 us; the launch traced here: 174 us
  blocking collectives  80.1 us (46%)
  Pallas kernels  40.1 us (23%)
  starting transfers between devices  16.6 us (9%)
  between operations  14.8 us (8%)
  waiting for transfers between devices  12 us (7%)
  local copies, waits for them, and re-layouts  9.23 us (5%)
    pallas_call x1, Pallas kernels, window(): pl.pallas_call(window_kernel, out_shape=(jax.ShapeDtypeStruct((STEPS, LIN...  35.6 us
    all_to_all x2, blocking collectives, copy_for_each(): lax.all_to_all(jnp.broadcast_to(x[None], (size, *x.shape)), axis, 0, 0, t...  25 us
    all_to_all x1, blocking collectives, per_device(): own = jnp.sum(lax.all_to_all(pieces, 'x', 0, 0, tiled=True), axis=0)  15.6 us
    all_to_all x1, blocking collectives, per_device(): flat = copy_for_each(lax.all_to_all(flat, 'z', 0, 0, tiled=True), ROW)  15.3 us
    all_to_all x1, blocking collectives, per_device(): mine = jnp.sum(lax.all_to_all(picked, ROW, 0, 0, tiled=True), axis=0)  12.8 us
    all_to_all x1, blocking collectives, per_device(): mine = jnp.sum(lax.all_to_all(mine, 'z', 0, 0, tiled=True), axis=0)  11.4 us
    all_gather x1, waiting for transfers between devices, per_device(): bus_voltage = lax.all_gather(block, 'z', axis=1, tiled=True)  10.3 us
    all_to_all x1, starting transfers between devices, per_device(): impedance = lax.all_to_all(blocks, 'z', 0, 0, tiled=True)  8.48 us
  transfers between devices with their start and end apart: 6, of which 2 were waited for; matrix products, arithmetic and copies ran while one was open for 1% of the time, Pallas kernels for 21%

profile of v3, /device:TPU:2, one launch (start us, length us, event | category | flops | bytes accessed | tf_op | source)
XLA Modules:
  0.0 174.1 jit_solution(7159016180925599450)
XLA Ops:
  7.2 1.1 copy-done.2
  8.3 0.7 copy-done.8
  8.9 1.3 pack_waves.1
  10.2 0.1 collective-permute-start
  10.3 3.8 %collective-permute-start.2 = (f32[12,40,128]{2,1,0:T(8,128)S(1)}, f32[12,40,128]{2,1,0:T(8,128)S(1)}, u32[]{:S(2)}, u32[]{:S(2)}) collective-permute-start(f32[12,40,128]{2,1,0:T(8,128)S(1)} %get-tuple-element.15), channel_id=1, source_target_pairs={{0,255},{1,0},{2,1},{3,2},{4,3},{5,4},{6,5},{7,6},{8,7},{9,8},{10,... | collective-permute-start | bytes 737288 | tf_op jit(solution)/shard_map/wave_exchange/ppermute | solution.py:426
  14.1 4.1 %collective-permute-start.3 = (f32[4,40,128]{2,1,0:T(8,128)S(1)}, f32[4,40,128]{2,1,0:T(8,128)S(1)}, u32[]{:S(2)}, u32[]{:S(2)}) collective-permute-start(f32[4,40,128]{2,1,0:T(8,128)S(1)} %get-tuple-element.16), channel_id=1, source_target_pairs={{0,254},{1,255},{2,0},{3,1},{4,2},{5,3},{6,4},{7,5},{8,6},{9,7},{1... | collective-permute-start | bytes 245768 | tf_op jit(solution)/shard_map/wave_exchange/ppermute | solution.py:426
  18.2 0.7 convert_element_type.14
  18.9 0.1 convert_element_type.15
  19.0 1.6 collective-permute-done.1.far_up.rest_1_
  20.7 0.0 copy-start.1
  20.7 1.5 copy-done.1
  22.2 1.5 turn_impedance.1
  23.7 8.5 %all-to-all-start = ((f32[8,328,128]{2,1,0:T(8,128)}), f32[8,328,128]{2,1,0:T(8,128)S(1)}, u32[]{:S(2)}, u32[]{:S(2)}) async-start(f32[8,328,128]{2,1,0:T(8,128)} %turn_impedance.1), calls=%async_computation | async-start | bytes 2686976 | tf_op jit(solution)/shard_map/impedance_exchange/all_to_all | solution.py:470
  32.2 0.0 all-gather.2.cloned.1.call-start
  32.9 35.6 %window.1 = (f32[20,32,128]{2,1,0:T(8,128)}, f32[1024,128]{1,0:T(8,128)}, f32[2,64,128]{2,1,0:T(8,128)}, f32[2,8,128]{2,1,0:T(8,128)}) custom-call(f32[2,20]{1,0:T(2,128)} %constant.26.clone.angle, s32[1,32]{1,0:T(1,128)} %partner.3, s32[1,32]{1,0:T(1,128)} %delay.1, s32[1]{0:T(128)S(6)} %copy.29.count, s32[1,32]{1,0:T(1,128)} %line_nodes.1, ...), custom_call_target="tpu_custom_call" | custom-call | flops 16106127360 | bytes 67108864 | tf_op jit(solution)/shard_map/window/window/pallas_call | solution.py:302
  68.5 0.0 copy-start.7
  68.5 0.7 copy-done.7
  69.2 15.3 %all_to_all.35 = f32[8,2,8,128]{3,2,1,0:T(8,128)S(1)} all-to-all(f32[8,2,8,128]{3,2,1,0:T(8,128)S(1)} %spread_currents.1), channel_id=1, replica_groups=mesh['z'=8,'x'=4,'y'=4,'core'=2] {'z'}, dimensions={0} | all-to-all | bytes 131072 | tf_op jit(solution)/shard_map/currents/all_to_all | solution.py:489
  84.6 15.6 %all_to_all.36.current = f32[8,8,2,8,128]{4,3,2,1,0:T(8,128)S(1)} all-to-all(f32[8,8,2,8,128]{4,3,2,1,0:T(8,128)S(1)} %broadcast_in_dim.30), channel_id=1, replica_groups=mesh['z'=8,'x'=4,'y'=4,'core'=2] {'y','core'}, dimensions={0} | all-to-all | bytes 1048576 | tf_op jit(solution)/shard_map/currents/all_to_all | solution.py:431
  100.2 0.7 bus_product.1
  100.9 15.6 %all_to_all.37 = f32[4,2,80,128]{3,2,1,0:T(8,128)S(1)} all-to-all(f32[4,2,80,128]{3,2,1,0:T(8,128)S(1)} %bus_product.1), channel_id=1, replica_groups=mesh['z'=8,'x'=4,'y'=4,'core'=2] {'x'}, dimensions={0} | all-to-all | bytes 655360 | tf_op jit(solution)/shard_map/bus_voltage/all_to_all | solution.py:493
  116.5 9.4 %all_to_all.38 = f32[4,2,80,128]{3,2,1,0:T(8,128)S(1)} all-to-all(f32[4,2,80,128]{3,2,1,0:T(8,128)S(1)} %broadcast_in_dim.31), channel_id=1, replica_groups=mesh['z'=8,'x'=4,'y'=4,'core'=2] {'x'}, dimensions={0} | all-to-all | bytes 655360 | tf_op jit(solution)/shard_map/bus_voltage/all_to_all | solution.py:431
  125.9 0.7 copy.26
  126.7 0.0 all-gather.2.cloned.1.call-update
  126.7 0.0 copy-start
  126.7 1.0 copy-done
  127.7 1.0 port_rows.1
  128.7 12.8 %all_to_all.39 = f32[8,8,8,256]{3,2,1,0:T(8,128)S(1)} all-to-all(f32[8,8,8,256]{3,2,1,0:T(8,128)S(1)} %port_rows.1), channel_id=1, replica_groups=mesh['z'=8,'x'=4,'y'=4,'core'=2] {'y','core'}, dimensions={0} | all-to-all | bytes 1048576 | tf_op jit(solution)/shard_map/port_voltage/all_to_all | solution.py:500
  141.6 11.4 %all_to_all.40 = f32[8,8,256]{2,1,0:T(8,128)S(1)} all-to-all(f32[8,8,256]{2,1,0:T(8,128)S(1)} %reduce_sum.28), channel_id=1, replica_groups=mesh['z'=8,'x'=4,'y'=4,'core'=2] {'z'}, dimensions={0} | all-to-all | bytes 131072 | tf_op jit(solution)/shard_map/port_voltage/all_to_all | solution.py:501
  153.0 0.6 maximum_bitcast_fusion
  153.6 10.3 %all-gather.2.cloned.1.call-done = f32[2,2560,128]{2,1,0:T(8,128)} async-done(((f32[2,320,128]{2,1,0:T(8,128)}), f32[2,2560,128]{2,1,0:T(8,128)}) %all-gather.2.cloned.1.call-update) | async-done | bytes 2621456 | tf_op jit(solution)/shard_map/bus_voltage/all_gather | solution.py:496
  163.9 3.4 %copy.30 = f32[2,2560,128]{2,1,0:T(8,128)} copy(f32[2,2560,128]{2,1,0:T(8,128)} %all-gather.2.cloned.1.call-done) | data formatting | bytes 5242880
  (23 shorter events, 0.2 us)
Async XLA Ops:
  7.2 1.1 copy-start.2
  8.3 0.7 copy-start.8
  10.2 10.5 %collective-permute-start = (f32[12,40,128]{2,1,0:T(8,128)S(1)}, f32[12,40,128]{2,1,0:T(8,128)S(1)}, u32[]{:S(2)}, u32[]{:S(2)}) collective-permute-start(f32[12,40,128]{2,1,0:T(8,128)S(1)} %get-tuple-element.13), channel_id=1, source_target_pairs={{0,1},{1,2},{2,3},{3,4},{4,5},{5,6},{6,7},{7,8},{8,9},{9,10},{10,1... | collective-permute-start | bytes 737288 | tf_op jit(solution)/shard_map/wave_exchange/ppermute | solution.py:426
  10.3 10.4 %collective-permute-start.2 = (f32[12,40,128]{2,1,0:T(8,128)S(1)}, f32[12,40,128]{2,1,0:T(8,128)S(1)}, u32[]{:S(2)}, u32[]{:S(2)}) collective-permute-start(f32[12,40,128]{2,1,0:T(8,128)S(1)} %get-tuple-element.15), channel_id=1, source_target_pairs={{0,255},{1,0},{2,1},{3,2},{4,3},{5,4},{6,5},{7,6},{8,7},{9,8},{10,... | collective-permute-start | bytes 737288 | tf_op jit(solution)/shard_map/wave_exchange/ppermute | solution.py:426
  14.1 6.6 %collective-permute-start.1 = (f32[4,40,128]{2,1,0:T(8,128)S(1)}, f32[4,40,128]{2,1,0:T(8,128)S(1)}, u32[]{:S(2)}, u32[]{:S(2)}) collective-permute-start(f32[4,40,128]{2,1,0:T(8,128)S(1)} %get-tuple-element.14), channel_id=1, source_target_pairs={{0,2},{1,3},{2,4},{3,5},{4,6},{5,7},{6,8},{7,9},{8,10},{9,11},{10,... | collective-permute-start | bytes 245768 | tf_op jit(solution)/shard_map/wave_exchange/ppermute | solution.py:426
  14.1 6.6 %collective-permute-start.3 = (f32[4,40,128]{2,1,0:T(8,128)S(1)}, f32[4,40,128]{2,1,0:T(8,128)S(1)}, u32[]{:S(2)}, u32[]{:S(2)}) collective-permute-start(f32[4,40,128]{2,1,0:T(8,128)S(1)} %get-tuple-element.16), channel_id=1, source_target_pairs={{0,254},{1,255},{2,0},{3,1},{4,2},{5,3},{6,4},{7,5},{8,6},{9,7},{1... | collective-permute-start | bytes 245768 | tf_op jit(solution)/shard_map/wave_exchange/ppermute | solution.py:426
  20.7 3.0 %copy-start.5 = (f32[4,40,128]{2,1,0:T(8,128)}, f32[4,40,128]{2,1,0:T(8,128)S(1)}, u32[]{:S(2)}) copy-start(f32[4,40,128]{2,1,0:T(8,128)S(1)} %collective-permute-done.1.far_up.rest_1_) | copy-start | bytes 245764
  20.7 3.0 %copy-start.6 = (f32[4,40,128]{2,1,0:T(8,128)}, f32[4,40,128]{2,1,0:T(8,128)S(1)}, u32[]{:S(2)}) copy-start(f32[4,40,128]{2,1,0:T(8,128)S(1)} %collective-permute-done.3.far_down.rest_3_) | copy-start | bytes 245764
  20.7 3.0 %copy-start.3 = (f32[12,40,128]{2,1,0:T(8,128)}, f32[12,40,128]{2,1,0:T(8,128)S(1)}, u32[]{:S(2)}) copy-start(f32[12,40,128]{2,1,0:T(8,128)S(1)} %collective-permute-done.near_up.rest_0_) | copy-start | bytes 737284
  20.7 3.0 %copy-start.4 = (f32[12,40,128]{2,1,0:T(8,128)}, f32[12,40,128]{2,1,0:T(8,128)S(1)}, u32[]{:S(2)}) copy-start(f32[12,40,128]{2,1,0:T(8,128)S(1)} %collective-permute-done.2.near_down.rest_2_) | copy-start | bytes 737284
  20.7 1.5 copy-start.1
  23.7 44.8 %all-to-all-start = ((f32[8,328,128]{2,1,0:T(8,128)}), f32[8,328,128]{2,1,0:T(8,128)S(1)}, u32[]{:S(2)}, u32[]{:S(2)}) async-start(f32[8,328,128]{2,1,0:T(8,128)} %turn_impedance.1), calls=%async_computation | async-start | bytes 2686976 | tf_op jit(solution)/shard_map/impedance_exchange/all_to_all | solution.py:470
  32.2 131.7 %all-gather.2.cloned.1.call-start = ((), (), s32[]{:S(2)}) async-start(), calls=%async_computation.7 | async-start | bytes 2949120 | tf_op jit(solution)/shard_map/bus_voltage/all_gather | solution.py:496
  68.5 0.7 copy-start.7
  126.7 1.0 copy-start
Sparse Core Ops, SparseCore 0:
  126.8 37.0 all-gather.1

commit v4 on v3

--- a/solution.py
+++ b/solution.py
@@ -18,6 +18,7 @@
 HALF = LINES // 2
 PROBES = LINES + CONV + PORTS
 SAG_FACTOR = 0.3
+UNROLL = 4
 ALL = ("z", "x", "y", "core")
 AREA = ("z", "x")
 ROW = ("y", "core")
@@ -224,8 +225,12 @@
         at = pl.ds(i * rows, rows)
         g_high[at, pl.ds(0, nodes)] = high
         g_low[at, :] = low
-        g_high[at, pl.ds(nodes, 128)] = dot(high, picks).astype(BF16)
-        g_high[at, pl.ds(nodes + 128, 128)] = dot(low, picks).astype(BF16)
+
+    half = nodes // 2
+    for i in range(0, nodes, half):
+        at = pl.ds(i, half)
+        g_high[at, pl.ds(nodes, 128)] = dot(g_high[at, pl.ds(0, nodes)], picks).astype(BF16)
+        g_high[at, pl.ds(nodes + 128, 128)] = dot(g_low[at, :], picks).astype(BF16)
 
     for move in moves:
         move.wait()
@@ -282,12 +287,13 @@
         current[0] = current[0] + flow * cos
         current[1] = current[1] - flow * sin
 
-    def pair(i, _):
-        step(2 * i, w_even, w_odd)
-        step(2 * i + 1, w_odd, w_even)
+    def several(i, _):
+        for j in range(0, UNROLL, 2):
+            step(UNROLL * i + j, w_even, w_odd)
+            step(UNROLL * i + j + 1, w_odd, w_even)
         return 0
 
-    lax.fori_loop(0, STEPS // 2, pair, 0)
+    lax.fori_loop(0, STEPS // UNROLL, several, 0)
     current[...] = current[...] * (2.0 / STEPS)
 
 
@@ -360,38 +366,62 @@
     )(current, impedance)
 
 
-def bus_kernel(impedance, current, out):
-    members, areas = current.shape[:2]
-    rows = pl.ds(0, out.shape[0] * out.shape[2])
+def bus_kernel(place, impedance, own, other, out, gathered):
+    chips, areas = own.shape[:2]
+    y, core = place[0], place[1]
+    for k in range(chips):
+        row = lax.rem(y - k + chips, chips) * 2
+        for i in range(areas):
+            for part in range(2):
+                gathered[i, part, row + core] = own[k, i, part]
+                gathered[i, part, row + 1 - core] = other[k, i, part]
+    rows = pl.ds(0, out.shape[1])
     z = jnp.concatenate([impedance[i, rows, :] for i in range(areas)], axis=1)
     parts = []
     for i in range(areas):
-        real = jnp.concatenate([current[r, i, 0] for r in range(members)], axis=0)
-        imag = jnp.concatenate([current[r, i, 1] for r in range(members)], axis=0)
+        real = gathered[i, 0].reshape(-1, 128)
+        imag = gathered[i, 1].reshape(-1, 128)
         parts.append(jnp.concatenate([real, imag], axis=1))
         parts.append(jnp.concatenate([-imag, real], axis=1))
     w = jnp.concatenate(parts, axis=0)
     z_high, z_low = split(z)
     w_high, w_low = split(w)
     volts = dot(z_high, w_high) + dot(z_low, w_high) + dot(z_high, w_low)
-    size = out.shape[2]
-    for i in range(out.shape[0]):
-        for k in range(2):
-            out[i, k] = volts[i * size : (i + 1) * size, k * 128 : (k + 1) * 128]
-
-
-def bus_product(impedance, current, pieces):
+    out[0] = volts[:, :128]
+    out[1] = volts[:, 128:]
+
+
+def bus_product(place, impedance, own, other):
+    chips, areas, _, ports, cases = own.shape
     vmem = pl.BlockSpec(memory_space=pltpu.VMEM)
     return pl.pallas_call(
         bus_kernel,
-        out_shape=jax.ShapeDtypeStruct(
-            (pieces, 2, (impedance.shape[1] - 8) // pieces, 128), F32
-        ),
-        in_specs=[vmem] * 2,
+        out_shape=jax.ShapeDtypeStruct((2, impedance.shape[1] - 8, cases), F32),
+        in_specs=[pl.BlockSpec(memory_space=pltpu.SMEM)] + [vmem] * 3,
         out_specs=vmem,
+        scratch_shapes=[pltpu.VMEM((areas, 2, 2 * chips, ports, cases), F32)],
         compiler_params=pltpu.CompilerParams(vmem_limit_bytes=32 << 20),
         name="bus_product",
-    )(impedance, current)
+    )(place, impedance, own, other)
+
+
+def sum_kernel(*refs):
+    total = refs[0][...]
+    for ref in refs[1:-1]:
+        total = total + ref[...]
+    refs[-1][...] = total
+
+
+def sum_of(parts):
+    vmem = pl.BlockSpec(memory_space=pltpu.VMEM)
+    return pl.pallas_call(
+        sum_kernel,
+        out_shape=jax.ShapeDtypeStruct(parts[0].shape, F32),
+        in_specs=[vmem] * len(parts),
+        out_specs=vmem,
+        compiler_params=pltpu.CompilerParams(vmem_limit_bytes=16 << 20),
+        name="sum_of_parts",
+    )(*parts)
 
 
 def port_kernel(first, ports, volts, out):
@@ -426,9 +456,14 @@
     return lax.ppermute(x, ALL, [(i, (i + by) % size) for i in range(size)])
 
 
-def copy_for_each(x, axis):
+def along(x, axis, by):
     size = lax.axis_size(axis)
-    return lax.all_to_all(jnp.broadcast_to(x[None], (size, *x.shape)), axis, 0, 0, tiled=True)
+    return lax.ppermute(x, axis, [(i, (i + by) % size) for i in range(size)])
+
+
+def from_all(x, axis):
+    near, far, back = (along(x, axis, by) for by in (1, 3, 2))
+    return x, near, back, far
 
 
 def per_device(
@@ -486,13 +521,13 @@
         )
     with jax.named_scope("currents"):
         flat = spread(current, impedance, areas)
-        flat = copy_for_each(lax.all_to_all(flat, "z", 0, 0, tiled=True), ROW)
-        flat = flat.reshape(members, areas, *current.shape)
+        flat = lax.all_to_all(flat, "z", 0, 0, tiled=True)
+        own = jnp.stack(from_all(flat, "y"))
+        other = along(own, "core", 1)
+        place = jnp.stack([lax.axis_index("y"), lax.axis_index("core")]).astype(jnp.int32)
     with jax.named_scope("bus_voltage"):
-        pieces = bus_product(impedance, flat, lax.axis_size("x"))
-        own = jnp.sum(lax.all_to_all(pieces, "x", 0, 0, tiled=True), axis=0)
-        block = jnp.moveaxis(copy_for_each(own, "x"), 0, 1)
-        block = block.reshape(2, -1, block.shape[-1])
+        partial = bus_product(place, impedance, own, other)
+        block = sum_of(from_all(partial, "x"))
         bus_voltage = lax.all_gather(block, "z", axis=1, tiled=True)
     with jax.named_scope("port_voltage"):
         first = lax.axis_index(ROW) * bus_rows + lax.axis_index("z") * block.shape[1]

time: 175 us -> 169 us (0.966)
  blocking collectives: 80.1 us -> 39.4 us
  waiting for transfers between devices: 12 us -> 31.7 us
  starting transfers between devices: 16.6 us -> 33.5 us
  local copies, waits for them, and re-layouts: 9.23 us -> 7.45 us
    all_to_all x4 -> x1, blocking collectives: 55.9 us -> 15.2 us  [per_device(): flat = lax.all_to_all(flat, 'z', 0, 0, tiled=True)]
    ppermute x0 -> x7, waiting for transfers between devices: none -> 17.5 us  [along(): return lax.ppermute(x, axis, [(i, (i + by) % size) for i in range(size)])]
    ppermute x0 -> x7, starting transfers between devices: none -> 16.7 us  [along(): return lax.ppermute(x, axis, [(i, (i + by) % size) for i in range(size)])]
    all_gather x1, waiting for transfers between devices: 10.3 us -> 12.5 us  [per_device(): bus_voltage = lax.all_gather(block, 'z', axis=1, tiled=True)]
    pallas_call x1, Pallas kernels: 35.6 us -> 33.6 us  [window(): pl.pallas_call(window_kernel, out_shape=(jax.ShapeDtypeStruct((STEPS, LIN...]
    unnamed x19 -> x17, local copies, waits for them, and re-layouts: 8.33 us -> 7.36 us
  transfers between devices with their start and end apart: 6 -> 13, of which waited for: 2 -> 9; matrix products, arithmetic and copies ran while one was open for 1% -> 1% of each run, Pallas kernels for 21% -> 21%
where the time goes in v4:
time: 169 us
  Pallas kernels  40.4 us (24%)
  blocking collectives  39.4 us (23%)
  starting transfers between devices  33.5 us (20%)
  waiting for transfers between devices  31.7 us (19%)
  between operations  14.8 us (9%)
  local copies, waits for them, and re-layouts  7.45 us (4%)
    pallas_call x1, Pallas kernels, window(): pl.pallas_call(window_kernel, out_shape=(jax.ShapeDtypeStruct((STEPS, LIN...  33.6 us
    ppermute x7, waiting for transfers between devices, along(): return lax.ppermute(x, axis, [(i, (i + by) % size) for i in range(size)])  17.5 us
    ppermute x7, starting transfers between devices, along(): return lax.ppermute(x, axis, [(i, (i + by) % size) for i in range(size)])  16.7 us
    all_to_all x1, blocking collectives, per_device(): flat = lax.all_to_all(flat, 'z', 0, 0, tiled=True)  15.2 us
    all_to_all x1, blocking collectives, per_device(): mine = jnp.sum(lax.all_to_all(picked, ROW, 0, 0, tiled=True), axis=0)  13 us
    all_gather x1, waiting for transfers between devices, per_device(): bus_voltage = lax.all_gather(block, 'z', axis=1, tiled=True)  12.5 us
    all_to_all x1, blocking collectives, per_device(): mine = jnp.sum(lax.all_to_all(mine, 'z', 0, 0, tiled=True), axis=0)  11.3 us
    all_to_all x1, starting transfers between devices, per_device(): impedance = lax.all_to_all(blocks, 'z', 0, 0, tiled=True)  8.48 us
  transfers between devices with their start and end apart: 13, of which 9 were waited for; matrix products, arithmetic and copies ran while one was open for 1% of the time, Pallas kernels for 21%

profile of v4, /device:TPU:2, one launch (start us, length us, event | category | flops | bytes accessed | tf_op | source)
XLA Modules:
  0.0 168.7 jit_solution(2442490422626857547)
XLA Ops:
  7.2 1.1 copy-done.1
  8.3 0.7 copy-done.7
  8.9 1.3 pack_waves.1
  10.3 3.8 %collective-permute-start.2 = (f32[12,40,128]{2,1,0:T(8,128)S(1)}, f32[12,40,128]{2,1,0:T(8,128)S(1)}, u32[]{:S(2)}, u32[]{:S(2)}) collective-permute-start(f32[12,40,128]{2,1,0:T(8,128)S(1)} %get-tuple-element.15), channel_id=1, source_target_pairs={{0,255},{1,0},{2,1},{3,2},{4,3},{5,4},{6,5},{7,6},{8,7},{9,8},{10,... | collective-permute-start | bytes 737288 | tf_op jit(solution)/shard_map/wave_exchange/ppermute | solution.py:456
  14.1 4.1 %collective-permute-start.3 = (f32[4,40,128]{2,1,0:T(8,128)S(1)}, f32[4,40,128]{2,1,0:T(8,128)S(1)}, u32[]{:S(2)}, u32[]{:S(2)}) collective-permute-start(f32[4,40,128]{2,1,0:T(8,128)S(1)} %get-tuple-element.16), channel_id=1, source_target_pairs={{0,254},{1,255},{2,0},{3,1},{4,2},{5,3},{6,4},{7,5},{8,6},{9,7},{1... | collective-permute-start | bytes 245768 | tf_op jit(solution)/shard_map/wave_exchange/ppermute | solution.py:456
  18.2 0.7 convert_element_type.14
  19.0 1.6 collective-permute-done.1.far_up.rest_1_
  20.7 1.5 copy-done
  22.2 1.5 turn_impedance.1
  23.7 8.5 %all-to-all-start = ((f32[8,328,128]{2,1,0:T(8,128)}), f32[8,328,128]{2,1,0:T(8,128)S(1)}, u32[]{:S(2)}, u32[]{:S(2)}) async-start(f32[8,328,128]{2,1,0:T(8,128)} %turn_impedance.1), calls=%async_computation | async-start | bytes 2686976 | tf_op jit(solution)/shard_map/impedance_exchange/all_to_all | solution.py:505
  33.1 33.6 %window.1 = (f32[20,32,128]{2,1,0:T(8,128)}, f32[1024,128]{1,0:T(8,128)}, f32[2,64,128]{2,1,0:T(8,128)}, f32[2,8,128]{2,1,0:T(8,128)}) custom-call(f32[2,20]{1,0:T(2,128)} %constant.26.clone.angle, s32[1,32]{1,0:T(1,128)} %partner.3, s32[1,32]{1,0:T(1,128)} %delay.1, s32[1]{0:T(128)S(6)} %copy.27.count, s32[1,32]{1,0:T(1,128)} %line_nodes.1, ...), custom_call_target="tpu_custom_call" | custom-call | flops 16106127360 | bytes 67108864 | tf_op jit(solution)/shard_map/window/window/pallas_call | solution.py:308
  66.7 0.7 copy-done.6
  67.4 15.2 %all_to_all.20 = f32[8,2,8,128]{3,2,1,0:T(8,128)S(1)} all-to-all(f32[8,2,8,128]{3,2,1,0:T(8,128)S(1)} %spread_currents.1), channel_id=1, replica_groups=mesh['z'=8,'x'=4,'y'=4,'core'=2] {'z'}, dimensions={0} | all-to-all | bytes 131072 | tf_op jit(solution)/shard_map/currents/all_to_all | solution.py:524
  82.5 0.4 collective-permute-start.4
  82.9 5.2 %collective-permute-start.5 = (f32[8,2,8,128]{3,2,1,0:T(8,128)S(1)}, f32[8,2,8,128]{3,2,1,0:T(8,128)S(1)}, u32[]{:S(2)}, u32[]{:S(2)}) collective-permute-start(f32[8,2,8,128]{3,2,1,0:T(8,128)S(1)} %all_to_all.20), channel_id=1, source_target_pairs={{0,4},{2,6},{4,0},{6,2},{1,5},{3,7},{5,1},{7,3},{8,12},{10,14},{12... | collective-permute-start | bytes 196616 | tf_op jit(solution)/shard_map/currents/ppermute | solution.py:461
  88.1 0.8 collective-permute-done.4
  88.9 2.2 %collective-permute-done.5 = f32[8,2,8,128]{3,2,1,0:T(8,128)S(1)} collective-permute-done((f32[8,2,8,128]{3,2,1,0:T(8,128)S(1)}, f32[8,2,8,128]{3,2,1,0:T(8,128)S(1)}, u32[]{:S(2)}, u32[]{:S(2)}) %collective-permute-start.5) | collective-permute-done | bytes 65568 | tf_op jit(solution)/shard_map/currents/ppermute | solution.py:461
  91.1 1.3 collective-permute-done.6
  92.6 1.4 collective-permute-done.7.other
  94.0 1.3 bus_product.1.refs_0_
  95.3 4.4 %collective-permute-start.10 = (f32[2,320,128]{2,1,0:T(8,128)S(1)}, f32[2,320,128]{2,1,0:T(8,128)S(1)}, u32[]{:S(2)}, u32[]{:S(2)}) collective-permute-start(f32[2,320,128]{2,1,0:T(8,128)S(1)} %bus_product.1.refs_0_), channel_id=1, source_target_pairs={{0,24},{8,0},{16,8},{24,16},{1,25},{9,1},{17,9},{25,17},{2,26},{10... | collective-permute-start | bytes 983048 | tf_op jit(solution)/shard_map/bus_voltage/ppermute | solution.py:461
  99.7 6.6 %collective-permute-start.9 = (f32[2,320,128]{2,1,0:T(8,128)S(1)}, f32[2,320,128]{2,1,0:T(8,128)S(1)}, u32[]{:S(2)}, u32[]{:S(2)}) collective-permute-start(f32[2,320,128]{2,1,0:T(8,128)S(1)} %bus_product.1.refs_0_), channel_id=1, source_target_pairs={{0,16},{8,24},{16,0},{24,8},{1,17},{9,25},{17,1},{25,9},{2,18},{10... | collective-permute-start | bytes 983048 | tf_op jit(solution)/shard_map/bus_voltage/ppermute | solution.py:461
  106.4 1.4 collective-permute-done.10.refs_3_
  107.8 5.0 %collective-permute-done.8.refs_1_ = f32[2,320,128]{2,1,0:T(8,128)S(1)} collective-permute-done((f32[2,320,128]{2,1,0:T(8,128)S(1)}, f32[2,320,128]{2,1,0:T(8,128)S(1)}, u32[]{:S(2)}, u32[]{:S(2)}) %collective-permute-start.8) | collective-permute-done | bytes 327712 | tf_op jit(solution)/shard_map/bus_voltage/ppermute | solution.py:461
  112.8 5.3 %collective-permute-done.9.refs_2_ = f32[2,320,128]{2,1,0:T(8,128)S(1)} collective-permute-done((f32[2,320,128]{2,1,0:T(8,128)S(1)}, f32[2,320,128]{2,1,0:T(8,128)S(1)}, u32[]{:S(2)}, u32[]{:S(2)}) %collective-permute-start.9) | collective-permute-done | bytes 327712 | tf_op jit(solution)/shard_map/bus_voltage/ppermute | solution.py:461
  118.2 0.8 sum_of_parts.1.volts
  119.0 2.0 %port_rows.1 = f32[8,8,8,256]{3,2,1,0:T(8,128)S(1)} custom-call(s32[1]{0:T(128)} %bitcast.16.first, f32[8,328,128]{2,1,0:T(8,128)S(1)} %all-to-all-done.impedance.ports, f32[2,320,128]{2,1,0:T(8,128)} %sum_of_parts.1.volts), custom_call_target="tpu_custom_call" | custom-call | tf_op jit(solution)/shard_map/port_voltage/port_rows/pallas_call | solution.py:444
  121.0 13.0 %all_to_all.21 = f32[8,8,8,256]{3,2,1,0:T(8,128)S(1)} all-to-all(f32[8,8,8,256]{3,2,1,0:T(8,128)S(1)} %port_rows.1), channel_id=1, replica_groups=mesh['z'=8,'x'=4,'y'=4,'core'=2] {'y','core'}, dimensions={0} | all-to-all | bytes 1048576 | tf_op jit(solution)/shard_map/port_voltage/all_to_all | solution.py:535
  134.0 11.3 %all_to_all.22 = f32[8,8,256]{2,1,0:T(8,128)S(1)} all-to-all(f32[8,8,256]{2,1,0:T(8,128)S(1)} %reduce_sum.18), channel_id=1, replica_groups=mesh['z'=8,'x'=4,'y'=4,'core'=2] {'z'}, dimensions={0} | all-to-all | bytes 131072 | tf_op jit(solution)/shard_map/port_voltage/all_to_all | solution.py:536
  145.4 0.6 maximum_bitcast_fusion
  146.0 12.5 %all-gather.2.cloned.1.call-done = f32[2,2560,128]{2,1,0:T(8,128)} async-done(((f32[2,320,128]{2,1,0:T(8,128)}), f32[2,2560,128]{2,1,0:T(8,128)}) %all-gather.2.cloned.1.call-update) | async-done | bytes 2621456 | tf_op jit(solution)/shard_map/bus_voltage/all_gather | solution.py:531
  158.5 3.4 %copy.28 = f32[2,2560,128]{2,1,0:T(8,128)} copy(f32[2,2560,128]{2,1,0:T(8,128)} %all-gather.2.cloned.1.call-done) | data formatting | bytes 5242880
  (31 shorter events, 0.7 us)
Async XLA Ops:
  7.2 1.1 copy-start.1
  8.3 0.7 copy-start.7
  10.2 10.5 %collective-permute-start = (f32[12,40,128]{2,1,0:T(8,128)S(1)}, f32[12,40,128]{2,1,0:T(8,128)S(1)}, u32[]{:S(2)}, u32[]{:S(2)}) collective-permute-start(f32[12,40,128]{2,1,0:T(8,128)S(1)} %get-tuple-element.13), channel_id=1, source_target_pairs={{0,1},{1,2},{2,3},{3,4},{4,5},{5,6},{6,7},{7,8},{8,9},{9,10},{10,1... | collective-permute-start | bytes 737288 | tf_op jit(solution)/shard_map/wave_exchange/ppermute | solution.py:456
  10.3 10.4 %collective-permute-start.2 = (f32[12,40,128]{2,1,0:T(8,128)S(1)}, f32[12,40,128]{2,1,0:T(8,128)S(1)}, u32[]{:S(2)}, u32[]{:S(2)}) collective-permute-start(f32[12,40,128]{2,1,0:T(8,128)S(1)} %get-tuple-element.15), channel_id=1, source_target_pairs={{0,255},{1,0},{2,1},{3,2},{4,3},{5,4},{6,5},{7,6},{8,7},{9,8},{10,... | collective-permute-start | bytes 737288 | tf_op jit(solution)/shard_map/wave_exchange/ppermute | solution.py:456
  14.1 6.6 %collective-permute-start.1 = (f32[4,40,128]{2,1,0:T(8,128)S(1)}, f32[4,40,128]{2,1,0:T(8,128)S(1)}, u32[]{:S(2)}, u32[]{:S(2)}) collective-permute-start(f32[4,40,128]{2,1,0:T(8,128)S(1)} %get-tuple-element.14), channel_id=1, source_target_pairs={{0,2},{1,3},{2,4},{3,5},{4,6},{5,7},{6,8},{7,9},{8,10},{9,11},{10,... | collective-permute-start | bytes 245768 | tf_op jit(solution)/shard_map/wave_exchange/ppermute | solution.py:456
  14.1 6.6 %collective-permute-start.3 = (f32[4,40,128]{2,1,0:T(8,128)S(1)}, f32[4,40,128]{2,1,0:T(8,128)S(1)}, u32[]{:S(2)}, u32[]{:S(2)}) collective-permute-start(f32[4,40,128]{2,1,0:T(8,128)S(1)} %get-tuple-element.16), channel_id=1, source_target_pairs={{0,254},{1,255},{2,0},{3,1},{4,2},{5,3},{6,4},{7,5},{8,6},{9,7},{1... | collective-permute-start | bytes 245768 | tf_op jit(solution)/shard_map/wave_exchange/ppermute | solution.py:456
  20.7 3.0 %copy-start.4 = (f32[4,40,128]{2,1,0:T(8,128)}, f32[4,40,128]{2,1,0:T(8,128)S(1)}, u32[]{:S(2)}) copy-start(f32[4,40,128]{2,1,0:T(8,128)S(1)} %collective-permute-done.1.far_up.rest_1_) | copy-start | bytes 245764
  20.7 3.0 %copy-start.5 = (f32[4,40,128]{2,1,0:T(8,128)}, f32[4,40,128]{2,1,0:T(8,128)S(1)}, u32[]{:S(2)}) copy-start(f32[4,40,128]{2,1,0:T(8,128)S(1)} %collective-permute-done.3.far_down.rest_3_) | copy-start | bytes 245764
  20.7 3.0 %copy-start.2 = (f32[12,40,128]{2,1,0:T(8,128)}, f32[12,40,128]{2,1,0:T(8,128)S(1)}, u32[]{:S(2)}) copy-start(f32[12,40,128]{2,1,0:T(8,128)S(1)} %collective-permute-done.near_up.rest_0_) | copy-start | bytes 737284
  20.7 3.0 %copy-start.3 = (f32[12,40,128]{2,1,0:T(8,128)}, f32[12,40,128]{2,1,0:T(8,128)S(1)}, u32[]{:S(2)}) copy-start(f32[12,40,128]{2,1,0:T(8,128)S(1)} %collective-permute-done.2.near_down.rest_2_) | copy-start | bytes 737284
  20.7 1.5 copy-start
  23.7 42.9 %all-to-all-start = ((f32[8,328,128]{2,1,0:T(8,128)}), f32[8,328,128]{2,1,0:T(8,128)S(1)}, u32[]{:S(2)}, u32[]{:S(2)}) async-start(f32[8,328,128]{2,1,0:T(8,128)} %turn_impedance.1), calls=%async_computation | async-start | bytes 2686976 | tf_op jit(solution)/shard_map/impedance_exchange/all_to_all | solution.py:505
  32.2 126.3 %all-gather.2.cloned.1.call-start = ((), (), s32[]{:S(2)}) async-start(), calls=%async_computation.4 | async-start | bytes 2949120 | tf_op jit(solution)/shard_map/bus_voltage/all_gather | solution.py:531
  66.6 0.7 copy-start.6
  82.5 6.4 %collective-permute-start.4 = (f32[8,2,8,128]{3,2,1,0:T(8,128)S(1)}, f32[8,2,8,128]{3,2,1,0:T(8,128)S(1)}, u32[]{:S(2)}, u32[]{:S(2)}) collective-permute-start(f32[8,2,8,128]{3,2,1,0:T(8,128)S(1)} %all_to_all.20), channel_id=1, source_target_pairs={{0,2},{2,4},{4,6},{6,0},{1,3},{3,5},{5,7},{7,1},{8,10},{10,12},{12... | collective-permute-start | bytes 196616 | tf_op jit(solution)/shard_map/currents/ppermute | solution.py:461
  82.9 8.2 %collective-permute-start.5 = (f32[8,2,8,128]{3,2,1,0:T(8,128)S(1)}, f32[8,2,8,128]{3,2,1,0:T(8,128)S(1)}, u32[]{:S(2)}, u32[]{:S(2)}) collective-permute-start(f32[8,2,8,128]{3,2,1,0:T(8,128)S(1)} %all_to_all.20), channel_id=1, source_target_pairs={{0,4},{2,6},{4,0},{6,2},{1,5},{3,7},{5,1},{7,3},{8,12},{10,14},{12... | collective-permute-start | bytes 196616 | tf_op jit(solution)/shard_map/currents/ppermute | solution.py:461
  88.1 4.3 %collective-permute-start.6 = (f32[8,2,8,128]{3,2,1,0:T(8,128)S(1)}, f32[8,2,8,128]{3,2,1,0:T(8,128)S(1)}, u32[]{:S(2)}, u32[]{:S(2)}) collective-permute-start(f32[8,2,8,128]{3,2,1,0:T(8,128)S(1)} %all_to_all.20), channel_id=1, source_target_pairs={{0,6},{2,0},{4,2},{6,4},{1,7},{3,1},{5,3},{7,5},{8,14},{10,8},{12,... | collective-permute-start | bytes 196616 | tf_op jit(solution)/shard_map/currents/ppermute | solution.py:461
  92.4 1.6 collective-permute-start.7
  95.3 12.5 %collective-permute-start.10 = (f32[2,320,128]{2,1,0:T(8,128)S(1)}, f32[2,320,128]{2,1,0:T(8,128)S(1)}, u32[]{:S(2)}, u32[]{:S(2)}) collective-permute-start(f32[2,320,128]{2,1,0:T(8,128)S(1)} %bus_product.1.refs_0_), channel_id=1, source_target_pairs={{0,24},{8,0},{16,8},{24,16},{1,25},{9,1},{17,9},{25,17},{2,26},{10... | collective-permute-start | bytes 983048 | tf_op jit(solution)/shard_map/bus_voltage/ppermute | solution.py:461
  99.7 13.1 %collective-permute-start.8 = (f32[2,320,128]{2,1,0:T(8,128)S(1)}, f32[2,320,128]{2,1,0:T(8,128)S(1)}, u32[]{:S(2)}, u32[]{:S(2)}) collective-permute-start(f32[2,320,128]{2,1,0:T(8,128)S(1)} %bus_product.1.refs_0_), channel_id=1, source_target_pairs={{0,8},{8,16},{16,24},{24,0},{1,9},{9,17},{17,25},{25,1},{2,10},{10... | collective-permute-start | bytes 983048 | tf_op jit(solution)/shard_map/bus_voltage/ppermute | solution.py:461
  99.7 18.4 %collective-permute-start.9 = (f32[2,320,128]{2,1,0:T(8,128)S(1)}, f32[2,320,128]{2,1,0:T(8,128)S(1)}, u32[]{:S(2)}, u32[]{:S(2)}) collective-permute-start(f32[2,320,128]{2,1,0:T(8,128)S(1)} %bus_product.1.refs_0_), channel_id=1, source_target_pairs={{0,16},{8,24},{16,0},{24,8},{1,17},{9,25},{17,1},{25,9},{2,18},{10... | collective-permute-start | bytes 983048 | tf_op jit(solution)/shard_map/bus_voltage/ppermute | solution.py:461
Sparse Core Ops, SparseCore 0:
  119.1 39.3 all-gather.1

commit v5 on v4

--- a/solution.py
+++ b/solution.py
@@ -39,7 +39,7 @@
     return jnp.bitwise_and(partner[0, line] - partner[0, HALF + line], 255) // 2
 
 
-def pack_kernel(partner, waves, near_up, far_up, near_down, far_down):
+def pack_kernel(partner, waves, near_up, far_down, near_down, far_up):
     near = jnp.int32(0)
     for line in range(HALF):
         is_near = reach_of(partner, line) == 1
@@ -74,8 +74,7 @@
     )(partner, waves)
 
 
-def turn_kernel(impedance, ports, *rest):
-    blocks = rest[-1]
+def turn_kernel(impedance, blocks):
     areas, rows, _ = blocks.shape
     rows = rows - 8
     for first in range(0, areas * rows, 128):
@@ -87,20 +86,19 @@
             size = min(128 - done, rows - at)
             blocks[area, pl.ds(at, size), :] = turned[done : done + size]
             done += size
-    for area in range(areas):
-        blocks[area, pl.ds(rows, 8), :] = jnp.broadcast_to(ports[...], (8, 128))
-
-
-def turn(impedance, ports, arrivals, areas):
+    blocks[:, pl.ds(rows, 8), :] = jnp.zeros((areas, 8, 128), F32)
+
+
+def turn(impedance, areas):
     vmem = pl.BlockSpec(memory_space=pltpu.VMEM)
     return pl.pallas_call(
         turn_kernel,
         out_shape=jax.ShapeDtypeStruct((areas, impedance.shape[2] // areas + 8, 128), F32),
-        in_specs=[vmem] * (2 + len(arrivals)),
+        in_specs=[vmem],
         out_specs=vmem,
         compiler_params=pltpu.CompilerParams(vmem_limit_bytes=32 << 20),
         name="turn_impedance",
-    )(impedance, ports, *arrivals)
+    )(impedance)
 
 
 def column(row):
@@ -122,9 +120,9 @@
     setpoint_hbm,
     pvolt_hbm,
     near_up,
+    far_down,
+    near_down,
     far_up,
-    near_down,
-    far_down,
     line_nodes,
     conv_nodes,
     port_nodes,
@@ -491,17 +489,19 @@
     members = lax.axis_size(ROW)
     bus_rows = transfer_impedance.shape[1]
     with jax.named_scope("wave_exchange"):
-        near_up, far_up, near_down, far_down = pack(line_partner, wave_history[0])
-        arrivals = (
-            shifted(near_up, 1),
-            shifted(far_up, 2),
-            shifted(near_down, -1),
-            shifted(far_down, -2),
-        )
+        near_up, far_down, near_down, far_up = pack(line_partner, wave_history[0])
+        from_below = shifted(near_up, 1)
+        from_above = shifted(near_down, -1)
+        from_far_above = shifted(far_down, -2)
+        from_far_below = shifted(far_up, 2)
+        arrivals = (from_below, from_far_above, from_above, from_far_below)
     with jax.named_scope("impedance_exchange"):
-        ports = port_bus.reshape(1, -1).astype(F32)
-        ports = jnp.pad(ports, ((0, 0), (0, 128 - ports.shape[1])), constant_values=-1.0)
-        blocks = turn(jnp.swapaxes(transfer_impedance, 1, 2), ports, arrivals, areas)
+        blocks = turn(jnp.swapaxes(transfer_impedance, 1, 2), areas)
+        ports = port_bus.reshape(1, 1, -1).astype(F32)
+        ports = jnp.pad(ports, ((0, 0), (0, 0), (0, 128 - ports.shape[2])), constant_values=-1.0)
+        ports = ports + 0.0 * sum(x[0, 0, 0] for x in arrivals)
+        ports = jnp.broadcast_to(ports, (areas, 8, 128))
+        blocks = lax.dynamic_update_slice(blocks, ports, (0, blocks.shape[1] - 8, 0))
         impedance = lax.all_to_all(blocks, "z", 0, 0, tiled=True)
     with jax.named_scope("window"):
         theta = np.arange(1, STEPS + 1, dtype=np.float32) * np.float32(2.0 * math.pi / STEPS)

time: 169 us -> 169 us (level)
  starting transfers between devices: 33.5 us -> 26.6 us
  between operations: 14.8 us -> 17.4 us
  local copies, waits for them, and re-layouts: 7.45 us -> 10 us
    ppermute x7, starting transfers between devices: 16.7 us -> 12 us  [along(): return lax.ppermute(x, axis, [(i, (i + by) % size) for i in range(size)])]
    slice x0 -> x4, local copies, waits for them, and re-layouts: none -> 2.18 us  [per_device(): ports = ports + 0.0 * sum((x[0, 0, 0] for x in arrivals))]
    ppermute x4, starting transfers between devices: 8.06 us -> 5.95 us  [shifted(): return lax.ppermute(x, ALL, [(i, (i + by) % size) for i in range(size)])]
  transfers between devices with their start and end apart: 13 -> 13, of which waited for: 9 -> 9; matrix products, arithmetic and copies ran while one was open for 1% -> 2% of each run, Pallas kernels for 21% -> 22%
where the time goes in v5:
time: 169 us
  Pallas kernels  40.4 us (24%)
  blocking collectives  40.3 us (24%)
  waiting for transfers between devices  32.4 us (19%)
  starting transfers between devices  26.6 us (16%)
  between operations  17.4 us (10%)
  local copies, waits for them, and re-layouts  10 us (6%)
    pallas_call x1, Pallas kernels, window(): pl.pallas_call(window_kernel, out_shape=(jax.ShapeDtypeStruct((STEPS, LIN...  33.6 us
    ppermute x7, waiting for transfers between devices, along(): return lax.ppermute(x, axis, [(i, (i + by) % size) for i in range(size)])  17.5 us
    all_to_all x1, blocking collectives, per_device(): flat = lax.all_to_all(flat, 'z', 0, 0, tiled=True)  15.2 us
    all_to_all x1, blocking collectives, per_device(): mine = jnp.sum(lax.all_to_all(picked, ROW, 0, 0, tiled=True), axis=0)  13.7 us
    all_gather x1, waiting for transfers between devices, per_device(): bus_voltage = lax.all_gather(block, 'z', axis=1, tiled=True)  13.6 us
    ppermute x7, starting transfers between devices, along(): return lax.ppermute(x, axis, [(i, (i + by) % size) for i in range(size)])  12 us
    all_to_all x1, blocking collectives, per_device(): mine = jnp.sum(lax.all_to_all(mine, 'z', 0, 0, tiled=True), axis=0)  11.4 us
    all_to_all x1, starting transfers between devices, per_device(): impedance = lax.all_to_all(blocks, 'z', 0, 0, tiled=True)  8.48 us
  transfers between devices with their start and end apart: 13, of which 9 were waited for; matrix products, arithmetic and copies ran while one was open for 2% of the time, Pallas kernels for 22%

profile of v5, /device:TPU:2, one launch (start us, length us, event | category | flops | bytes accessed | tf_op | source)
XLA Modules:
  0.0 168.6 jit_solution(5248783088972472565)
XLA Ops:
  7.2 1.1 copy-done.1
  8.3 0.7 copy-done.3
  8.9 1.3 pack_waves.1
  10.3 3.8 %collective-permute-start.2 = (f32[12,40,128]{2,1,0:T(8,128)S(1)}, f32[12,40,128]{2,1,0:T(8,128)S(1)}, u32[]{:S(2)}, u32[]{:S(2)}) collective-permute-start(f32[12,40,128]{2,1,0:T(8,128)S(1)} %get-tuple-element.15), channel_id=1, source_target_pairs={{0,255},{1,0},{2,1},{3,2},{4,3},{5,4},{6,5},{7,6},{8,7},{9,8},{10,... | collective-permute-start | bytes 737288 | tf_op jit(solution)/shard_map/wave_exchange/ppermute | solution.py:454
  14.1 0.9 collective-permute-start.1
  15.0 1.1 collective-permute-start.3
  16.1 0.7 convert_element_type.14
  16.9 1.3 copy-done
  18.2 1.5 turn_impedance.1
  20.3 1.3 collective-permute-done.3.far_up
  25.8 0.6 broadcast_dynamic-update-slice_fusion
  26.5 8.5 %all-to-all-start = ((f32[8,328,128]{2,1,0:T(8,128)}), f32[8,328,128]{2,1,0:T(8,128)S(1)}, u32[]{:S(2)}, u32[]{:S(2)}) async-start(f32[8,328,128]{2,1,0:T(8,128)} %broadcast_dynamic-update-slice_fusion), calls=%async_computation | async-start | bytes 2686976 | tf_op jit(solution)/shard_map/impedance_exchange/all_to_all | solution.py:505
  35.8 33.6 %window.1 = (f32[20,32,128]{2,1,0:T(8,128)}, f32[1024,128]{1,0:T(8,128)}, f32[2,64,128]{2,1,0:T(8,128)}, f32[2,8,128]{2,1,0:T(8,128)}) custom-call(f32[2,20]{1,0:T(2,128)} %constant.30.clone.angle, s32[1,32]{1,0:T(1,128)} %partner.3, s32[1,32]{1,0:T(1,128)} %delay.1, s32[1]{0:T(128)S(6)} %copy.28.count, s32[1,32]{1,0:T(1,128)} %line_nodes.1, ...), custom_call_target="tpu_custom_call" | custom-call | flops 16106127360 | bytes 67108864 | tf_op jit(solution)/shard_map/window/window/pallas_call | solution.py:306
  69.4 0.7 copy-done.2
  70.1 15.2 %all_to_all.20 = f32[8,2,8,128]{3,2,1,0:T(8,128)S(1)} all-to-all(f32[8,2,8,128]{3,2,1,0:T(8,128)S(1)} %spread_currents.1), channel_id=1, replica_groups=mesh['z'=8,'x'=4,'y'=4,'core'=2] {'z'}, dimensions={0} | all-to-all | bytes 131072 | tf_op jit(solution)/shard_map/currents/all_to_all | solution.py:524
  85.3 4.1 %collective-permute-start.5 = (f32[8,2,8,128]{3,2,1,0:T(8,128)S(1)}, f32[8,2,8,128]{3,2,1,0:T(8,128)S(1)}, u32[]{:S(2)}, u32[]{:S(2)}) collective-permute-start(f32[8,2,8,128]{3,2,1,0:T(8,128)S(1)} %all_to_all.20), channel_id=1, source_target_pairs={{0,4},{2,6},{4,0},{6,2},{1,5},{3,7},{5,1},{7,3},{8,12},{10,14},{12... | collective-permute-start | bytes 196616 | tf_op jit(solution)/shard_map/currents/ppermute | solution.py:459
  89.4 1.4 collective-permute-done.4
  90.8 1.6 collective-permute-done.5
  92.3 1.3 collective-permute-done.6
  93.9 1.4 collective-permute-done.7.other
  95.3 1.3 bus_product.1.refs_0_
  96.6 5.1 %collective-permute-start.10 = (f32[2,320,128]{2,1,0:T(8,128)S(1)}, f32[2,320,128]{2,1,0:T(8,128)S(1)}, u32[]{:S(2)}, u32[]{:S(2)}) collective-permute-start(f32[2,320,128]{2,1,0:T(8,128)S(1)} %bus_product.1.refs_0_), channel_id=1, source_target_pairs={{0,24},{8,0},{16,8},{24,16},{1,25},{9,1},{17,9},{25,17},{2,26},{10... | collective-permute-start | bytes 983048 | tf_op jit(solution)/shard_map/bus_voltage/ppermute | solution.py:459
  101.7 2.7 %collective-permute-start.9 = (f32[2,320,128]{2,1,0:T(8,128)S(1)}, f32[2,320,128]{2,1,0:T(8,128)S(1)}, u32[]{:S(2)}, u32[]{:S(2)}) collective-permute-start(f32[2,320,128]{2,1,0:T(8,128)S(1)} %bus_product.1.refs_0_), channel_id=1, source_target_pairs={{0,16},{8,24},{16,0},{24,8},{1,17},{9,25},{17,1},{25,9},{2,18},{10... | collective-permute-start | bytes 983048 | tf_op jit(solution)/shard_map/bus_voltage/ppermute | solution.py:459
  104.4 5.4 %collective-permute-done.10.refs_3_ = f32[2,320,128]{2,1,0:T(8,128)S(1)} collective-permute-done((f32[2,320,128]{2,1,0:T(8,128)S(1)}, f32[2,320,128]{2,1,0:T(8,128)S(1)}, u32[]{:S(2)}, u32[]{:S(2)}) %collective-permute-start.10) | collective-permute-done | bytes 327712 | tf_op jit(solution)/shard_map/bus_voltage/ppermute | solution.py:459
  109.8 2.5 %collective-permute-done.8.refs_1_ = f32[2,320,128]{2,1,0:T(8,128)S(1)} collective-permute-done((f32[2,320,128]{2,1,0:T(8,128)S(1)}, f32[2,320,128]{2,1,0:T(8,128)S(1)}, u32[]{:S(2)}, u32[]{:S(2)}) %collective-permute-start.8) | collective-permute-done | bytes 327712 | tf_op jit(solution)/shard_map/bus_voltage/ppermute | solution.py:459
  112.3 3.9 %collective-permute-done.9.refs_2_ = f32[2,320,128]{2,1,0:T(8,128)S(1)} collective-permute-done((f32[2,320,128]{2,1,0:T(8,128)S(1)}, f32[2,320,128]{2,1,0:T(8,128)S(1)}, u32[]{:S(2)}, u32[]{:S(2)}) %collective-permute-start.9) | collective-permute-done | bytes 327712 | tf_op jit(solution)/shard_map/bus_voltage/ppermute | solution.py:459
  116.2 0.8 sum_of_parts.1.volts
  117.0 2.0 %port_rows.1 = f32[8,8,8,256]{3,2,1,0:T(8,128)S(1)} custom-call(s32[1]{0:T(128)} %bitcast.18.first, f32[8,328,128]{2,1,0:T(8,128)S(1)} %all-to-all-done.impedance.ports, f32[2,320,128]{2,1,0:T(8,128)} %sum_of_parts.1.volts), custom_call_target="tpu_custom_call" | custom-call | tf_op jit(solution)/shard_map/port_voltage/port_rows/pallas_call | solution.py:442
  119.0 13.7 %all_to_all.21 = f32[8,8,8,256]{3,2,1,0:T(8,128)S(1)} all-to-all(f32[8,8,8,256]{3,2,1,0:T(8,128)S(1)} %port_rows.1), channel_id=1, replica_groups=mesh['z'=8,'x'=4,'y'=4,'core'=2] {'y','core'}, dimensions={0} | all-to-all | bytes 1048576 | tf_op jit(solution)/shard_map/port_voltage/all_to_all | solution.py:535
  132.7 11.4 %all_to_all.22 = f32[8,8,256]{2,1,0:T(8,128)S(1)} all-to-all(f32[8,8,256]{2,1,0:T(8,128)S(1)} %reduce_sum.18), channel_id=1, replica_groups=mesh['z'=8,'x'=4,'y'=4,'core'=2] {'z'}, dimensions={0} | all-to-all | bytes 131072 | tf_op jit(solution)/shard_map/port_voltage/all_to_all | solution.py:536
  144.8 13.6 %all-gather.2.cloned.1.call-done = f32[2,2560,128]{2,1,0:T(8,128)} async-done(((f32[2,320,128]{2,1,0:T(8,128)}), f32[2,2560,128]{2,1,0:T(8,128)}) %all-gather.2.cloned.1.call-update) | async-done | bytes 2621456 | tf_op jit(solution)/shard_map/bus_voltage/all_gather | solution.py:531
  158.4 3.4 %copy.29 = f32[2,2560,128]{2,1,0:T(8,128)} copy(f32[2,2560,128]{2,1,0:T(8,128)} %all-gather.2.cloned.1.call-done) | data formatting | bytes 5242880
  (36 shorter events, 3.5 us)
Async XLA Ops:
  7.2 1.1 copy-start.1
  8.3 0.7 copy-start.3
  10.2 11.9 %collective-permute-start = (f32[12,40,128]{2,1,0:T(8,128)S(1)}, f32[12,40,128]{2,1,0:T(8,128)S(1)}, u32[]{:S(2)}, u32[]{:S(2)}) collective-permute-start(f32[12,40,128]{2,1,0:T(8,128)S(1)} %get-tuple-element.13), channel_id=1, source_target_pairs={{0,1},{1,2},{2,3},{3,4},{4,5},{5,6},{6,7},{7,8},{8,9},{9,10},{10,1... | collective-permute-start | bytes 737288 | tf_op jit(solution)/shard_map/wave_exchange/ppermute | solution.py:454
  10.3 13.7 %collective-permute-start.2 = (f32[12,40,128]{2,1,0:T(8,128)S(1)}, f32[12,40,128]{2,1,0:T(8,128)S(1)}, u32[]{:S(2)}, u32[]{:S(2)}) collective-permute-start(f32[12,40,128]{2,1,0:T(8,128)S(1)} %get-tuple-element.15), channel_id=1, source_target_pairs={{0,255},{1,0},{2,1},{3,2},{4,3},{5,4},{6,5},{7,6},{8,7},{9,8},{10,... | collective-permute-start | bytes 737288 | tf_op jit(solution)/shard_map/wave_exchange/ppermute | solution.py:454
  14.1 5.6 %collective-permute-start.1 = (f32[4,40,128]{2,1,0:T(8,128)S(1)}, f32[4,40,128]{2,1,0:T(8,128)S(1)}, u32[]{:S(2)}, u32[]{:S(2)}) collective-permute-start(f32[4,40,128]{2,1,0:T(8,128)S(1)} %get-tuple-element.14), channel_id=1, source_target_pairs={{0,254},{1,255},{2,0},{3,1},{4,2},{5,3},{6,4},{7,5},{8,6},{9,7},{1... | collective-permute-start | bytes 245768 | tf_op jit(solution)/shard_map/wave_exchange/ppermute | solution.py:454
  15.0 6.6 %collective-permute-start.3 = (f32[4,40,128]{2,1,0:T(8,128)S(1)}, f32[4,40,128]{2,1,0:T(8,128)S(1)}, u32[]{:S(2)}, u32[]{:S(2)}) collective-permute-start(f32[4,40,128]{2,1,0:T(8,128)S(1)} %get-tuple-element.16), channel_id=1, source_target_pairs={{0,2},{1,3},{2,4},{3,5},{4,6},{5,7},{6,8},{7,9},{8,10},{9,11},{10,... | collective-permute-start | bytes 245768 | tf_op jit(solution)/shard_map/wave_exchange/ppermute | solution.py:454
  16.9 1.3 copy-start
  19.7 6.7 %copy-start.6 = (f32[4,40,128]{2,1,0:T(8,128)}, f32[4,40,128]{2,1,0:T(8,128)S(1)}, u32[]{:S(2)}) copy-start(f32[4,40,128]{2,1,0:T(8,128)S(1)} %collective-permute-done.1.far_down) | copy-start | bytes 245764
  21.5 4.9 %copy-start.7 = (f32[4,40,128]{2,1,0:T(8,128)}, f32[4,40,128]{2,1,0:T(8,128)S(1)}, u32[]{:S(2)}) copy-start(f32[4,40,128]{2,1,0:T(8,128)S(1)} %collective-permute-done.3.far_up) | copy-start | bytes 245764
  22.1 4.4 %copy-start.4 = (f32[12,40,128]{2,1,0:T(8,128)}, f32[12,40,128]{2,1,0:T(8,128)S(1)}, u32[]{:S(2)}) copy-start(f32[12,40,128]{2,1,0:T(8,128)S(1)} %collective-permute-done.near_up) | copy-start | bytes 737284
  23.9 2.5 %copy-start.5 = (f32[12,40,128]{2,1,0:T(8,128)}, f32[12,40,128]{2,1,0:T(8,128)S(1)}, u32[]{:S(2)}) copy-start(f32[12,40,128]{2,1,0:T(8,128)S(1)} %collective-permute-done.2.near_down) | copy-start | bytes 737284
  26.5 42.9 %all-to-all-start = ((f32[8,328,128]{2,1,0:T(8,128)}), f32[8,328,128]{2,1,0:T(8,128)S(1)}, u32[]{:S(2)}, u32[]{:S(2)}) async-start(f32[8,328,128]{2,1,0:T(8,128)} %broadcast_dynamic-update-slice_fusion), calls=%async_computation | async-start | bytes 2686976 | tf_op jit(solution)/shard_map/impedance_exchange/all_to_all | solution.py:505
  34.9 123.4 %all-gather.2.cloned.1.call-start = ((), (), s32[]{:S(2)}) async-start(), calls=%async_computation.4 | async-start | bytes 2949120 | tf_op jit(solution)/shard_map/bus_voltage/all_gather | solution.py:531
  69.4 0.7 copy-start.2
  85.3 5.5 %collective-permute-start.4 = (f32[8,2,8,128]{3,2,1,0:T(8,128)S(1)}, f32[8,2,8,128]{3,2,1,0:T(8,128)S(1)}, u32[]{:S(2)}, u32[]{:S(2)}) collective-permute-start(f32[8,2,8,128]{3,2,1,0:T(8,128)S(1)} %all_to_all.20), channel_id=1, source_target_pairs={{0,2},{2,4},{4,6},{6,0},{1,3},{3,5},{5,7},{7,1},{8,10},{10,12},{12... | collective-permute-start | bytes 196616 | tf_op jit(solution)/shard_map/currents/ppermute | solution.py:459
  85.3 7.1 %collective-permute-start.5 = (f32[8,2,8,128]{3,2,1,0:T(8,128)S(1)}, f32[8,2,8,128]{3,2,1,0:T(8,128)S(1)}, u32[]{:S(2)}, u32[]{:S(2)}) collective-permute-start(f32[8,2,8,128]{3,2,1,0:T(8,128)S(1)} %all_to_all.20), channel_id=1, source_target_pairs={{0,4},{2,6},{4,0},{6,2},{1,5},{3,7},{5,1},{7,3},{8,12},{10,14},{12... | collective-permute-start | bytes 196616 | tf_op jit(solution)/shard_map/currents/ppermute | solution.py:459
  89.4 4.3 %collective-permute-start.6 = (f32[8,2,8,128]{3,2,1,0:T(8,128)S(1)}, f32[8,2,8,128]{3,2,1,0:T(8,128)S(1)}, u32[]{:S(2)}, u32[]{:S(2)}) collective-permute-start(f32[8,2,8,128]{3,2,1,0:T(8,128)S(1)} %all_to_all.20), channel_id=1, source_target_pairs={{0,6},{2,0},{4,2},{6,4},{1,7},{3,1},{5,3},{7,5},{8,14},{10,8},{12,... | collective-permute-start | bytes 196616 | tf_op jit(solution)/shard_map/currents/ppermute | solution.py:459
  93.7 1.6 collective-permute-start.7
  96.6 13.1 %collective-permute-start.10 = (f32[2,320,128]{2,1,0:T(8,128)S(1)}, f32[2,320,128]{2,1,0:T(8,128)S(1)}, u32[]{:S(2)}, u32[]{:S(2)}) collective-permute-start(f32[2,320,128]{2,1,0:T(8,128)S(1)} %bus_product.1.refs_0_), channel_id=1, source_target_pairs={{0,24},{8,0},{16,8},{24,16},{1,25},{9,1},{17,9},{25,17},{2,26},{10... | collective-permute-start | bytes 983048 | tf_op jit(solution)/shard_map/bus_voltage/ppermute | solution.py:459
  101.7 10.6 %collective-permute-start.8 = (f32[2,320,128]{2,1,0:T(8,128)S(1)}, f32[2,320,128]{2,1,0:T(8,128)S(1)}, u32[]{:S(2)}, u32[]{:S(2)}) collective-permute-start(f32[2,320,128]{2,1,0:T(8,128)S(1)} %bus_product.1.refs_0_), channel_id=1, source_target_pairs={{0,8},{8,16},{16,24},{24,0},{1,9},{9,17},{17,25},{25,1},{2,10},{10... | collective-permute-start | bytes 983048 | tf_op jit(solution)/shard_map/bus_voltage/ppermute | solution.py:459
  101.7 14.5 %collective-permute-start.9 = (f32[2,320,128]{2,1,0:T(8,128)S(1)}, f32[2,320,128]{2,1,0:T(8,128)S(1)}, u32[]{:S(2)}, u32[]{:S(2)}) collective-permute-start(f32[2,320,128]{2,1,0:T(8,128)S(1)} %bus_product.1.refs_0_), channel_id=1, source_target_pairs={{0,16},{8,24},{16,0},{24,8},{1,17},{9,25},{17,1},{25,9},{2,18},{10... | collective-permute-start | bytes 983048 | tf_op jit(solution)/shard_map/bus_voltage/ppermute | solution.py:459
Sparse Core Ops, SparseCore 0:
  117.1 41.2 all-gather.1

commit v6 on v5

--- a/solution.py
+++ b/solution.py
@@ -99,6 +99,22 @@
         compiler_params=pltpu.CompilerParams(vmem_limit_bytes=32 << 20),
         name="turn_impedance",
     )(impedance)
+
+
+def port_block_kernel(ports, *rest):
+    rest[-1][...] = jnp.broadcast_to(ports[...], rest[-1].shape)
+
+
+def port_block(ports, before, areas):
+    vmem = pl.BlockSpec(memory_space=pltpu.VMEM)
+    return pl.pallas_call(
+        port_block_kernel,
+        out_shape=jax.ShapeDtypeStruct((areas, 8, 128), F32),
+        in_specs=[vmem] * (1 + len(before)),
+        out_specs=vmem,
+        compiler_params=pltpu.CompilerParams(vmem_limit_bytes=16 << 20),
+        name="port_block",
+    )(ports, *before)
 
 
 def column(row):
@@ -454,6 +470,42 @@
     return lax.ppermute(x, ALL, [(i, (i + by) % size) for i in range(size)])
 
 
+def copy_kernel(source, target, parts, in_sem, out_sem):
+    count, rows, _ = parts.shape
+    each = source.shape[1] // rows
+    fetches, stores = [], []
+    for i in range(count):
+        at = pl.ds((i % each) * rows, rows)
+        fetches.append(pltpu.make_async_copy(source.at[i // each, at], parts.at[i], in_sem.at[i]))
+        stores.append(pltpu.make_async_copy(parts.at[i], target.at[i // each, at], out_sem.at[i]))
+    for fetch in fetches:
+        fetch.start()
+    for fetch, store in zip(fetches, stores):
+        fetch.wait()
+        store.start()
+    for store in stores:
+        store.wait()
+
+
+def copied(x):
+    each = 4
+    count = x.shape[0] * each
+    anywhere = pl.BlockSpec(memory_space=pl.ANY)
+    return pl.pallas_call(
+        copy_kernel,
+        out_shape=jax.ShapeDtypeStruct(x.shape, x.dtype),
+        in_specs=[anywhere],
+        out_specs=anywhere,
+        scratch_shapes=[
+            pltpu.VMEM((count, x.shape[1] // each, x.shape[2]), x.dtype),
+            pltpu.SemaphoreType.DMA((count,)),
+            pltpu.SemaphoreType.DMA((count,)),
+        ],
+        compiler_params=pltpu.CompilerParams(vmem_limit_bytes=60 << 20),
+        name="copy_voltages",
+    )(x)
+
+
 def along(x, axis, by):
     size = lax.axis_size(axis)
     return lax.ppermute(x, axis, [(i, (i + by) % size) for i in range(size)])
@@ -499,8 +551,7 @@
         blocks = turn(jnp.swapaxes(transfer_impedance, 1, 2), areas)
         ports = port_bus.reshape(1, 1, -1).astype(F32)
         ports = jnp.pad(ports, ((0, 0), (0, 0), (0, 128 - ports.shape[2])), constant_values=-1.0)
-        ports = ports + 0.0 * sum(x[0, 0, 0] for x in arrivals)
-        ports = jnp.broadcast_to(ports, (areas, 8, 128))
+        ports = port_block(ports[0], arrivals, areas)
         blocks = lax.dynamic_update_slice(blocks, ports, (0, blocks.shape[1] - 8, 0))
         impedance = lax.all_to_all(blocks, "z", 0, 0, tiled=True)
     with jax.named_scope("window"):
@@ -528,7 +579,7 @@
     with jax.named_scope("bus_voltage"):
         partial = bus_product(place, impedance, own, other)
         block = sum_of(from_all(partial, "x"))
-        bus_voltage = lax.all_gather(block, "z", axis=1, tiled=True)
+        bus_voltage = copied(lax.all_gather(block, "z", axis=1, tiled=True))
     with jax.named_scope("port_voltage"):
         first = lax.axis_index(ROW) * bus_rows + lax.axis_index("z") * block.shape[1]
         picked = port_rows(first[None].astype(jnp.int32), impedance, block, members)

time: 169 us -> 164 us (0.970)
  local copies, waits for them, and re-layouts: 10 us -> 4.64 us
  Pallas kernels: 40.4 us -> 43 us
  between operations: 17.4 us -> 14.8 us
    unnamed x17 -> x16, local copies, waits for them, and re-layouts: 7.16 us -> 3.86 us
    pallas_call x0 -> x2, Pallas kernels: none -> 2.59 us  [the longest x1 2.59 us: copied(): pl.pallas_call(copy_kernel, out_shape=jax.ShapeDtypeStruct(x.shape, x.dty...]
    slice x4 -> x0, local copies, waits for them, and re-layouts: 2.18 us -> none  [per_device(): ports = ports + 0.0 * sum((x[0, 0, 0] for x in arrivals))]
  transfers between devices with their start and end apart: 13 -> 13, of which waited for: 9 -> 9; matrix products, arithmetic and copies ran while one was open for 2% -> 1% of each run, Pallas kernels for 22% -> 23%
where the time goes in v6:
time: 164 us
  Pallas kernels  43 us (26%)
  blocking collectives  40.4 us (25%)
  waiting for transfers between devices  33.2 us (20%)
  starting transfers between devices  26.3 us (16%)
  between operations  14.8 us (9%)
  local copies, waits for them, and re-layouts  4.64 us (3%)
    pallas_call x1, Pallas kernels, window(): pl.pallas_call(window_kernel, out_shape=(jax.ShapeDtypeStruct((STEPS, LIN...  33.6 us
    ppermute x7, waiting for transfers between devices, along(): return lax.ppermute(x, axis, [(i, (i + by) % size) for i in range(size)])  17.6 us
    all_to_all x1, blocking collectives, per_device(): flat = lax.all_to_all(flat, 'z', 0, 0, tiled=True)  15.1 us
    all_to_all x1, blocking collectives, per_device(): mine = jnp.sum(lax.all_to_all(picked, ROW, 0, 0, tiled=True), axis=0)  13.9 us
    all_gather x1, waiting for transfers between devices, per_device(): bus_voltage = copied(lax.all_gather(block, 'z', axis=1, tiled=True))  13.7 us
    ppermute x7, starting transfers between devices, along(): return lax.ppermute(x, axis, [(i, (i + by) % size) for i in range(size)])  11.7 us
    all_to_all x1, blocking collectives, per_device(): mine = jnp.sum(lax.all_to_all(mine, 'z', 0, 0, tiled=True), axis=0)  11.4 us
    all_to_all x1, starting transfers between devices, per_device(): impedance = lax.all_to_all(blocks, 'z', 0, 0, tiled=True)  8.47 us
  transfers between devices with their start and end apart: 13, of which 9 were waited for; matrix products, arithmetic and copies ran while one was open for 1% of the time, Pallas kernels for 23%

profile of v6, /device:TPU:2, one launch (start us, length us, event | category | flops | bytes accessed | tf_op | source)
XLA Modules:
  0.0 163.8 jit_solution(1131783219857234521)
XLA Ops:
  7.2 1.1 copy-done.1
  8.3 0.7 copy-done.7
  8.9 1.3 pack_waves.1
  10.3 3.8 %collective-permute-start.2 = (f32[12,40,128]{2,1,0:T(8,128)S(1)}, f32[12,40,128]{2,1,0:T(8,128)S(1)}, u32[]{:S(2)}, u32[]{:S(2)}) collective-permute-start(f32[12,40,128]{2,1,0:T(8,128)S(1)} %get-tuple-element.15), channel_id=1, source_target_pairs={{0,255},{1,0},{2,1},{3,2},{4,3},{5,4},{6,5},{7,6},{8,7},{9,8},{10,... | collective-permute-start | bytes 737288 | tf_op jit(solution)/shard_map/wave_exchange/ppermute | solution.py:470
  14.1 0.9 collective-permute-start.1
  15.0 1.1 collective-permute-start.3
  16.1 0.7 convert_element_type.14
  16.9 1.3 copy-done
  18.2 1.5 turn_impedance.1
  19.7 1.8 %collective-permute-done.3.far_up.rest_3_ = f32[4,40,128]{2,1,0:T(8,128)S(1)} collective-permute-done((f32[4,40,128]{2,1,0:T(8,128)S(1)}, f32[4,40,128]{2,1,0:T(8,128)S(1)}, u32[]{:S(2)}, u32[]{:S(2)}) %collective-permute-start.3) | collective-permute-done | bytes 81952 | tf_op jit(solution)/shard_map/wave_exchange/ppermute | solution.py:470
  21.6 0.7 constant_dynamic-update-slice_fusion
  22.4 8.5 %all-to-all-start = ((f32[8,328,128]{2,1,0:T(8,128)}), f32[8,328,128]{2,1,0:T(8,128)S(1)}, u32[]{:S(2)}, u32[]{:S(2)}) async-start(f32[8,328,128]{2,1,0:T(8,128)} %constant_dynamic-update-slice_fusion), calls=%async_computation | async-start | bytes 2686976 | tf_op jit(solution)/shard_map/impedance_exchange/all_to_all | solution.py:556
  31.7 33.6 %window.1 = (f32[20,32,128]{2,1,0:T(8,128)}, f32[1024,128]{1,0:T(8,128)}, f32[2,64,128]{2,1,0:T(8,128)}, f32[2,8,128]{2,1,0:T(8,128)}) custom-call(f32[2,20]{1,0:T(2,128)} %constant.28.clone.angle, s32[1,32]{1,0:T(1,128)} %partner.3, s32[1,32]{1,0:T(1,128)} %delay.1, s32[1]{0:T(128)S(6)} %copy.27.count, s32[1,32]{1,0:T(1,128)} %line_nodes.1, ...), custom_call_target="tpu_custom_call" | custom-call | flops 16106127360 | bytes 67108864 | tf_op jit(solution)/shard_map/window/window/pallas_call | solution.py:322
  65.3 0.7 copy-done.6
  66.0 15.1 %all_to_all.20 = f32[8,2,8,128]{3,2,1,0:T(8,128)S(1)} all-to-all(f32[8,2,8,128]{3,2,1,0:T(8,128)S(1)} %spread_currents.1), channel_id=1, replica_groups=mesh['z'=8,'x'=4,'y'=4,'core'=2] {'z'}, dimensions={0} | all-to-all | bytes 131072 | tf_op jit(solution)/shard_map/currents/all_to_all | solution.py:575
  81.2 3.7 %collective-permute-start.5 = (f32[8,2,8,128]{3,2,1,0:T(8,128)S(1)}, f32[8,2,8,128]{3,2,1,0:T(8,128)S(1)}, u32[]{:S(2)}, u32[]{:S(2)}) collective-permute-start(f32[8,2,8,128]{3,2,1,0:T(8,128)S(1)} %all_to_all.20), channel_id=1, source_target_pairs={{0,4},{2,6},{4,0},{6,2},{1,5},{3,7},{5,1},{7,3},{8,12},{10,14},{12... | collective-permute-start | bytes 196616 | tf_op jit(solution)/shard_map/currents/ppermute | solution.py:511
  84.8 1.8 %collective-permute-done.4 = f32[8,2,8,128]{3,2,1,0:T(8,128)S(1)} collective-permute-done((f32[8,2,8,128]{3,2,1,0:T(8,128)S(1)}, f32[8,2,8,128]{3,2,1,0:T(8,128)S(1)}, u32[]{:S(2)}, u32[]{:S(2)}) %collective-permute-start.4) | collective-permute-done | bytes 65568 | tf_op jit(solution)/shard_map/currents/ppermute | solution.py:511
  86.6 1.2 collective-permute-done.5
  87.8 1.3 collective-permute-done.6
  89.3 1.4 collective-permute-done.7.other
  90.8 1.3 bus_product.1.refs_0_
  92.1 5.5 %collective-permute-start.10 = (f32[2,320,128]{2,1,0:T(8,128)S(1)}, f32[2,320,128]{2,1,0:T(8,128)S(1)}, u32[]{:S(2)}, u32[]{:S(2)}) collective-permute-start(f32[2,320,128]{2,1,0:T(8,128)S(1)} %bus_product.1.refs_0_), channel_id=1, source_target_pairs={{0,24},{8,0},{16,8},{24,16},{1,25},{9,1},{17,9},{25,17},{2,26},{10... | collective-permute-start | bytes 983048 | tf_op jit(solution)/shard_map/bus_voltage/ppermute | solution.py:511
  97.6 2.4 %collective-permute-start.9 = (f32[2,320,128]{2,1,0:T(8,128)S(1)}, f32[2,320,128]{2,1,0:T(8,128)S(1)}, u32[]{:S(2)}, u32[]{:S(2)}) collective-permute-start(f32[2,320,128]{2,1,0:T(8,128)S(1)} %bus_product.1.refs_0_), channel_id=1, source_target_pairs={{0,16},{8,24},{16,0},{24,8},{1,17},{9,25},{17,1},{25,9},{2,18},{10... | collective-permute-start | bytes 983048 | tf_op jit(solution)/shard_map/bus_voltage/ppermute | solution.py:511
  100.0 5.7 %collective-permute-done.10.refs_3_ = f32[2,320,128]{2,1,0:T(8,128)S(1)} collective-permute-done((f32[2,320,128]{2,1,0:T(8,128)S(1)}, f32[2,320,128]{2,1,0:T(8,128)S(1)}, u32[]{:S(2)}, u32[]{:S(2)}) %collective-permute-start.10) | collective-permute-done | bytes 327712 | tf_op jit(solution)/shard_map/bus_voltage/ppermute | solution.py:511
  105.7 2.5 %collective-permute-done.8.refs_1_ = f32[2,320,128]{2,1,0:T(8,128)S(1)} collective-permute-done((f32[2,320,128]{2,1,0:T(8,128)S(1)}, f32[2,320,128]{2,1,0:T(8,128)S(1)}, u32[]{:S(2)}, u32[]{:S(2)}) %collective-permute-start.8) | collective-permute-done | bytes 327712 | tf_op jit(solution)/shard_map/bus_voltage/ppermute | solution.py:511
  108.2 3.7 %collective-permute-done.9.refs_2_ = f32[2,320,128]{2,1,0:T(8,128)S(1)} collective-permute-done((f32[2,320,128]{2,1,0:T(8,128)S(1)}, f32[2,320,128]{2,1,0:T(8,128)S(1)}, u32[]{:S(2)}, u32[]{:S(2)}) %collective-permute-start.9) | collective-permute-done | bytes 327712 | tf_op jit(solution)/shard_map/bus_voltage/ppermute | solution.py:511
  111.9 0.8 sum_of_parts.1.volts
  112.7 2.0 %port_rows.1 = f32[8,8,8,256]{3,2,1,0:T(8,128)S(1)} custom-call(s32[1]{0:T(128)} %bitcast.17.first, f32[8,328,128]{2,1,0:T(8,128)S(1)} %all-to-all-done.impedance.ports, f32[2,320,128]{2,1,0:T(8,128)} %sum_of_parts.1.volts), custom_call_target="tpu_custom_call" | custom-call | tf_op jit(solution)/shard_map/port_voltage/port_rows/pallas_call | solution.py:458
  114.7 13.9 %all_to_all.21 = f32[8,8,8,256]{3,2,1,0:T(8,128)S(1)} all-to-all(f32[8,8,8,256]{3,2,1,0:T(8,128)S(1)} %port_rows.1), channel_id=1, replica_groups=mesh['z'=8,'x'=4,'y'=4,'core'=2] {'y','core'}, dimensions={0} | all-to-all | bytes 1048576 | tf_op jit(solution)/shard_map/port_voltage/all_to_all | solution.py:586
  128.6 11.4 %all_to_all.22 = f32[8,8,256]{2,1,0:T(8,128)S(1)} all-to-all(f32[8,8,256]{2,1,0:T(8,128)S(1)} %reduce_sum.18), channel_id=1, replica_groups=mesh['z'=8,'x'=4,'y'=4,'core'=2] {'z'}, dimensions={0} | all-to-all | bytes 131072 | tf_op jit(solution)/shard_map/port_voltage/all_to_all | solution.py:587
  140.7 13.7 %all-gather.2.cloned.1.call-done.source = f32[2,2560,128]{2,1,0:T(8,128)} async-done(((f32[2,320,128]{2,1,0:T(8,128)}), f32[2,2560,128]{2,1,0:T(8,128)}) %all-gather.2.cloned.1.call-update) | async-done | bytes 2621456 | tf_op jit(solution)/shard_map/bus_voltage/all_gather | solution.py:582
  154.4 2.6 %copy_voltages.1 = f32[2,2560,128]{2,1,0:T(8,128)} custom-call(f32[2,2560,128]{2,1,0:T(8,128)} %all-gather.2.cloned.1.call-done.source), custom_call_target="tpu_custom_call" | custom-call | tf_op jit(solution)/shard_map/bus_voltage/copy_voltages/pallas_call | solution.py:494
  (33 shorter events, 1.4 us)
Async XLA Ops:
  7.2 1.1 copy-start.1
  8.3 0.7 copy-start.7
  10.2 11.4 %collective-permute-start = (f32[12,40,128]{2,1,0:T(8,128)S(1)}, f32[12,40,128]{2,1,0:T(8,128)S(1)}, u32[]{:S(2)}, u32[]{:S(2)}) collective-permute-start(f32[12,40,128]{2,1,0:T(8,128)S(1)} %get-tuple-element.13), channel_id=1, source_target_pairs={{0,1},{1,2},{2,3},{3,4},{4,5},{5,6},{6,7},{7,8},{8,9},{9,10},{10,1... | collective-permute-start | bytes 737288 | tf_op jit(solution)/shard_map/wave_exchange/ppermute | solution.py:470
  10.3 11.3 %collective-permute-start.2 = (f32[12,40,128]{2,1,0:T(8,128)S(1)}, f32[12,40,128]{2,1,0:T(8,128)S(1)}, u32[]{:S(2)}, u32[]{:S(2)}) collective-permute-start(f32[12,40,128]{2,1,0:T(8,128)S(1)} %get-tuple-element.15), channel_id=1, source_target_pairs={{0,255},{1,0},{2,1},{3,2},{4,3},{5,4},{6,5},{7,6},{8,7},{9,8},{10,... | collective-permute-start | bytes 737288 | tf_op jit(solution)/shard_map/wave_exchange/ppermute | solution.py:470
  14.1 5.6 %collective-permute-start.1 = (f32[4,40,128]{2,1,0:T(8,128)S(1)}, f32[4,40,128]{2,1,0:T(8,128)S(1)}, u32[]{:S(2)}, u32[]{:S(2)}) collective-permute-start(f32[4,40,128]{2,1,0:T(8,128)S(1)} %get-tuple-element.14), channel_id=1, source_target_pairs={{0,254},{1,255},{2,0},{3,1},{4,2},{5,3},{6,4},{7,5},{8,6},{9,7},{1... | collective-permute-start | bytes 245768 | tf_op jit(solution)/shard_map/wave_exchange/ppermute | solution.py:470
  15.0 6.6 %collective-permute-start.3 = (f32[4,40,128]{2,1,0:T(8,128)S(1)}, f32[4,40,128]{2,1,0:T(8,128)S(1)}, u32[]{:S(2)}, u32[]{:S(2)}) collective-permute-start(f32[4,40,128]{2,1,0:T(8,128)S(1)} %get-tuple-element.16), channel_id=1, source_target_pairs={{0,2},{1,3},{2,4},{3,5},{4,6},{5,7},{6,8},{7,9},{8,10},{9,11},{10,... | collective-permute-start | bytes 245768 | tf_op jit(solution)/shard_map/wave_exchange/ppermute | solution.py:470
  16.9 1.3 copy-start
  19.7 2.6 %copy-start.4 = (f32[4,40,128]{2,1,0:T(8,128)}, f32[4,40,128]{2,1,0:T(8,128)S(1)}, u32[]{:S(2)}) copy-start(f32[4,40,128]{2,1,0:T(8,128)S(1)} %collective-permute-done.1.far_down.rest_1_) | copy-start | bytes 245764
  21.5 0.7 copy-start.5
  21.5 0.7 copy-start.2
  21.6 0.8 copy-start.3
  22.4 42.9 %all-to-all-start = ((f32[8,328,128]{2,1,0:T(8,128)}), f32[8,328,128]{2,1,0:T(8,128)S(1)}, u32[]{:S(2)}, u32[]{:S(2)}) async-start(f32[8,328,128]{2,1,0:T(8,128)} %constant_dynamic-update-slice_fusion), calls=%async_computation | async-start | bytes 2686976 | tf_op jit(solution)/shard_map/impedance_exchange/all_to_all | solution.py:556
  30.8 123.5 %all-gather.2.cloned.1.call-start = ((), (), s32[]{:S(2)}) async-start(), calls=%async_computation.4 | async-start | bytes 2949120 | tf_op jit(solution)/shard_map/bus_voltage/all_gather | solution.py:582
  65.3 0.7 copy-start.6
  81.1 5.5 %collective-permute-start.4 = (f32[8,2,8,128]{3,2,1,0:T(8,128)S(1)}, f32[8,2,8,128]{3,2,1,0:T(8,128)S(1)}, u32[]{:S(2)}, u32[]{:S(2)}) collective-permute-start(f32[8,2,8,128]{3,2,1,0:T(8,128)S(1)} %all_to_all.20), channel_id=1, source_target_pairs={{0,2},{2,4},{4,6},{6,0},{1,3},{3,5},{5,7},{7,1},{8,10},{10,12},{12... | collective-permute-start | bytes 196616 | tf_op jit(solution)/shard_map/currents/ppermute | solution.py:511
  81.2 6.6 %collective-permute-start.5 = (f32[8,2,8,128]{3,2,1,0:T(8,128)S(1)}, f32[8,2,8,128]{3,2,1,0:T(8,128)S(1)}, u32[]{:S(2)}, u32[]{:S(2)}) collective-permute-start(f32[8,2,8,128]{3,2,1,0:T(8,128)S(1)} %all_to_all.20), channel_id=1, source_target_pairs={{0,4},{2,6},{4,0},{6,2},{1,5},{3,7},{5,1},{7,3},{8,12},{10,14},{12... | collective-permute-start | bytes 196616 | tf_op jit(solution)/shard_map/currents/ppermute | solution.py:511
  84.8 4.3 %collective-permute-start.6 = (f32[8,2,8,128]{3,2,1,0:T(8,128)S(1)}, f32[8,2,8,128]{3,2,1,0:T(8,128)S(1)}, u32[]{:S(2)}, u32[]{:S(2)}) collective-permute-start(f32[8,2,8,128]{3,2,1,0:T(8,128)S(1)} %all_to_all.20), channel_id=1, source_target_pairs={{0,6},{2,0},{4,2},{6,4},{1,7},{3,1},{5,3},{7,5},{8,14},{10,8},{12,... | collective-permute-start | bytes 196616 | tf_op jit(solution)/shard_map/currents/ppermute | solution.py:511
  89.1 1.6 collective-permute-start.7
  92.1 13.6 %collective-permute-start.10 = (f32[2,320,128]{2,1,0:T(8,128)S(1)}, f32[2,320,128]{2,1,0:T(8,128)S(1)}, u32[]{:S(2)}, u32[]{:S(2)}) collective-permute-start(f32[2,320,128]{2,1,0:T(8,128)S(1)} %bus_product.1.refs_0_), channel_id=1, source_target_pairs={{0,24},{8,0},{16,8},{24,16},{1,25},{9,1},{17,9},{25,17},{2,26},{10... | collective-permute-start | bytes 983048 | tf_op jit(solution)/shard_map/bus_voltage/ppermute | solution.py:511
  97.6 10.6 %collective-permute-start.8 = (f32[2,320,128]{2,1,0:T(8,128)S(1)}, f32[2,320,128]{2,1,0:T(8,128)S(1)}, u32[]{:S(2)}, u32[]{:S(2)}) collective-permute-start(f32[2,320,128]{2,1,0:T(8,128)S(1)} %bus_product.1.refs_0_), channel_id=1, source_target_pairs={{0,8},{8,16},{16,24},{24,0},{1,9},{9,17},{17,25},{25,1},{2,10},{10... | collective-permute-start | bytes 983048 | tf_op jit(solution)/shard_map/bus_voltage/ppermute | solution.py:511
  97.6 14.3 %collective-permute-start.9 = (f32[2,320,128]{2,1,0:T(8,128)S(1)}, f32[2,320,128]{2,1,0:T(8,128)S(1)}, u32[]{:S(2)}, u32[]{:S(2)}) collective-permute-start(f32[2,320,128]{2,1,0:T(8,128)S(1)} %bus_product.1.refs_0_), channel_id=1, source_target_pairs={{0,16},{8,24},{16,0},{24,8},{1,17},{9,25},{17,1},{25,9},{2,18},{10... | collective-permute-start | bytes 983048 | tf_op jit(solution)/shard_map/bus_voltage/ppermute | solution.py:511
Sparse Core Ops, SparseCore 0:
  112.8 41.5 all-gather.1

commit v7 on v6

--- a/solution.py
+++ b/solution.py
@@ -470,14 +470,14 @@
     return lax.ppermute(x, ALL, [(i, (i + by) % size) for i in range(size)])
 
 
-def copy_kernel(source, target, parts, in_sem, out_sem):
-    count, rows, _ = parts.shape
-    each = source.shape[1] // rows
+def place_kernel(source, target, parts, in_sem, out_sem):
+    areas, halves, rows, _ = source.shape
     fetches, stores = [], []
-    for i in range(count):
-        at = pl.ds((i % each) * rows, rows)
-        fetches.append(pltpu.make_async_copy(source.at[i // each, at], parts.at[i], in_sem.at[i]))
-        stores.append(pltpu.make_async_copy(parts.at[i], target.at[i // each, at], out_sem.at[i]))
+    for i in range(areas * halves):
+        area, half = divmod(i, halves)
+        at = target.at[half, pl.ds(area * rows, rows)]
+        fetches.append(pltpu.make_async_copy(source.at[area, half], parts.at[i], in_sem.at[i]))
+        stores.append(pltpu.make_async_copy(parts.at[i], at, out_sem.at[i]))
     for fetch in fetches:
         fetch.start()
     for fetch, store in zip(fetches, stores):
@@ -487,22 +487,22 @@
         store.wait()
 
 
-def copied(x):
-    each = 4
-    count = x.shape[0] * each
+def placed(x):
+    areas, halves, rows, cases = x.shape
+    count = areas * halves
     anywhere = pl.BlockSpec(memory_space=pl.ANY)
     return pl.pallas_call(
-        copy_kernel,
-        out_shape=jax.ShapeDtypeStruct(x.shape, x.dtype),
+        place_kernel,
+        out_shape=jax.ShapeDtypeStruct((halves, areas * rows, cases), x.dtype),
         in_specs=[anywhere],
         out_specs=anywhere,
         scratch_shapes=[
-            pltpu.VMEM((count, x.shape[1] // each, x.shape[2]), x.dtype),
+            pltpu.VMEM((count, rows, cases), x.dtype),
             pltpu.SemaphoreType.DMA((count,)),
             pltpu.SemaphoreType.DMA((count,)),
         ],
         compiler_params=pltpu.CompilerParams(vmem_limit_bytes=60 << 20),
-        name="copy_voltages",
+        name="place_voltages",
     )(x)
 
 
@@ -579,7 +579,7 @@
     with jax.named_scope("bus_voltage"):
         partial = bus_product(place, impedance, own, other)
         block = sum_of(from_all(partial, "x"))
-        bus_voltage = copied(lax.all_gather(block, "z", axis=1, tiled=True))
+        bus_voltage = placed(lax.all_gather(block, "z"))
     with jax.named_scope("port_voltage"):
         first = lax.axis_index(ROW) * bus_rows + lax.axis_index("z") * block.shape[1]
         picked = port_rows(first[None].astype(jnp.int32), impedance, block, members)

time: 164 us -> 164 us (level)
  no operation moved by 1% of the time
where the time goes in v7:
time: 164 us
  Pallas kernels  43.2 us (26%)
  blocking collectives  40.5 us (25%)
  waiting for transfers between devices  33 us (20%)
  starting transfers between devices  26.3 us (16%)
  between operations  14.8 us (9%)
  local copies, waits for them, and re-layouts  4.64 us (3%)
    pallas_call x1, Pallas kernels, window(): pl.pallas_call(window_kernel, out_shape=(jax.ShapeDtypeStruct((STEPS, LIN...  33.6 us
    ppermute x7, waiting for transfers between devices, along(): return lax.ppermute(x, axis, [(i, (i + by) % size) for i in range(size)])  17.6 us
    all_to_all x1, blocking collectives, per_device(): flat = lax.all_to_all(flat, 'z', 0, 0, tiled=True)  15.2 us
    all_to_all x1, blocking collectives, per_device(): mine = jnp.sum(lax.all_to_all(picked, ROW, 0, 0, tiled=True), axis=0)  13.9 us
    all_gather x1, waiting for transfers between devices, per_device(): bus_voltage = placed(lax.all_gather(block, 'z'))  13.6 us
    ppermute x7, starting transfers between devices, along(): return lax.ppermute(x, axis, [(i, (i + by) % size) for i in range(size)])  11.7 us
    all_to_all x1, blocking collectives, per_device(): mine = jnp.sum(lax.all_to_all(mine, 'z', 0, 0, tiled=True), axis=0)  11.4 us
    all_to_all x1, starting transfers between devices, per_device(): impedance = lax.all_to_all(blocks, 'z', 0, 0, tiled=True)  8.47 us
  transfers between devices with their start and end apart: 13, of which 9 were waited for; matrix products, arithmetic and copies ran while one was open for 1% of the time, Pallas kernels for 23%

profile of v7, /device:TPU:2, one launch (start us, length us, event | category | flops | bytes accessed | tf_op | source)
XLA Modules:
  0.0 163.9 jit_solution(1542775132354257420)
XLA Ops:
  7.2 1.1 copy-done.1
  8.3 0.7 copy-done.7
  8.9 1.3 pack_waves.1
  10.3 3.8 %collective-permute-start.2 = (f32[12,40,128]{2,1,0:T(8,128)S(1)}, f32[12,40,128]{2,1,0:T(8,128)S(1)}, u32[]{:S(2)}, u32[]{:S(2)}) collective-permute-start(f32[12,40,128]{2,1,0:T(8,128)S(1)} %get-tuple-element.15), channel_id=1, source_target_pairs={{0,255},{1,0},{2,1},{3,2},{4,3},{5,4},{6,5},{7,6},{8,7},{9,8},{10,... | collective-permute-start | bytes 737288 | tf_op jit(solution)/shard_map/wave_exchange/ppermute | solution.py:470
  14.1 0.9 collective-permute-start.1
  15.0 1.1 collective-permute-start.3
  16.1 0.7 convert_element_type.14
  16.9 1.3 copy-done
  18.2 1.5 turn_impedance.1
  19.7 1.8 %collective-permute-done.3.far_up.rest_3_ = f32[4,40,128]{2,1,0:T(8,128)S(1)} collective-permute-done((f32[4,40,128]{2,1,0:T(8,128)S(1)}, f32[4,40,128]{2,1,0:T(8,128)S(1)}, u32[]{:S(2)}, u32[]{:S(2)}) %collective-permute-start.3) | collective-permute-done | bytes 81952 | tf_op jit(solution)/shard_map/wave_exchange/ppermute | solution.py:470
  21.6 0.7 constant_dynamic-update-slice_fusion
  22.4 8.5 %all-to-all-start = ((f32[8,328,128]{2,1,0:T(8,128)}), f32[8,328,128]{2,1,0:T(8,128)S(1)}, u32[]{:S(2)}, u32[]{:S(2)}) async-start(f32[8,328,128]{2,1,0:T(8,128)} %constant_dynamic-update-slice_fusion), calls=%async_computation | async-start | bytes 2686976 | tf_op jit(solution)/shard_map/impedance_exchange/all_to_all | solution.py:556
  31.7 33.6 %window.1 = (f32[20,32,128]{2,1,0:T(8,128)}, f32[1024,128]{1,0:T(8,128)}, f32[2,64,128]{2,1,0:T(8,128)}, f32[2,8,128]{2,1,0:T(8,128)}) custom-call(f32[2,20]{1,0:T(2,128)} %constant.28.clone.angle, s32[1,32]{1,0:T(1,128)} %partner.3, s32[1,32]{1,0:T(1,128)} %delay.1, s32[1]{0:T(128)S(6)} %copy.27.count, s32[1,32]{1,0:T(1,128)} %line_nodes.1, ...), custom_call_target="tpu_custom_call" | custom-call | flops 16106127360 | bytes 67108864 | tf_op jit(solution)/shard_map/window/window/pallas_call | solution.py:322
  65.3 0.7 copy-done.6
  66.0 15.2 %all_to_all.20 = f32[8,2,8,128]{3,2,1,0:T(8,128)S(1)} all-to-all(f32[8,2,8,128]{3,2,1,0:T(8,128)S(1)} %spread_currents.1), channel_id=1, replica_groups=mesh['z'=8,'x'=4,'y'=4,'core'=2] {'z'}, dimensions={0} | all-to-all | bytes 131072 | tf_op jit(solution)/shard_map/currents/all_to_all | solution.py:575
  81.2 3.6 %collective-permute-start.5 = (f32[8,2,8,128]{3,2,1,0:T(8,128)S(1)}, f32[8,2,8,128]{3,2,1,0:T(8,128)S(1)}, u32[]{:S(2)}, u32[]{:S(2)}) collective-permute-start(f32[8,2,8,128]{3,2,1,0:T(8,128)S(1)} %all_to_all.20), channel_id=1, source_target_pairs={{0,4},{2,6},{4,0},{6,2},{1,5},{3,7},{5,1},{7,3},{8,12},{10,14},{12... | collective-permute-start | bytes 196616 | tf_op jit(solution)/shard_map/currents/ppermute | solution.py:511
  84.8 1.9 %collective-permute-done.4 = f32[8,2,8,128]{3,2,1,0:T(8,128)S(1)} collective-permute-done((f32[8,2,8,128]{3,2,1,0:T(8,128)S(1)}, f32[8,2,8,128]{3,2,1,0:T(8,128)S(1)}, u32[]{:S(2)}, u32[]{:S(2)}) %collective-permute-start.4) | collective-permute-done | bytes 65568 | tf_op jit(solution)/shard_map/currents/ppermute | solution.py:511
  86.7 1.0 collective-permute-done.5
  87.7 1.3 collective-permute-done.6
  89.2 1.4 collective-permute-done.7.other
  90.7 1.3 bus_product.1.refs_0_
  92.0 5.6 %collective-permute-start.10 = (f32[2,320,128]{2,1,0:T(8,128)S(1)}, f32[2,320,128]{2,1,0:T(8,128)S(1)}, u32[]{:S(2)}, u32[]{:S(2)}) collective-permute-start(f32[2,320,128]{2,1,0:T(8,128)S(1)} %bus_product.1.refs_0_), channel_id=1, source_target_pairs={{0,24},{8,0},{16,8},{24,16},{1,25},{9,1},{17,9},{25,17},{2,26},{10... | collective-permute-start | bytes 983048 | tf_op jit(solution)/shard_map/bus_voltage/ppermute | solution.py:511
  97.6 2.4 %collective-permute-start.9 = (f32[2,320,128]{2,1,0:T(8,128)S(1)}, f32[2,320,128]{2,1,0:T(8,128)S(1)}, u32[]{:S(2)}, u32[]{:S(2)}) collective-permute-start(f32[2,320,128]{2,1,0:T(8,128)S(1)} %bus_product.1.refs_0_), channel_id=1, source_target_pairs={{0,16},{8,24},{16,0},{24,8},{1,17},{9,25},{17,1},{25,9},{2,18},{10... | collective-permute-start | bytes 983048 | tf_op jit(solution)/shard_map/bus_voltage/ppermute | solution.py:511
  100.0 5.7 %collective-permute-done.10.refs_3_ = f32[2,320,128]{2,1,0:T(8,128)S(1)} collective-permute-done((f32[2,320,128]{2,1,0:T(8,128)S(1)}, f32[2,320,128]{2,1,0:T(8,128)S(1)}, u32[]{:S(2)}, u32[]{:S(2)}) %collective-permute-start.10) | collective-permute-done | bytes 327712 | tf_op jit(solution)/shard_map/bus_voltage/ppermute | solution.py:511
  105.7 2.5 %collective-permute-done.8.refs_1_ = f32[2,320,128]{2,1,0:T(8,128)S(1)} collective-permute-done((f32[2,320,128]{2,1,0:T(8,128)S(1)}, f32[2,320,128]{2,1,0:T(8,128)S(1)}, u32[]{:S(2)}, u32[]{:S(2)}) %collective-permute-start.8) | collective-permute-done | bytes 327712 | tf_op jit(solution)/shard_map/bus_voltage/ppermute | solution.py:511
  108.2 3.7 %collective-permute-done.9.refs_2_ = f32[2,320,128]{2,1,0:T(8,128)S(1)} collective-permute-done((f32[2,320,128]{2,1,0:T(8,128)S(1)}, f32[2,320,128]{2,1,0:T(8,128)S(1)}, u32[]{:S(2)}, u32[]{:S(2)}) %collective-permute-start.9) | collective-permute-done | bytes 327712 | tf_op jit(solution)/shard_map/bus_voltage/ppermute | solution.py:511
  111.9 0.8 sum_of_parts.1.volts
  112.7 2.0 %port_rows.1 = f32[8,8,8,256]{3,2,1,0:T(8,128)S(1)} custom-call(s32[1]{0:T(128)} %bitcast.18.first, f32[8,328,128]{2,1,0:T(8,128)S(1)} %all-to-all-done.impedance.ports, f32[2,320,128]{2,1,0:T(8,128)} %sum_of_parts.1.volts), custom_call_target="tpu_custom_call" | custom-call | tf_op jit(solution)/shard_map/port_voltage/port_rows/pallas_call | solution.py:458
  114.7 13.9 %all_to_all.21 = f32[8,8,8,256]{3,2,1,0:T(8,128)S(1)} all-to-all(f32[8,8,8,256]{3,2,1,0:T(8,128)S(1)} %port_rows.1), channel_id=1, replica_groups=mesh['z'=8,'x'=4,'y'=4,'core'=2] {'y','core'}, dimensions={0} | all-to-all | bytes 1048576 | tf_op jit(solution)/shard_map/port_voltage/all_to_all | solution.py:586
  128.6 11.4 %all_to_all.22 = f32[8,8,256]{2,1,0:T(8,128)S(1)} all-to-all(f32[8,8,256]{2,1,0:T(8,128)S(1)} %reduce_sum.18), channel_id=1, replica_groups=mesh['z'=8,'x'=4,'y'=4,'core'=2] {'z'}, dimensions={0} | all-to-all | bytes 131072 | tf_op jit(solution)/shard_map/port_voltage/all_to_all | solution.py:587
  140.7 13.6 %all-gather.3.cloned.1.call-done = f32[16,320,128]{2,1,0:T(8,128)} async-done(((f32[2,320,128]{2,1,0:T(8,128)}), f32[16,320,128]{2,1,0:T(8,128)}) %all-gather.3.cloned.1.call-update) | async-done | bytes 2621456 | tf_op jit(solution)/shard_map/bus_voltage/all_gather | solution.py:582
  154.3 2.8 %place_voltages.1 = f32[2,2560,128]{2,1,0:T(8,128)} custom-call(f32[8,2,320,128]{3,2,1,0:T(8,128)} %bitcast.30), custom_call_target="tpu_custom_call" | custom-call | tf_op jit(solution)/shard_map/bus_voltage/place_voltages/pallas_call | solution.py:494
  (33 shorter events, 1.4 us)
Async XLA Ops:
  7.2 1.1 copy-start.1
  8.3 0.7 copy-start.7
  10.2 11.4 %collective-permute-start = (f32[12,40,128]{2,1,0:T(8,128)S(1)}, f32[12,40,128]{2,1,0:T(8,128)S(1)}, u32[]{:S(2)}, u32[]{:S(2)}) collective-permute-start(f32[12,40,128]{2,1,0:T(8,128)S(1)} %get-tuple-element.13), channel_id=1, source_target_pairs={{0,1},{1,2},{2,3},{3,4},{4,5},{5,6},{6,7},{7,8},{8,9},{9,10},{10,1... | collective-permute-start | bytes 737288 | tf_op jit(solution)/shard_map/wave_exchange/ppermute | solution.py:470
  10.3 11.3 %collective-permute-start.2 = (f32[12,40,128]{2,1,0:T(8,128)S(1)}, f32[12,40,128]{2,1,0:T(8,128)S(1)}, u32[]{:S(2)}, u32[]{:S(2)}) collective-permute-start(f32[12,40,128]{2,1,0:T(8,128)S(1)} %get-tuple-element.15), channel_id=1, source_target_pairs={{0,255},{1,0},{2,1},{3,2},{4,3},{5,4},{6,5},{7,6},{8,7},{9,8},{10,... | collective-permute-start | bytes 737288 | tf_op jit(solution)/shard_map/wave_exchange/ppermute | solution.py:470
  14.1 5.6 %collective-permute-start.1 = (f32[4,40,128]{2,1,0:T(8,128)S(1)}, f32[4,40,128]{2,1,0:T(8,128)S(1)}, u32[]{:S(2)}, u32[]{:S(2)}) collective-permute-start(f32[4,40,128]{2,1,0:T(8,128)S(1)} %get-tuple-element.14), channel_id=1, source_target_pairs={{0,254},{1,255},{2,0},{3,1},{4,2},{5,3},{6,4},{7,5},{8,6},{9,7},{1... | collective-permute-start | bytes 245768 | tf_op jit(solution)/shard_map/wave_exchange/ppermute | solution.py:470
  15.0 6.6 %collective-permute-start.3 = (f32[4,40,128]{2,1,0:T(8,128)S(1)}, f32[4,40,128]{2,1,0:T(8,128)S(1)}, u32[]{:S(2)}, u32[]{:S(2)}) collective-permute-start(f32[4,40,128]{2,1,0:T(8,128)S(1)} %get-tuple-element.16), channel_id=1, source_target_pairs={{0,2},{1,3},{2,4},{3,5},{4,6},{5,7},{6,8},{7,9},{8,10},{9,11},{10,... | collective-permute-start | bytes 245768 | tf_op jit(solution)/shard_map/wave_exchange/ppermute | solution.py:470
  16.9 1.3 copy-start
  19.7 2.6 %copy-start.4 = (f32[4,40,128]{2,1,0:T(8,128)}, f32[4,40,128]{2,1,0:T(8,128)S(1)}, u32[]{:S(2)}) copy-start(f32[4,40,128]{2,1,0:T(8,128)S(1)} %collective-permute-done.1.far_down.rest_1_) | copy-start | bytes 245764
  21.5 0.7 copy-start.5
  21.5 0.7 copy-start.2
  21.6 0.8 copy-start.3
  22.4 42.9 %all-to-all-start = ((f32[8,328,128]{2,1,0:T(8,128)}), f32[8,328,128]{2,1,0:T(8,128)S(1)}, u32[]{:S(2)}, u32[]{:S(2)}) async-start(f32[8,328,128]{2,1,0:T(8,128)} %constant_dynamic-update-slice_fusion), calls=%async_computation | async-start | bytes 2686976 | tf_op jit(solution)/shard_map/impedance_exchange/all_to_all | solution.py:556
  30.8 123.4 %all-gather.3.cloned.1.call-start = ((), (), s32[]{:S(2)}) async-start(), calls=%async_computation.4 | async-start | bytes 2949120 | tf_op jit(solution)/shard_map/bus_voltage/all_gather | solution.py:582
  65.3 0.7 copy-start.6
  81.2 5.5 %collective-permute-start.4 = (f32[8,2,8,128]{3,2,1,0:T(8,128)S(1)}, f32[8,2,8,128]{3,2,1,0:T(8,128)S(1)}, u32[]{:S(2)}, u32[]{:S(2)}) collective-permute-start(f32[8,2,8,128]{3,2,1,0:T(8,128)S(1)} %all_to_all.20), channel_id=1, source_target_pairs={{0,2},{2,4},{4,6},{6,0},{1,3},{3,5},{5,7},{7,1},{8,10},{10,12},{12... | collective-permute-start | bytes 196616 | tf_op jit(solution)/shard_map/currents/ppermute | solution.py:511
  81.2 6.5 %collective-permute-start.5 = (f32[8,2,8,128]{3,2,1,0:T(8,128)S(1)}, f32[8,2,8,128]{3,2,1,0:T(8,128)S(1)}, u32[]{:S(2)}, u32[]{:S(2)}) collective-permute-start(f32[8,2,8,128]{3,2,1,0:T(8,128)S(1)} %all_to_all.20), channel_id=1, source_target_pairs={{0,4},{2,6},{4,0},{6,2},{1,5},{3,7},{5,1},{7,3},{8,12},{10,14},{12... | collective-permute-start | bytes 196616 | tf_op jit(solution)/shard_map/currents/ppermute | solution.py:511
  84.8 4.3 %collective-permute-start.6 = (f32[8,2,8,128]{3,2,1,0:T(8,128)S(1)}, f32[8,2,8,128]{3,2,1,0:T(8,128)S(1)}, u32[]{:S(2)}, u32[]{:S(2)}) collective-permute-start(f32[8,2,8,128]{3,2,1,0:T(8,128)S(1)} %all_to_all.20), channel_id=1, source_target_pairs={{0,6},{2,0},{4,2},{6,4},{1,7},{3,1},{5,3},{7,5},{8,14},{10,8},{12,... | collective-permute-start | bytes 196616 | tf_op jit(solution)/shard_map/currents/ppermute | solution.py:511
  89.0 1.6 collective-permute-start.7
  92.0 13.7 %collective-permute-start.10 = (f32[2,320,128]{2,1,0:T(8,128)S(1)}, f32[2,320,128]{2,1,0:T(8,128)S(1)}, u32[]{:S(2)}, u32[]{:S(2)}) collective-permute-start(f32[2,320,128]{2,1,0:T(8,128)S(1)} %bus_product.1.refs_0_), channel_id=1, source_target_pairs={{0,24},{8,0},{16,8},{24,16},{1,25},{9,1},{17,9},{25,17},{2,26},{10... | collective-permute-start | bytes 983048 | tf_op jit(solution)/shard_map/bus_voltage/ppermute | solution.py:511
  97.6 10.6 %collective-permute-start.8 = (f32[2,320,128]{2,1,0:T(8,128)S(1)}, f32[2,320,128]{2,1,0:T(8,128)S(1)}, u32[]{:S(2)}, u32[]{:S(2)}) collective-permute-start(f32[2,320,128]{2,1,0:T(8,128)S(1)} %bus_product.1.refs_0_), channel_id=1, source_target_pairs={{0,8},{8,16},{16,24},{24,0},{1,9},{9,17},{17,25},{25,1},{2,10},{10... | collective-permute-start | bytes 983048 | tf_op jit(solution)/shard_map/bus_voltage/ppermute | solution.py:511
  97.6 14.3 %collective-permute-start.9 = (f32[2,320,128]{2,1,0:T(8,128)S(1)}, f32[2,320,128]{2,1,0:T(8,128)S(1)}, u32[]{:S(2)}, u32[]{:S(2)}) collective-permute-start(f32[2,320,128]{2,1,0:T(8,128)S(1)} %bus_product.1.refs_0_), channel_id=1, source_target_pairs={{0,16},{8,24},{16,0},{24,8},{1,17},{9,25},{17,1},{25,9},{2,18},{10... | collective-permute-start | bytes 983048 | tf_op jit(solution)/shard_map/bus_voltage/ppermute | solution.py:511
Sparse Core Ops, SparseCore 0:
  112.8 41.3 all-gather.2
